TPU v7x, 32 devices: a whole 2x2x4 slice. The times are simulated.
32 devices in a mesh: tm: 4 (over z), seq: 8 (over y, x, core).
Axes of the slice: x: 2, y: 2, z: 4, core: 2. Of those that a mesh axis runs over, the one named last changes fastest.
Arguments:
- states: float32 [32, 384, 64], P('tm', 'seq'), may hold values from -11 to 11
- first_state: float32 [384, 64], P('seq'), may hold values from -6 to 6
- now_step: int32 [32], P('tm'), may hold values from 1 to 960, as said below
- next_step: int32 [32], P('tm'), may hold values from 0 to 959, as said below
- embed_weight: bfloat16 [64, 1536], replicated, may hold values from -0.75 to 0.75
- mod_weight: bfloat16 [256, 4608], replicated, may hold values from -0.375 to 0.375
- qkv_weight: bfloat16 [1536, 12, 384], P('seq'), may hold values from -1 to 1
- out_weight: bfloat16 [1536, 1536], P('seq'), may hold values from -0.15625 to 0.15625
- final_weight: bfloat16 [1536, 64], replicated, may hold values from -0.15625 to 0.15625
Outputs:
- advanced: float32 [32, 384, 64], P('tm', 'seq')
- errors: float32 [32], P('tm')
Inputs may be any that keep to these rules, and one draw needn't show every extreme that they name: now_step[0] = 960 and now_step[j + 1] = next_step[j]. next_step[j] is now_step[j] minus a gap of 1 to 30.
All inputs are finite; a program needn't handle non-finite values.
Results may differ from a plain program's by a relative error of at most 0.002.
Values may be sent and summed in bfloat16 or wider, within the bound.
No kernel may reach another device: no remote copies, remote signals or barrier semaphores. Data moves between devices by JAX's collectives and lax.ppermute only.
A program may use at most 64 MiB of HBM per device.

v0:
```python
import math

import jax
import jax.numpy as jnp
from jax import lax
from jax.sharding import PartitionSpec as P


def from_behind(shard, axis, by):
    count = lax.axis_size(axis)
    pairs = [(i, i + by) for i in range(count) if 0 <= i + by < count]
    return lax.ppermute(shard, axis, pairs)


def entering(part, axis, combine, identity):
    place = lax.axis_index(axis)
    gathered = lax.all_gather(part, axis)
    state = jnp.zeros_like(part) + jnp.asarray(identity, part.dtype)

    def one(step, state):
        return combine(state, lax.dynamic_index_in_dim(gathered, step, 0, False))

    return lax.fori_loop(0, place, one, state)


def layer_norm(rows):
    row_mean = jnp.mean(rows, axis=-1, keepdims=True)
    centered = rows - row_mean
    variance = jnp.mean(centered * centered, axis=-1, keepdims=True)
    return centered * lax.rsqrt(variance + 1e-06)


def alpha_bar(step_ids):
    fraction = (step_ids.astype(jnp.float32) / 1000.0 + 0.008) / 1.008
    return jnp.cos(fraction * (math.pi / 2)) ** 2


def coefficients(now_step, next_step):
    alpha_now = alpha_bar(now_step)
    alpha_next = alpha_bar(next_step)
    step_ratio = jnp.sqrt(alpha_next / alpha_now)
    keep_coef = step_ratio - 1.0
    noise_coef = jnp.sqrt(1.0 - alpha_next) - step_ratio * jnp.sqrt(1.0 - alpha_now)
    return (keep_coef, noise_coef)


def modulation(step_ids, mod_weight):
    half_freq = mod_weight.shape[0] // 2
    frequency = jnp.exp(-math.log(10000.0) * jnp.arange(half_freq, dtype=jnp.float32) / half_freq)
    angles = step_ids.astype(jnp.float32)[:, None] * frequency[None, :]
    time_embed = jnp.concatenate([jnp.cos(angles), jnp.sin(angles)], axis=1).astype(jnp.bfloat16)
    return jnp.dot(time_embed, mod_weight, preferred_element_type=jnp.float32)


def attend_one(pair_item):
    hdim = pair_item.shape[1] // 3
    length = pair_item.shape[0]
    query_rows = 512 if length % 512 == 0 else length
    queries = pair_item[:, :hdim]
    key_rows = pair_item[:, hdim : 2 * hdim]
    values = pair_item[:, 2 * hdim :]

    def one_block(query_block):
        scores = jnp.dot(query_block, key_rows.T, preferred_element_type=jnp.float32) * hdim ** (
            -0.5
        )
        row_max = jnp.max(scores, axis=1, keepdims=True)
        exponent = jnp.exp(scores - row_max)
        weights = (exponent / jnp.sum(exponent, axis=1, keepdims=True)).astype(jnp.bfloat16)
        return jnp.dot(weights, values, preferred_element_type=jnp.float32).astype(jnp.bfloat16)

    blocks_out = lax.map(one_block, queries.reshape(length // query_rows, query_rows, hdim))
    return blocks_out.reshape(length, hdim)


def attend_pairs(pair_block):
    return lax.map(attend_one, pair_block[0])[None]


def add_terms(earlier, later):
    return earlier + later


def per_device(
    states,
    first_state,
    now_step,
    next_step,
    embed_weight,
    mod_weight,
    qkv_weight,
    out_weight,
    final_weight,
):
    step_count, tokd, chans = states.shape
    seq_devs = lax.axis_size("seq")
    time_index = lax.axis_index("tm")
    heads = qkv_weight.shape[1]
    width_three = qkv_weight.shape[2]
    hdim = width_three // 3
    width = heads * hdim
    edge_state = from_behind(states[-1], "tm", 1)
    opening = jnp.where(time_index == 0, first_state, edge_state)
    previous = jnp.concatenate([opening[None], states[:-1]], axis=0)
    keep_coef, noise_coef = coefficients(now_step, next_step)
    modulated_all = modulation(now_step, mod_weight)
    shift_mod = modulated_all[:, :width]
    scale_mod = modulated_all[:, width : 2 * width]
    gate_mod = modulated_all[:, 2 * width :]
    residual = jnp.einsum(
        "tsc,cd->tsd",
        previous.astype(jnp.bfloat16),
        embed_weight,
        preferred_element_type=jnp.float32,
    )
    modulated = (
        layer_norm(residual) * (1.0 + scale_mod[:, None, :]) + shift_mod[:, None, :]
    ).astype(jnp.bfloat16)
    columns = modulated
    projected = jnp.einsum(
        "tsd,dhc->thsc",
        columns,
        lax.all_gather(qkv_weight, "seq", axis=0, tiled=True),
        preferred_element_type=jnp.float32,
    ).astype(jnp.bfloat16)
    pair_count = step_count * heads
    per_dev = pair_count // seq_devs
    grouped = projected.reshape(seq_devs, per_dev, tokd, width_three)
    routed = attend_pairs(lax.all_to_all(grouped, "seq", split_axis=0, concat_axis=2, tiled=True))
    returned = lax.all_to_all(routed, "seq", split_axis=2, concat_axis=0, tiled=True)
    flattened = jnp.transpose(
        returned.reshape(step_count, heads, tokd, hdim), (0, 2, 1, 3)
    ).reshape(step_count, tokd, width)
    columns = flattened
    projection = jnp.einsum(
        "tsd,de->tse",
        columns,
        lax.all_gather(out_weight, "seq", axis=0, tiled=True),
        preferred_element_type=jnp.float32,
    )
    updated = residual + gate_mod[:, None, :] * projection
    normed_out = layer_norm(updated).astype(jnp.bfloat16)
    noise_pred = jnp.einsum(
        "tsd,dc->tsc", normed_out, final_weight, preferred_element_type=jnp.float32
    )
    drift_terms = keep_coef[:, None, None] * previous + noise_coef[:, None, None] * noise_pred
    running_sums = jnp.cumsum(drift_terms, axis=0)
    block_total = running_sums[-1]
    carried = entering(block_total, "tm", add_terms, jnp.zeros_like(block_total))
    advanced = first_state[None] + carried[None] + running_sums
    difference = advanced - states
    partial_value = jnp.sum(difference * difference, axis=(1, 2))
    errors = lax.psum(partial_value, "seq") / (tokd * seq_devs * chans)
    return (advanced, errors)


def solution(mesh):
    in_specs = (
        P("tm", "seq", None),
        P("seq", None),
        P("tm"),
        P("tm"),
        P(),
        P(),
        P("seq", None, None),
        P("seq", None),
        P(),
    )
    out_specs = (P("tm", "seq", None), P("tm"))
    return jax.shard_map(
        per_device, mesh=mesh, in_specs=in_specs, out_specs=out_specs, check_vma=False
    )
```

profile of v0, /device:TPU:0, one launch (start us, length us, event | category | flops | bytes accessed | tf_op | source)
XLA Modules:
  0.0 265.3 jit_solution(14366329195402225964)
XLA Ops:
  8.8 4.9 %collective-permute-start = (f32[48,64]{1,0:T(8,128)S(1)}, f32[48,64]{1,0:T(8,128)S(1)}, u32[]{:S(2)}, u32[]{:S(2)}) collective-permute-start(f32[48,64]{1,0:T(8,128)S(1)} %slice_bitcast_fusion), channel_id=1, source_target_pairs={{0,8},{8,16},{16,24},{1,9},{9,17},{17,25},{2,10},{10,18},{18,26},{... | collective-permute-start | bytes 36872 | tf_op jit(solution)/shard_map/ppermute | solution.py:12
  15.7 1.4 copy-done.1
  17.5 74.0 %all-gather.3.cloned.1.call-done = bf16[1536,12,384]{2,0,1:T(8,128)(2,1)} async-done(((bf16[192,12,384]{2,0,1:T(8,128)(2,1)}), bf16[1536,12,384]{2,0,1:T(8,128)(2,1)}) %all-gather.3.cloned.1.call-update) | async-done | bytes 14155792 | tf_op jit(solution)/shard_map/all_gather | solution.py:123
  91.5 11.1 %convert_bitcast_fusion = bf16[8,12,48,384]{3,2,1,0:T(8,128)(2,1)} fusion(bf16[1536,12,384]{2,0,1:T(8,128)(2,1)} %all-gather.3.cloned.1.call-done, f32[8,48,1536]{2,1,0:T(8,128)} %copy-done.1, f32[8,1536]{1,0:T(8,128)S(1)} %get-tuple-element.80, f32[8,1536]{1,0:T(8,128)S(1)} %get-tuple-element.81, f32[8,48]{1,0:T(8,128)S(1)} %add_rsqrt_fusion.1, ...), kind=kOutput, calls=%fused_computation.18 | convolution fusion | flops 5440536576 | bytes 20155392 | tf_op jit(solution)/shard_map/tsd,dhc->thsc/dot_general | solution.py:120
  102.5 4.5 %all-to-all-start = ((bf16[8,12,48,384]{3,2,1,0:T(8,128)(2,1)}), bf16[8,12,48,384]{3,2,1,0:T(8,128)(2,1)}, u32[]{:S(2)}, u32[]{:S(2)}) async-start(bf16[8,12,48,384]{3,2,1,0:T(8,128)(2,1)} %convert_bitcast_fusion), calls=%async_computation | async-start | bytes 7077888 | tf_op jit(solution)/shard_map/all_to_all | solution.py:129
  107.8 52.8 %all-to-all-done = bf16[8,12,48,384]{3,2,1,0:T(8,128)(2,1)} async-done(((bf16[8,12,48,384]{3,2,1,0:T(8,128)(2,1)}), bf16[8,12,48,384]{3,2,1,0:T(8,128)(2,1)}, u32[]{:S(2)}, u32[]{:S(2)}) %all-to-all-start) | async-done | bytes 3538976 | tf_op jit(solution)/shard_map/all_to_all | solution.py:129
  160.7 4.3 %copy.14 = bf16[1,12,8,48,384]{4,3,2,1,0:T(8,128)(2,1)} copy(bf16[1,12,8,48,384]{4,3,1,2,0:T(8,128)(2,1)} %bitcast.11) | data formatting | bytes 7077888 | tf_op jit(solution)/shard_map/all_to_all | solution.py:129
  164.9 27.9 %while.24 = (s32[]{:T(128)}, bf16[12,384,128]{2,1,0:T(8,128)(2,1)}, bf16[12,384,384]{2,1,0:T(8,128)(2,1)}, s32[]{:T(128)}) while((s32[]{:T(128)}, bf16[12,384,128]{2,1,0:T(8,128)(2,1)}, bf16[12,384,384]{2,1,0:T(8,128)(2,1)}, s32[]{:T(128)}) %tuple.57), condition=%wide.region_5.6_spmd, body=%wide.region_2.5_spmd.sunk | while | flops 76578048 | bytes 2761785 | solution.py:77
  164.9 1.0 dynamic-slice_bitcast_fusion.2
  167.2 1.0 dynamic-slice_bitcast_fusion.2
  169.6 1.0 dynamic-slice_bitcast_fusion.2
  171.9 1.0 dynamic-slice_bitcast_fusion.2
  176.5 1.0 dynamic-slice_bitcast_fusion.2
  178.9 1.0 dynamic-slice_bitcast_fusion.2
  181.2 1.0 dynamic-slice_bitcast_fusion.2
  185.8 1.0 dynamic-slice_bitcast_fusion.2
  188.2 1.0 dynamic-slice_bitcast_fusion.2
  192.8 3.3 %copy.18 = bf16[12,384,128]{2,0,1:T(8,128)(2,1)} copy(bf16[12,384,128]{2,1,0:T(8,128)(2,1)} %get-tuple-element.57) | data formatting | bytes 2359296 | tf_op jit(solution)/shard_map/while | solution.py:77
  196.1 4.3 %all-to-all-start.1 = ((bf16[1,12,384,128]{3,1,0,2:T(8,128)(2,1)}), bf16[1,12,384,128]{3,1,0,2:T(8,128)(2,1)}, u32[]{:S(2)}, u32[]{:S(2)}) async-start(bf16[1,12,384,128]{3,1,0,2:T(8,128)(2,1)} %bitcast.64), calls=%async_computation.1 | async-start | bytes 3145728 | tf_op jit(solution)/shard_map/all_to_all | solution.py:130
  200.5 20.9 %all-to-all-done.1 = bf16[1,12,384,128]{3,1,0,2:T(8,128)(2,1)} async-done(((bf16[1,12,384,128]{3,1,0,2:T(8,128)(2,1)}), bf16[1,12,384,128]{3,1,0,2:T(8,128)(2,1)}, u32[]{:S(2)}, u32[]{:S(2)}) %all-to-all-start.1) | async-done | bytes 1179680 | tf_op jit(solution)/shard_map/all_to_all | solution.py:130
  221.4 3.4 %reshape.52 = bf16[8,48,1536]{2,1,0:T(8,128)(2,1)} reshape(bf16[8,48,12,128]{3,2,1,0:T(8,128)(2,1)} %bitcast.17) | data formatting | bytes 2359296 | tf_op jit(solution)/shard_map/reshape | solution.py:133
  224.9 5.5 %fusion.51 = (f32[8,48]{1,0:T(8,128)S(1)}, f32[8,48,1536]{2,1,0:T(8,128)S(1)}) fusion(f32[8,48,1536]{2,1,0:T(8,128)} %copy-done.1, bf16[8,48,1536]{2,1,0:T(8,128)(2,1)} %reshape.52, bf16[1536,1536]{1,0:T(8,128)(2,1)} %all-gather.5.cloned.1.call-done, f32[8,1536]{1,0:T(8,128)S(1)} %get-tuple-element.79), kind=kOutput, calls=%fused_computation.74 | convolution fusion | flops 1813708416 | bytes 10667520 | tf_op jit(solution)/shard_map/tsd,de->tse/dot_general | solution.py:135
  232.0 13.5 %all_gather.11 = f32[4,48,64]{2,1,0:T(8,128)S(1)} all-gather(f32[1,48,64]{2,1,0:T(8,128)S(1)} %slice.39), channel_id=1, replica_groups=mesh['tm'=4,'seq'=8] {'tm'}, dimensions={0}, use_global_device_ids=true | all-gather | bytes 61440 | tf_op jit(solution)/shard_map/all_gather | solution.py:17
  246.2 11.8 %psum.7 = f32[8]{0:T(128)S(1)} all-reduce(f32[8]{0:T(128)S(1)} %get-tuple-element.73), channel_id=1, replica_groups=mesh['tm'=4,'seq'=8] {'seq'}, use_global_device_ids=true, to_apply=%region_12.13 | all-reduce | flops 8 | bytes 64 | tf_op jit(solution)/shard_map/psum | solution.py:153
  (86 shorter events, 26.5 us)
Async XLA Ops:
  7.2 7.3 %copy-start = (bf16[256,4608]{1,0:T(8,128)(2,1)S(1)}, bf16[256,4608]{1,0:T(8,128)(2,1)}, u32[]{:S(2)}) copy-start(bf16[256,4608]{1,0:T(8,128)(2,1)} %param.18) | copy-start | bytes 7077892
  7.2 7.7 %copy-start.2 = (f32[8,48,64]{2,1,0:T(8,128)S(1)}, f32[8,48,64]{2,1,0:T(8,128)}, u32[]{:S(2)}) copy-start(f32[8,48,64]{2,1,0:T(8,128)} %param.13) | copy-start | bytes 294916
  7.2 8.0 %copy-start.5 = (f32[48,64]{1,0:T(8,128)S(1)}, f32[48,64]{1,0:T(8,128)}, u32[]{:S(2)}) copy-start(f32[48,64]{1,0:T(8,128)} %param.14) | copy-start | bytes 36868
  7.2 8.0 %copy-start.4 = (bf16[64,1536]{1,0:T(8,128)(2,1)S(1)}, bf16[64,1536]{1,0:T(8,128)(2,1)}, u32[]{:S(2)}) copy-start(bf16[64,1536]{1,0:T(8,128)(2,1)} %param.17) | copy-start | bytes 589828
  7.2 84.3 %all-gather.3.cloned.1.call-start = ((), (), s32[]{:S(2)}) async-start(), calls=%async_computation.2 | async-start | bytes 15925248 | tf_op jit(solution)/shard_map/all_gather | solution.py:123
  8.8 6.4 %collective-permute-start = (f32[48,64]{1,0:T(8,128)S(1)}, f32[48,64]{1,0:T(8,128)S(1)}, u32[]{:S(2)}, u32[]{:S(2)}) collective-permute-start(f32[48,64]{1,0:T(8,128)S(1)} %slice_bitcast_fusion), channel_id=1, source_target_pairs={{0,8},{8,16},{16,24},{1,9},{9,17},{17,25},{2,10},{10,18},{18,26},{... | collective-permute-start | bytes 36872 | tf_op jit(solution)/shard_map/ppermute | solution.py:12
  15.7 1.4 copy-start.1
  102.5 58.1 %all-to-all-start = ((bf16[8,12,48,384]{3,2,1,0:T(8,128)(2,1)}), bf16[8,12,48,384]{3,2,1,0:T(8,128)(2,1)}, u32[]{:S(2)}, u32[]{:S(2)}) async-start(bf16[8,12,48,384]{3,2,1,0:T(8,128)(2,1)} %convert_bitcast_fusion), calls=%async_computation | async-start | bytes 7077888 | tf_op jit(solution)/shard_map/all_to_all | solution.py:129
  107.1 117.8 %all-gather.5.cloned.1.call-start = ((), (), s32[]{:S(2)}) async-start(), calls=%async_computation.3 | async-start | bytes 5308416 | tf_op jit(solution)/shard_map/all_gather | solution.py:138
  192.8 7.6 %copy-start.6 = (s32[8]{0:T(128)S(1)}, s32[8]{0:T(128)}, u32[]{:S(2)}) copy-start(s32[8]{0:T(128)} %param.15) | copy-start | bytes 100
  192.8 7.6 %copy-start.7 = (s32[8]{0:T(128)S(1)}, s32[8]{0:T(128)}, u32[]{:S(2)}) copy-start(s32[8]{0:T(128)} %param.16) | copy-start | bytes 100
  196.1 25.3 %all-to-all-start.1 = ((bf16[1,12,384,128]{3,1,0,2:T(8,128)(2,1)}), bf16[1,12,384,128]{3,1,0,2:T(8,128)(2,1)}, u32[]{:S(2)}, u32[]{:S(2)}) async-start(bf16[1,12,384,128]{3,1,0,2:T(8,128)(2,1)} %bitcast.64), calls=%async_computation.1 | async-start | bytes 3145728 | tf_op jit(solution)/shard_map/all_to_all | solution.py:130
  230.4 0.9 copy-start.3
Sparse Core Ops, SparseCore 0:
  9.9 81.4 all-gather.2
  109.8 59.9 all-gather.4
where the time goes:
time: 266 us; the launch traced here: 265 us
  waiting for transfers between devices  149 us (56%)
  matrix products  32.5 us (12%)
  local copies, waits for them, and re-layouts  25.6 us (10%)
  blocking collectives  25.2 us (9%)
  between operations  14.2 us (5%)
  starting transfers between devices  13.8 us (5%)
  other arithmetic  4.53 us (2%)
    all_gather x1, waiting for transfers between devices, per_device(): lax.all_gather(qkv_weight, 'seq', axis=0, tiled=True)  74 us
    all_to_all x1, waiting for transfers between devices, per_device(): lax.all_to_all(grouped, 'seq', split_axis=0, concat_axis=2, tiled=True)  52.8 us
    all_to_all x1, waiting for transfers between devices, per_device(): lax.all_to_all(routed, 'seq', split_axis=2, concat_axis=0, tiled=True)  20.9 us
    all_gather x1, blocking collectives, entering(): gathered = lax.all_gather(part, axis)  13.5 us
    squeeze x12, local copies, waits for them, and re-layouts, attend_pairs(): return lax.map(attend_one, pair_block[0])[None]  11.9 us
    psum x1, blocking collectives, per_device(): errors = lax.psum(partial_value, 'seq') / (tokd * seq_devs * chans)  11.8 us
    dot_general x12, matrix products, one_block(): jnp.dot(weights, values, preferred_element_type=jnp.float32)  11.1 us
    dot_general x1, matrix products, per_device(): jnp.einsum('tsd,dhc->thsc', columns, lax.all_gather(qkv_weight, 'seq', ax...  11.1 us
  transfers between devices with their start and end apart: 5, of which 4 were waited for; matrix products, arithmetic and copies ran while one was open for 16% of the time, Pallas kernels for 0%

commit v1 on v0

v1 whole, which is shorter than its diff:
```python
import functools
import math

import jax
import jax.numpy as jnp
from jax import lax
from jax.experimental import pallas as pl
from jax.experimental.pallas import tpu as pltpu
from jax.sharding import PartitionSpec as P

BF = jnp.bfloat16
F32 = jnp.float32
ROWS = 80
VMEM_LIMIT = 48 * 1024 * 1024


def dot(a, b, dims=((1,), (0,))):
    return lax.dot_general(a, b, (dims, ((), ())), preferred_element_type=F32)


def alpha_bar(step_ids):
    fraction = (step_ids.astype(F32) / 1000.0 + 0.008) / 1.008
    return jnp.cos(fraction * (math.pi / 2)) ** 2


def coefficients(now_step, next_step):
    alpha_now = alpha_bar(now_step)
    alpha_next = alpha_bar(next_step)
    step_ratio = jnp.sqrt(alpha_next / alpha_now)
    keep_coef = step_ratio - 1.0
    noise_coef = jnp.sqrt(1.0 - alpha_next) - step_ratio * jnp.sqrt(1.0 - alpha_now)
    return (keep_coef, noise_coef)


def modulation(step_ids, mod_weight):
    half_freq = mod_weight.shape[0] // 2
    frequency = jnp.exp(-math.log(10000.0) * jnp.arange(half_freq, dtype=F32) / half_freq)
    angles = step_ids.astype(F32)[:, None] * frequency[None, :]
    time_embed = jnp.concatenate([jnp.cos(angles), jnp.sin(angles)], axis=1).astype(BF)
    return jnp.dot(time_embed, mod_weight, preferred_element_type=F32)


def prepare_kernel(steps, per, sub, embed_ref, mod_ref, w_ref, out_ref, b_scr):
    chans, width = embed_ref.shape
    embed = embed_ref[...].astype(F32)
    centred = embed - jnp.mean(embed, axis=1, keepdims=True)
    pad = jnp.zeros((ROWS - chans - 8, width), F32)
    first = lax.broadcasted_iota(jnp.int32, (8, width), 0) == 0
    for t in range(steps):
        shift = mod_ref[t : t + 1, :width]
        scale = mod_ref[t : t + 1, width : 2 * width]
        tail = jnp.where(first, jnp.broadcast_to(shift, (8, width)), 0.0)
        rows = jnp.concatenate([centred * (1.0 + scale), tail, pad], axis=0)
        b_scr[t * ROWS : (t + 1) * ROWS, :] = rows.astype(BF)
    cols = per * sub
    a_all = dot(b_scr[...], w_ref[...]).astype(BF)
    for t in range(steps):
        a_t = a_all[t * ROWS : (t + 1) * ROWS]
        for i in range(per):
            q = a_t[:, i * sub : (i + 1) * sub]
            k = a_t[:, cols + i * sub : cols + (i + 1) * sub]
            prod = dot(q, k, ((1,), (1,)))
            out_ref[t, :, i * chans : (i + 1) * chans] = prod[:, :chans].astype(BF)
        out_ref[t, :, per * chans :] = a_t[:, 2 * cols :]


def prepare(embed, mod_all, w_mine, steps, per, sub):
    chans = embed.shape[0]
    return pl.pallas_call(
        functools.partial(prepare_kernel, steps, per, sub),
        out_shape=jax.ShapeDtypeStruct((steps, ROWS, per * (chans + sub)), BF),
        scratch_shapes=[pltpu.VMEM((steps * ROWS, embed.shape[1]), BF)],
        compiler_params=pltpu.CompilerParams(vmem_limit_bytes=VMEM_LIMIT),
        name="prepare",
    )(embed, mod_all, w_mine)


def attend_kernel(heads, n_sub, per, sub, embed_ref, keys_ref, queries_ref, pay_ref, out_ref):
    chans, width = embed_ref.shape
    hdim = n_sub * sub
    embed = embed_ref[...].astype(F32)
    centred = embed - jnp.mean(embed, axis=1, keepdims=True)
    centred = centred.astype(BF)

    def inverse_dev(p):
        rows = dot(p, embed_ref[...])
        mean = jnp.mean(rows, axis=1, keepdims=True)
        rows = rows - mean
        return lax.rsqrt(jnp.mean(rows * rows, axis=1, keepdims=True) + 1e-6)

    keys = keys_ref[...]
    keys_t = keys.astype(F32).T.astype(BF)
    queries = queries_ref[...]
    key_dev = inverse_dev(keys)
    query_dev = inverse_dev(queries)
    factor = hdim**-0.5 * math.log2(math.e)
    halves = []
    for h in range(heads):
        product = None
        value_parts = []
        for j in range(n_sub):
            source, slot = divmod(h * n_sub + j, per)
            part = pay_ref[source, :, slot * chans : (slot + 1) * chans].astype(F32)
            product = part if product is None else product + part
            start = per * chans + slot * sub
            value_parts.append(pay_ref[source, :, start : start + sub])
        value = jnp.concatenate(value_parts, axis=1) if n_sub > 1 else value_parts[0]
        side = dot(queries, product[:chans].astype(BF)) * query_dev + product[chans : chans + 1]
        side = (side * factor).astype(BF)
        scores = dot(keys, side, ((1,), (1,))) * key_dev
        top = jnp.max(scores, axis=0, keepdims=True)
        weights = jnp.exp2(scores - top)
        total = jnp.sum(weights, axis=0, keepdims=True)
        mixed = dot(keys_t, (weights * key_dev).astype(BF)) / total
        mixed = mixed.T.astype(BF)
        result = dot(mixed, value[:chans]) + value[chans : chans + 1].astype(F32)
        out_ref[:, h * hdim : (h + 1) * hdim] = result.astype(BF)


def attend(embed, keys, queries, payload, heads, n_sub, per, sub):
    return pl.pallas_call(
        functools.partial(attend_kernel, heads, n_sub, per, sub),
        out_shape=jax.ShapeDtypeStruct((queries.shape[0], heads * n_sub * sub), BF),
        compiler_params=pltpu.CompilerParams(vmem_limit_bytes=VMEM_LIMIT),
        name="attend",
    )(embed, keys, queries, payload)


def finish_kernel(embed_ref, queries_ref, att_ref, wo_ref, gate_ref, final_ref, out_ref):
    residual = dot(queries_ref[...], embed_ref[...])
    updated = residual + gate_ref[...] * dot(att_ref[...], wo_ref[...])
    mean = jnp.mean(updated, axis=1, keepdims=True)
    centred = updated - mean
    variance = jnp.mean(centred * centred, axis=1, keepdims=True)
    normed = (centred * lax.rsqrt(variance + 1e-6)).astype(BF)
    out_ref[...] = dot(normed, final_ref[...])


def finish(embed, queries, att, wo, gate, final):
    return pl.pallas_call(
        finish_kernel,
        out_shape=jax.ShapeDtypeStruct((queries.shape[0], final.shape[1]), F32),
        compiler_params=pltpu.CompilerParams(vmem_limit_bytes=VMEM_LIMIT),
        name="finish",
    )(embed, queries, att, wo, gate, final)


def swap(x, mask, count):
    return lax.ppermute(x, "seq", [(i, i ^ mask) for i in range(count)])


def gather_rows(shard, count):
    if count != 8:
        return lax.all_gather(shard, "seq", axis=0, tiled=True)
    half = shard.shape[0] // 2
    a, b = shard[:half], shard[half:]
    xa, yb = swap(a, 2, count), swap(b, 4, count)
    ya, xya = swap(a, 4, count), swap(xa, 4, count)
    xb, xyb = swap(b, 2, count), swap(yb, 2, count)
    mine = jnp.stack([a, b, xa, xb, ya, yb, xya, xyb]).reshape(4, 2 * half, -1)
    other = swap(mine, 1, count)
    index = lax.axis_index("seq")
    core, chip = index % 2, index // 2
    first = jnp.where(core == 0, mine, other)
    second = jnp.where(core == 0, other, mine)
    pairs = jnp.stack([first, second], axis=1)
    order = jnp.arange(4) ^ chip
    return jnp.take(pairs, order, axis=0).reshape(count * shard.shape[0], -1)


def earlier_total(total, count):
    place = lax.axis_index("tm")
    carried = jnp.zeros_like(total)
    for by in range(1, count):
        carried += lax.ppermute(total, "tm", [(i, i + by) for i in range(count - by)])
    return carried


def per_device(
    states,
    first_state,
    now_step,
    next_step,
    embed_weight,
    mod_weight,
    qkv_weight,
    out_weight,
    final_weight,
):
    steps, tokd, chans = states.shape
    count = lax.axis_size("seq")
    tm_count = lax.axis_size("tm")
    time_index = lax.axis_index("tm")
    seq_index = lax.axis_index("seq")
    rows, heads, width_three = qkv_weight.shape
    hdim = width_three // 3
    width = heads * hdim
    share = count // steps
    n_sub = count // math.gcd(count, heads)
    per = heads * n_sub // count
    sub = hdim // n_sub

    w = qkv_weight.reshape(rows, heads, 3, n_sub, sub)
    w = w.transpose(1, 3, 0, 2, 4).reshape(count, per, rows, 3, sub)
    w = w.transpose(0, 2, 3, 1, 4).reshape(count, rows, 3 * per * sub)
    w_mine = lax.all_to_all(w, "seq", 0, 0, tiled=True).reshape(count * rows, 3 * per * sub)
    wo = gather_rows(out_weight, count)

    edge = lax.ppermute(states[-1], "tm", [(i, i + 1) for i in range(tm_count - 1)])
    opening = jnp.where(time_index == 0, first_state, edge)
    previous = jnp.concatenate([opening[None], states[:-1]], axis=0)
    sent = jnp.repeat(previous.astype(BF), share, axis=0)
    keys = lax.all_to_all(sent, "seq", 0, 0, tiled=True).reshape(count * tokd, chans)
    length = count * tokd // share
    mine = seq_index // share
    part = seq_index % share
    queries = lax.dynamic_slice_in_dim(keys, part * length, length, 0) if share > 1 else keys

    keep_coef, noise_coef = coefficients(now_step, next_step)
    mod_all = modulation(now_step, mod_weight)
    payload = prepare(embed_weight, mod_all, w_mine, steps, per, sub)
    payload = jnp.repeat(payload, share, axis=0)
    payload = lax.all_to_all(payload, "seq", 0, 0, tiled=True)
    att = attend(embed_weight, keys, queries, payload, heads, n_sub, per, sub)
    gate = lax.dynamic_slice(mod_all, (mine, 2 * width), (1, width))
    noise = finish(embed_weight, queries, att, wo, gate, final_weight)

    noise = noise.reshape(count // share, tokd, chans)
    if share > 1:
        full = jnp.zeros((share,) + noise.shape, F32)
        noise = lax.dynamic_update_slice(full, noise[None], (part, 0, 0, 0))
        noise = noise.reshape(count, tokd, chans)
    noise = lax.all_to_all(noise, "seq", 0, 0, tiled=True)
    if share > 1:
        noise = noise.reshape(steps, share, tokd, chans)
        own = seq_index // (count // share)
        noise = lax.dynamic_index_in_dim(noise, own, 1, False)

    drift_terms = keep_coef[:, None, None] * previous + noise_coef[:, None, None] * noise
    running_sums = jnp.cumsum(drift_terms, axis=0)
    carried = earlier_total(running_sums[-1], tm_count)
    advanced = first_state[None] + carried[None] + running_sums
    difference = advanced - states
    partial_value = jnp.sum(difference * difference, axis=(1, 2))
    errors = lax.psum(partial_value, "seq") / (tokd * count * chans)
    return (advanced, errors)


def solution(mesh):
    in_specs = (
        P("tm", "seq", None),
        P("seq", None),
        P("tm"),
        P("tm"),
        P(),
        P(),
        P("seq", None, None),
        P("seq", None),
        P(),
    )
    out_specs = (P("tm", "seq", None), P("tm"))
    return jax.shard_map(
        per_device, mesh=mesh, in_specs=in_specs, out_specs=out_specs, check_vma=False
    )
```

time: 266 us -> 166 us (0.62)
  waiting for transfers between devices: 149 us -> 45.1 us
  matrix products: 32.5 us -> 0.41 us
  starting transfers between devices: 13.8 us -> 35.4 us
  Pallas kernels: 0 us -> 19 us
  blocking collectives: 25.2 us -> 11.8 us
  between operations: 14.2 us -> 1 us
  other arithmetic: 4.53 us -> 16.6 us
  local copies, waits for them, and re-layouts: 25.6 us -> 36 us
    all_gather x2 -> x0, waiting for transfers between devices: 74 us -> none  [the longest x1 74 us: per_device(): lax.all_gather(qkv_weight, 'seq', axis=0, tiled=True)]
    all_to_all x2 -> x4, waiting for transfers between devices: 73.7 us -> 31.1 us  [the longest x1 18.7 us: per_device(): lax.all_to_all(w, 'seq', 0, 0, tiled=True)]
    dot_general x29 -> x1, matrix products: 32.5 us -> 0.41 us  [modulation(): return jnp.dot(time_embed, mod_weight, preferred_element_type=F32)]
    pallas_call x0 -> x3, Pallas kernels: none -> 19 us  [the longest x1 8.6 us: attend(): pl.pallas_call(functools.partial(attend_kernel, heads, n_sub, per, sub),...]
    unnamed x16 -> x51, local copies, waits for them, and re-layouts: 1.95 us -> 20.3 us
    ppermute x1 -> x11, starting transfers between devices: 4.92 us -> 20.1 us  [the longest x3 9.28 us: earlier_total(): lax.ppermute(total, 'tm', [(i, i + by) for i in range(count - by)])]
    ppermute x1 -> x11, waiting for transfers between devices: 0.23 us -> 14 us  [the longest x7 11.7 us: swap(): return lax.ppermute(x, 'seq', [(i, i ^ mask) for i in range(count)])]
    all_gather x1 -> x0, blocking collectives: 13.5 us -> none  [entering(): gathered = lax.all_gather(part, axis)]
  transfers between devices with their start and end apart: 5 -> 15, of which waited for: 4 -> 9; matrix products, arithmetic and copies ran while one was open for 16% -> 14% of each run, Pallas kernels for 0% -> 8%
where the time goes in v1:
time: 166 us; the launch traced here: 165 us
  waiting for transfers between devices  45.1 us (27%)
  local copies, waits for them, and re-layouts  36 us (22%)
  starting transfers between devices  35.4 us (21%)
  Pallas kernels  19 us (11%)
  other arithmetic  16.6 us (10%)
  blocking collectives  11.8 us (7%)
    unnamed x51, local copies, waits for them, and re-layouts  20.3 us
    all_to_all x1, waiting for transfers between devices, per_device(): lax.all_to_all(w, 'seq', 0, 0, tiled=True)  18.7 us
    psum x1, blocking collectives, per_device(): errors = lax.psum(partial_value, 'seq') / (tokd * count * chans)  11.8 us
    ppermute x7, waiting for transfers between devices, swap(): return lax.ppermute(x, 'seq', [(i, i ^ mask) for i in range(count)])  11.7 us
    ppermute x3, starting transfers between devices, earlier_total(): lax.ppermute(total, 'tm', [(i, i + by) for i in range(count - by)])  9.28 us
    pallas_call x1, Pallas kernels, attend(): pl.pallas_call(functools.partial(attend_kernel, heads, n_sub, per, sub),...  8.6 us
    all_to_all x1, waiting for transfers between devices, per_device(): payload = lax.all_to_all(payload, 'seq', 0, 0, tiled=True)  8.02 us
    ppermute x7, starting transfers between devices, swap(): return lax.ppermute(x, 'seq', [(i, i ^ mask) for i in range(count)])  7.24 us
  transfers between devices with their start and end apart: 15, of which 9 were waited for; matrix products, arithmetic and copies ran while one was open for 14% of the time, Pallas kernels for 8%

profile of v1, /device:TPU:0, one launch (start us, length us, event | category | flops | bytes accessed | tf_op | source)
XLA Modules:
  0.0 165.4 jit_solution(5515060734361080251)
XLA Ops:
  1.9 3.0 %collective-permute-start.1 = (bf16[96,1536]{1,0:T(8,128)(2,1)S(1)}, bf16[96,1536]{1,0:T(8,128)(2,1)S(1)}, u32[]{:S(2)}, u32[]{:S(2)}) collective-permute-start(bf16[96,1536]{1,0:T(8,128)(2,1)S(1)} %get-tuple-element.9), channel_id=1, source_target_pairs={{0,2},{1,3},{2,0},{3,1},{4,6},{5,7},{6,4},{7,5},{8,10},{9,11},{10,... | collective-permute-start | bytes 884744 | tf_op jit(solution)/shard_map/ppermute | solution.py:149
  10.4 2.3 %collective-permute-done.1 = bf16[96,1536]{1,0:T(8,128)(2,1)S(1)} collective-permute-done((bf16[96,1536]{1,0:T(8,128)(2,1)S(1)}, bf16[96,1536]{1,0:T(8,128)(2,1)S(1)}, u32[]{:S(2)}, u32[]{:S(2)}) %collective-permute-start.1) | collective-permute-done | bytes 294944 | tf_op jit(solution)/shard_map/ppermute | solution.py:149
  12.7 2.1 %collective-permute-start.5 = (bf16[96,1536]{1,0:T(8,128)(2,1)S(1)}, bf16[96,1536]{1,0:T(8,128)(2,1)S(1)}, u32[]{:S(2)}, u32[]{:S(2)}) collective-permute-start(bf16[96,1536]{1,0:T(8,128)(2,1)S(1)} %collective-permute-done.1), channel_id=1, source_target_pairs={{0,4},{1,5},{2,6},{3,7},{4,0},{5,1},{6,2},{7,3},{8,12},{9,13},{10,... | collective-permute-start | bytes 884744 | tf_op jit(solution)/shard_map/ppermute | solution.py:149
  14.8 6.3 %collective-permute-done.4 = bf16[96,1536]{1,0:T(8,128)(2,1)S(1)} collective-permute-done((bf16[96,1536]{1,0:T(8,128)(2,1)S(1)}, bf16[96,1536]{1,0:T(8,128)(2,1)S(1)}, u32[]{:S(2)}, u32[]{:S(2)}) %collective-permute-start.4) | collective-permute-done | bytes 294944 | tf_op jit(solution)/shard_map/ppermute | solution.py:149
  28.6 4.0 %copy.17 = bf16[192,12,384]{0,2,1:T(8,128)(2,1)} copy(bf16[192,12,384]{2,0,1:T(8,128)(2,1)} %param.15) | data formatting | bytes 3538944 | tf_op args[6]
  36.0 4.2 %copy.20 = bf16[8,192,576]{2,1,0:T(8,128)(2,1)} copy(bf16[8,192,576]{1,2,0:T(8,128)(2,1)} %bitcast.50) | data formatting | bytes 3538944 | tf_op jit(solution)/shard_map/reshape | solution.py:205
  40.2 4.5 %all-to-all-start.1 = ((bf16[8,192,576]{2,1,0:T(8,128)(2,1)}), bf16[8,192,576]{2,1,0:T(8,128)(2,1)}, u32[]{:S(2)}, u32[]{:S(2)}) async-start(bf16[8,192,576]{2,1,0:T(8,128)(2,1)} %copy.20), calls=%async_computation.1 | async-start | bytes 3932160 | tf_op jit(solution)/shard_map/all_to_all | solution.py:206
  44.8 3.6 %collective-permute-start = (f32[48,64]{1,0:T(8,128)S(1)}, f32[48,64]{1,0:T(8,128)S(1)}, u32[]{:S(2)}, u32[]{:S(2)}) collective-permute-start(f32[48,64]{1,0:T(8,128)S(1)} %slice_bitcast_fusion.1), channel_id=1, source_target_pairs={{0,8},{8,16},{16,24},{1,9},{9,17},{17,25},{2,10},{10,18},{18,26},{... | collective-permute-start | bytes 36872 | tf_op jit(solution)/shard_map/ppermute | solution.py:209
  51.3 18.7 %all-to-all-done.1 = bf16[8,192,576]{2,1,0:T(8,128)(2,1)} async-done(((bf16[8,192,576]{2,1,0:T(8,128)(2,1)}), bf16[8,192,576]{2,1,0:T(8,128)(2,1)}, u32[]{:S(2)}, u32[]{:S(2)}) %all-to-all-start.1) | async-done | bytes 1769504 | tf_op jit(solution)/shard_map/all_to_all | solution.py:206
  70.0 3.3 %all-to-all-start = ((bf16[8,2,1536]{2,1,0:T(2,128)(2,1)}), bf16[8,2,1536]{2,1,0:T(2,128)(2,1)S(1)}, u32[]{:S(2)}, u32[]{:S(2)}) async-start(bf16[8,2,1536]{2,1,0:T(2,128)(2,1)} %reshape.74), calls=%async_computation | async-start | bytes 98304 | tf_op jit(solution)/shard_map/all_to_all | solution.py:213
  74.5 4.5 %prepare.1 = bf16[8,80,384]{2,1,0:T(8,128)(2,1)} custom-call(bf16[64,1536]{1,0:T(8,128)(2,1)S(1)} %copy-done.3, f32[8,4608]{1,0:T(8,128)S(1)} %fusion.9.mod_ref, bf16[1536,576]{1,0:T(8,128)(2,1)} %bitcast.8.w_ref), custom_call_target="tpu_custom_call" | custom-call | tf_op jit(solution)/shard_map/prepare/pallas_call | solution.py:69
  78.9 4.1 %all-to-all-start.2 = ((bf16[8,80,384]{2,1,0:T(8,128)(2,1)}), bf16[8,80,384]{2,1,0:T(8,128)(2,1)S(1)}, u32[]{:S(2)}, u32[]{:S(2)}) async-start(bf16[8,80,384]{2,1,0:T(8,128)(2,1)} %prepare.1), calls=%async_computation.2 | async-start | bytes 983040 | tf_op jit(solution)/shard_map/all_to_all | solution.py:223
  84.4 8.0 %all-to-all-done.2.pay_ref = bf16[8,80,384]{2,1,0:T(8,128)(2,1)S(1)} async-done(((bf16[8,80,384]{2,1,0:T(8,128)(2,1)}), bf16[8,80,384]{2,1,0:T(8,128)(2,1)S(1)}, u32[]{:S(2)}, u32[]{:S(2)}) %all-to-all-start.2) | async-done | bytes 491552 | tf_op jit(solution)/shard_map/all_to_all | solution.py:223
  96.1 8.6 %attend.1.att_ref = bf16[384,1536]{1,0:T(8,128)(2,1)S(1)} custom-call(bf16[64,1536]{1,0:T(8,128)(2,1)S(1)} %copy-done.4, bf16[384,64]{1,0:T(8,128)(2,1)S(1)} %bitcast.45, bf16[384,64]{1,0:T(8,128)(2,1)S(1)} %bitcast.46, bf16[8,80,384]{2,1,0:T(8,128)(2,1)S(1)} %copy-done.2), custom_call_target="tpu_custom_call" | custom-call | tf_op jit(solution)/shard_map/attend/pallas_call | solution.py:121
  104.7 2.7 %select_bitcast_fusion.1 = (bf16[4,1,192,1536]{3,2,0,1:T(8,128)(2,1)S(1)}, bf16[4,1,192,1536]{3,2,0,1:T(8,128)(2,1)S(1)}) fusion(bf16[4,192,1536]{2,1,0:T(8,128)(2,1)} %collective-permute-done.7, pred[]{:T(512)S(6)} %eq.10, bf16[4,192,1536]{2,1,0:T(8,128)(2,1)} %bitcast.44), kind=kLoop, calls=%fused_computation.4 | loop fusion | flops 2359296 | bytes 9437185 | tf_op jit(solution)/shard_map/stack | solution.py:166
  107.4 2.6 %pad_maximum_fusion = bf16[4,2,192,1536]{3,2,0,1:T(8,128)(2,1)} fusion(bf16[4,1,192,1536]{3,2,0,1:T(8,128)(2,1)S(1)} %get-tuple-element.7, bf16[4,1,192,1536]{3,2,0,1:T(8,128)(2,1)S(1)} %get-tuple-element.6), kind=kLoop, calls=%fused_computation.1 | loop fusion | flops 2359296 | bytes 9437184 | tf_op jit(solution)/shard_map/stack | solution.py:166
  110.0 5.3 %gather_fusion = bf16[4,2,192,1536]{3,2,1,0:T(8,128)(2,1)} fusion(bf16[4,2,192,1536]{3,2,0,1:T(8,128)(2,1)} %pad_maximum_fusion, s32[1024]{0:T(1024)S(1)} %pad_clamp_fusion), kind=kCustom, calls=%fused_computation | custom fusion | bytes 9437200 | tf_op jit(solution)/shard_map/jit(_take)/gather | solution.py:168
  115.3 5.1 %bitcast_select_fusion.wo_ref = bf16[1536,1536]{1,0:T(8,128)(2,1)} fusion(bf16[4,2,192,1536]{3,2,1,0:T(8,128)(2,1)} %gather_fusion, pred[1536]{0:T(1024)(128)(4,1)S(1)} %broadcast_in_dim.25), kind=kLoop, calls=%fused_computation.2 | loop fusion | flops 2359296 | bytes 9438720 | tf_op jit(solution)/shard_map/jit(_take)/select_n | solution.py:168
  120.4 6.0 %finish.1 = f32[384,64]{1,0:T(8,128)S(1)} custom-call(bf16[64,1536]{1,0:T(8,128)(2,1)S(1)} %copy-done.5, bf16[384,64]{1,0:T(8,128)(2,1)S(1)} %bitcast.47, bf16[384,1536]{1,0:T(8,128)(2,1)S(1)} %attend.1.att_ref, bf16[1536,1536]{1,0:T(8,128)(2,1)} %bitcast_select_fusion.wo_ref, f32[1,1536]{1,0:T(1,128)S(1)} %constant_dynamic-slice_fusion.gate_ref, ...), custom_call_target="tpu_custom_call" | custom-call | tf_op jit(solution)/shard_map/finish/pallas_call | solution.py:140
  128.8 3.4 %all-to-all-start.3 = ((f32[8,1,3072]{2,1,0:T(1,128)}), f32[8,1,3072]{2,1,0:T(1,128)S(1)}, u32[]{:S(2)}, u32[]{:S(2)}) async-start(f32[8,1,3072]{2,1,0:T(1,128)} %reshape.76), calls=%async_computation.3 | async-start | bytes 196608 | tf_op jit(solution)/shard_map/all_to_all | solution.py:233
  132.9 4.4 %all-to-all-done.3 = f32[8,1,3072]{2,1,0:T(1,128)S(1)} async-done(((f32[8,1,3072]{2,1,0:T(1,128)}), f32[8,1,3072]{2,1,0:T(1,128)S(1)}, u32[]{:S(2)}, u32[]{:S(2)}) %all-to-all-start.3) | async-done | bytes 98336 | tf_op jit(solution)/shard_map/all_to_all | solution.py:233
  139.8 5.5 %collective-permute-start.10 = (f32[48,64]{1,0:T(8,128)S(1)}, f32[48,64]{1,0:T(8,128)S(1)}, u32[]{:S(2)}, u32[]{:S(2)}) collective-permute-start(f32[48,64]{1,0:T(8,128)S(1)} %slice_bitcast_fusion), channel_id=1, source_target_pairs={{0,24},{1,25},{2,26},{3,27},{4,28},{5,29},{6,30},{7,31}} | collective-permute-start | bytes 36872 | tf_op jit(solution)/shard_map/ppermute | solution.py:175
  146.7 2.5 %collective-permute-start.9 = (f32[48,64]{1,0:T(8,128)S(1)}, f32[48,64]{1,0:T(8,128)S(1)}, u32[]{:S(2)}, u32[]{:S(2)}) collective-permute-start(f32[48,64]{1,0:T(8,128)S(1)} %slice_bitcast_fusion), channel_id=1, source_target_pairs={{0,16},{8,24},{1,17},{9,25},{2,18},{10,26},{3,19},{11,27},{4,20},{... | collective-permute-start | bytes 36872 | tf_op jit(solution)/shard_map/ppermute | solution.py:175
  153.1 11.8 %psum.7 = f32[8]{0:T(128)S(1)} all-reduce(f32[8]{0:T(128)S(1)} %get-tuple-element.2), channel_id=1, replica_groups=mesh['tm'=4,'seq'=8] {'seq'}, use_global_device_ids=true, to_apply=%region_2.3 | all-reduce | flops 8 | bytes 64 | tf_op jit(solution)/shard_map/psum | solution.py:245
  (93 shorter events, 38.0 us)
Async XLA Ops:
  0.6 48.0 %copy-start = (bf16[256,4608]{1,0:T(8,128)(2,1)S(1)}, bf16[256,4608]{1,0:T(8,128)(2,1)}, u32[]{:S(2)}) copy-start(bf16[256,4608]{1,0:T(8,128)(2,1)} %param.14) | copy-start | bytes 7077892
  1.9 10.8 %collective-permute-start.1 = (bf16[96,1536]{1,0:T(8,128)(2,1)S(1)}, bf16[96,1536]{1,0:T(8,128)(2,1)S(1)}, u32[]{:S(2)}, u32[]{:S(2)}) collective-permute-start(bf16[96,1536]{1,0:T(8,128)(2,1)S(1)} %get-tuple-element.9), channel_id=1, source_target_pairs={{0,2},{1,3},{2,0},{3,1},{4,6},{5,7},{6,4},{7,5},{8,10},{9,11},{10,... | collective-permute-start | bytes 884744 | tf_op jit(solution)/shard_map/ppermute | solution.py:149
  4.9 17.7 %collective-permute-start.3 = (bf16[96,1536]{1,0:T(8,128)(2,1)S(1)}, bf16[96,1536]{1,0:T(8,128)(2,1)S(1)}, u32[]{:S(2)}, u32[]{:S(2)}) collective-permute-start(bf16[96,1536]{1,0:T(8,128)(2,1)S(1)} %get-tuple-element.9), channel_id=1, source_target_pairs={{0,4},{1,5},{2,6},{3,7},{4,0},{5,1},{6,2},{7,3},{8,12},{9,13},{10,... | collective-permute-start | bytes 884744 | tf_op jit(solution)/shard_map/ppermute | solution.py:149
  6.4 15.5 %collective-permute-start.2 = (bf16[96,1536]{1,0:T(8,128)(2,1)S(1)}, bf16[96,1536]{1,0:T(8,128)(2,1)S(1)}, u32[]{:S(2)}, u32[]{:S(2)}) collective-permute-start(bf16[96,1536]{1,0:T(8,128)(2,1)S(1)} %get-tuple-element.8), channel_id=1, source_target_pairs={{0,2},{1,3},{2,0},{3,1},{4,6},{5,7},{6,4},{7,5},{8,10},{9,11},{10,... | collective-permute-start | bytes 884744 | tf_op jit(solution)/shard_map/ppermute | solution.py:149
  7.0 14.2 %collective-permute-start.4 = (bf16[96,1536]{1,0:T(8,128)(2,1)S(1)}, bf16[96,1536]{1,0:T(8,128)(2,1)S(1)}, u32[]{:S(2)}, u32[]{:S(2)}) collective-permute-start(bf16[96,1536]{1,0:T(8,128)(2,1)S(1)} %get-tuple-element.8), channel_id=1, source_target_pairs={{0,4},{1,5},{2,6},{3,7},{4,0},{5,1},{6,2},{7,3},{8,12},{9,13},{10,... | collective-permute-start | bytes 884744 | tf_op jit(solution)/shard_map/ppermute | solution.py:149
  12.7 13.3 %collective-permute-start.5 = (bf16[96,1536]{1,0:T(8,128)(2,1)S(1)}, bf16[96,1536]{1,0:T(8,128)(2,1)S(1)}, u32[]{:S(2)}, u32[]{:S(2)}) collective-permute-start(bf16[96,1536]{1,0:T(8,128)(2,1)S(1)} %collective-permute-done.1), channel_id=1, source_target_pairs={{0,4},{1,5},{2,6},{3,7},{4,0},{5,1},{6,2},{7,3},{8,12},{9,13},{10,... | collective-permute-start | bytes 884744 | tf_op jit(solution)/shard_map/ppermute | solution.py:149
  21.1 6.7 %collective-permute-start.6 = (bf16[96,1536]{1,0:T(8,128)(2,1)S(1)}, bf16[96,1536]{1,0:T(8,128)(2,1)S(1)}, u32[]{:S(2)}, u32[]{:S(2)}) collective-permute-start(bf16[96,1536]{1,0:T(8,128)(2,1)S(1)} %collective-permute-done.4), channel_id=1, source_target_pairs={{0,2},{1,3},{2,0},{3,1},{4,6},{5,7},{6,4},{7,5},{8,10},{9,11},{10,... | collective-permute-start | bytes 884744 | tf_op jit(solution)/shard_map/ppermute | solution.py:149
  28.6 76.1 %collective-permute-start.7 = (bf16[4,192,1536]{2,1,0:T(8,128)(2,1)}, bf16[4,192,1536]{2,1,0:T(8,128)(2,1)}, u32[]{:S(2)}, u32[]{:S(2)}) collective-permute-start(bf16[4,192,1536]{2,1,0:T(8,128)(2,1)} %bitcast.17), channel_id=1, source_target_pairs={{0,1},{1,0},{2,3},{3,2},{4,5},{5,4},{6,7},{7,6},{8,9},{9,8},{10,11... | collective-permute-start | bytes 7077896 | tf_op jit(solution)/shard_map/ppermute | solution.py:149
  40.2 8.2 %copy-start.16 = (s32[8]{0:T(128)S(1)}, s32[8]{0:T(128)}, u32[]{:S(2)}) copy-start(s32[8]{0:T(128)} %param.11) | copy-start | bytes 100
  40.2 29.7 %all-to-all-start.1 = ((bf16[8,192,576]{2,1,0:T(8,128)(2,1)}), bf16[8,192,576]{2,1,0:T(8,128)(2,1)}, u32[]{:S(2)}, u32[]{:S(2)}) async-start(bf16[8,192,576]{2,1,0:T(8,128)(2,1)} %copy.20), calls=%async_computation.1 | async-start | bytes 3932160 | tf_op jit(solution)/shard_map/all_to_all | solution.py:206
  44.7 5.2 %copy-start.14 = (f32[48,64]{1,0:T(8,128)S(1)}, f32[48,64]{1,0:T(8,128)}, u32[]{:S(2)}) copy-start(f32[48,64]{1,0:T(8,128)} %param.10) | copy-start | bytes 36868
  44.7 28.8 %copy-start.13 = (bf16[1536,64]{0,1:T(8,128)(2,1)S(1)}, bf16[1536,64]{0,1:T(8,128)(2,1)}, u32[]{:S(2)}) copy-start(bf16[1536,64]{0,1:T(8,128)(2,1)} %param.17) | copy-start | bytes 589828
  44.8 29.7 %copy-start.3 = (bf16[64,1536]{1,0:T(8,128)(2,1)S(1)}, bf16[64,1536]{1,0:T(8,128)(2,1)}, u32[]{:S(2)}) copy-start(bf16[64,1536]{1,0:T(8,128)(2,1)} %embed_ref.5) | copy-start | bytes 589828
  44.8 5.1 %collective-permute-start = (f32[48,64]{1,0:T(8,128)S(1)}, f32[48,64]{1,0:T(8,128)S(1)}, u32[]{:S(2)}, u32[]{:S(2)}) collective-permute-start(f32[48,64]{1,0:T(8,128)S(1)} %slice_bitcast_fusion.1), channel_id=1, source_target_pairs={{0,8},{8,16},{16,24},{1,9},{9,17},{17,25},{2,10},{10,18},{18,26},{... | collective-permute-start | bytes 36872 | tf_op jit(solution)/shard_map/ppermute | solution.py:209
  49.0 29.9 %copy-start.10 = (f32[7,48,64]{2,1,0:T(8,128)}, f32[7,48,64]{2,1,0:T(8,128)S(1)}, u32[]{:S(2)}) copy-start(f32[7,48,64]{2,1,0:T(8,128)S(1)} %slice.16) | copy-start | bytes 258052
  50.6 32.5 %copy-start.18 = (s32[8]{0:T(128)S(1)}, s32[8]{0:T(128)}, u32[]{:S(2)}) copy-start(s32[8]{0:T(128)} %param.12) | copy-start | bytes 100
  70.0 8.9 %all-to-all-start = ((bf16[8,2,1536]{2,1,0:T(2,128)(2,1)}), bf16[8,2,1536]{2,1,0:T(2,128)(2,1)S(1)}, u32[]{:S(2)}, u32[]{:S(2)}) async-start(bf16[8,2,1536]{2,1,0:T(2,128)(2,1)} %reshape.74), calls=%async_computation | async-start | bytes 98304 | tf_op jit(solution)/shard_map/all_to_all | solution.py:213
  78.9 13.5 %all-to-all-start.2 = ((bf16[8,80,384]{2,1,0:T(8,128)(2,1)}), bf16[8,80,384]{2,1,0:T(8,128)(2,1)S(1)}, u32[]{:S(2)}, u32[]{:S(2)}) async-start(bf16[8,80,384]{2,1,0:T(8,128)(2,1)} %prepare.1), calls=%async_computation.2 | async-start | bytes 983040 | tf_op jit(solution)/shard_map/all_to_all | solution.py:223
  120.4 11.8 %copy-start.17 = (s32[8]{0:T(128)S(1)}, s32[8]{0:T(128)}, u32[]{:S(2)}) copy-start(s32[8]{0:T(128)} %param.11) | copy-start | bytes 100
  120.4 18.4 %copy-start.15 = (f32[8]{0:T(128)S(1)}, f32[8]{0:T(128)}, u32[]{:S(2)}) copy-start(f32[8]{0:T(128)} %get-tuple-element.4) | copy-start | bytes 100
  128.8 8.5 %all-to-all-start.3 = ((f32[8,1,3072]{2,1,0:T(1,128)}), f32[8,1,3072]{2,1,0:T(1,128)S(1)}, u32[]{:S(2)}, u32[]{:S(2)}) async-start(f32[8,1,3072]{2,1,0:T(1,128)} %reshape.76), calls=%async_computation.3 | async-start | bytes 196608 | tf_op jit(solution)/shard_map/all_to_all | solution.py:233
  139.8 9.3 %collective-permute-start.10 = (f32[48,64]{1,0:T(8,128)S(1)}, f32[48,64]{1,0:T(8,128)S(1)}, u32[]{:S(2)}, u32[]{:S(2)}) collective-permute-start(f32[48,64]{1,0:T(8,128)S(1)} %slice_bitcast_fusion), channel_id=1, source_target_pairs={{0,24},{1,25},{2,26},{3,27},{4,28},{5,29},{6,30},{7,31}} | collective-permute-start | bytes 36872 | tf_op jit(solution)/shard_map/ppermute | solution.py:175
  145.4 3.8 %collective-permute-start.8 = (f32[48,64]{1,0:T(8,128)S(1)}, f32[48,64]{1,0:T(8,128)S(1)}, u32[]{:S(2)}, u32[]{:S(2)}) collective-permute-start(f32[48,64]{1,0:T(8,128)S(1)} %slice_bitcast_fusion), channel_id=1, source_target_pairs={{0,8},{8,16},{16,24},{1,9},{9,17},{17,25},{2,10},{10,18},{18,26},{... | collective-permute-start | bytes 36872 | tf_op jit(solution)/shard_map/ppermute | solution.py:175
  146.7 4.0 %collective-permute-start.9 = (f32[48,64]{1,0:T(8,128)S(1)}, f32[48,64]{1,0:T(8,128)S(1)}, u32[]{:S(2)}, u32[]{:S(2)}) collective-permute-start(f32[48,64]{1,0:T(8,128)S(1)} %slice_bitcast_fusion), channel_id=1, source_target_pairs={{0,16},{8,24},{1,17},{9,25},{2,18},{10,26},{3,19},{11,27},{4,20},{... | collective-permute-start | bytes 36872 | tf_op jit(solution)/shard_map/ppermute | solution.py:175
  (10 other events, 24.7 us)

commit v2 on v1

v2 whole, which is shorter than its diff:
```python
import functools
import math

import jax
import jax.numpy as jnp
from jax import lax
from jax.experimental import pallas as pl
from jax.experimental.pallas import tpu as pltpu
from jax.sharding import PartitionSpec as P

BF = jnp.bfloat16
F32 = jnp.float32
ROWS = 80
MIB = 1024 * 1024


def dot(a, b, dims=((1,), (0,))):
    return lax.dot_general(a, b, (dims, ((), ())), preferred_element_type=F32)


def alpha_bar(step_ids):
    fraction = (step_ids.astype(F32) / 1000.0 + 0.008) / 1.008
    return jnp.cos(fraction * (math.pi / 2)) ** 2


def coefficients(now_step, next_step):
    alpha_now = alpha_bar(now_step)
    alpha_next = alpha_bar(next_step)
    step_ratio = jnp.sqrt(alpha_next / alpha_now)
    keep_coef = step_ratio - 1.0
    noise_coef = jnp.sqrt(1.0 - alpha_next) - step_ratio * jnp.sqrt(1.0 - alpha_now)
    return (keep_coef, noise_coef)


def modulation(step_ids, mod_weight):
    half_freq = mod_weight.shape[0] // 2
    frequency = jnp.exp(-math.log(10000.0) * jnp.arange(half_freq, dtype=F32) / half_freq)
    angles = step_ids.astype(F32)[:, None] * frequency[None, :]
    time_embed = jnp.concatenate([jnp.cos(angles), jnp.sin(angles)], axis=1).astype(BF)
    return jnp.dot(time_embed, mod_weight, preferred_element_type=F32)


SMEM = pl.BlockSpec(memory_space=pltpu.SMEM)
VMEM = pl.BlockSpec(memory_space=pltpu.VMEM)


def params(mib):
    return pltpu.CompilerParams(vmem_limit_bytes=mib * MIB)


def cut_kernel(n_sub, per, sub, w_ref, out_ref):
    for dest in range(out_ref.shape[0]):
        pieces = []
        for kind in (0, 2, 1):
            for i in range(per):
                head, part = divmod(dest * per + i, n_sub)
                start = kind * n_sub * sub + part * sub
                pieces.append(w_ref[head, :, start : start + sub])
        out_ref[dest] = jnp.concatenate(pieces, axis=1)


def cut(w, count, n_sub, per, sub):
    return pl.pallas_call(
        functools.partial(cut_kernel, n_sub, per, sub),
        out_shape=jax.ShapeDtypeStruct((count, w.shape[1], 3 * per * sub), BF),
        compiler_params=params(8),
        name="cut",
    )(w)


def prepare_kernel(per, sub, embed_ref, mod_ref, w_ref, states_ref, opening_ref, out_ref, basis_scr):
    steps, tokd, chans = states_ref.shape
    width = embed_ref.shape[1]
    embed = embed_ref[...].astype(F32)
    centred = embed - jnp.mean(embed, axis=1, keepdims=True)
    pad = jnp.zeros((ROWS - chans - 8, width), F32)
    first = lax.broadcasted_iota(jnp.int32, (8, width), 0) == 0
    for t in range(steps):
        shift = mod_ref[t : t + 1, :width]
        scale = mod_ref[t : t + 1, width : 2 * width]
        tail = jnp.where(first, jnp.broadcast_to(shift, (8, width)), 0.0)
        rows = jnp.concatenate([centred * (1.0 + scale), tail, pad], axis=0)
        basis_scr[t * ROWS : (t + 1) * ROWS, :] = rows.astype(BF)
    cols = per * sub
    row = lax.broadcasted_iota(jnp.int32, (per * chans, cols), 0) // chans
    lane = lax.broadcasted_iota(jnp.int32, (per * chans, cols), 1) // sub
    same = row == lane
    body = per * (chans + sub)
    values = lax.broadcasted_iota(jnp.int32, (ROWS, body), 1) >= per * chans
    half = steps // 2 * ROWS
    sides = [dot(basis_scr[:half, :], w_ref[...]), dot(basis_scr[half:, :], w_ref[...])]
    for t in range(steps):
        start = t * ROWS % half
        a_t = sides[t * ROWS // half][start : start + ROWS]
        k = jnp.concatenate([a_t[:chans, 2 * cols :].astype(BF)] * per, axis=0)
        k = jnp.where(same, k, jnp.zeros_like(k))
        product = dot(a_t[:, :cols].astype(BF), k, ((1,), (1,)))
        if sub == chans:
            product = jnp.concatenate([product, product], axis=1)
            block = jnp.where(values, a_t[:, : 2 * cols], product)
        else:
            block = jnp.concatenate([product, a_t[:, cols : 2 * cols]], axis=1)
        before = opening_ref if t == 0 else states_ref.at[t - 1]
        groups = [before[i : i + 8, :] for i in range(0, tokd, 8)]
        last = jnp.concatenate(groups, axis=1)
        low = block[ROWS - 16 : ROWS - 8]
        if last.shape[1] > body:
            low = jnp.concatenate([low, jnp.zeros((8, last.shape[1] - body), F32)], axis=1)
        out_ref[t, : ROWS - 16, :body] = block[: ROWS - 16].astype(BF)
        out_ref[t, ROWS - 16 :, :] = jnp.concatenate([low, last], axis=0).astype(BF)


def prepare(embed, mod_all, w_mine, states, opening, per, sub):
    steps, tokd, chans = states.shape
    lanes = max(per * (chans + sub), tokd // 8 * chans)
    return pl.pallas_call(
        functools.partial(prepare_kernel, per, sub),
        out_shape=jax.ShapeDtypeStruct((steps, ROWS, lanes), BF),
        scratch_shapes=[pltpu.VMEM((steps * ROWS, embed.shape[1]), BF)],
        compiler_params=params(16),
        name="prepare",
    )(embed, mod_all, w_mine, states, opening)


def attend_kernel(
    heads, n_sub, per, sub, tokd, part_ref, embed_ref, pay_ref, out_ref, queries_ref, keys_scr
):
    chans = embed_ref.shape[0]
    hdim = n_sub * sub
    length = queries_ref.shape[0]
    for source in range(pay_ref.shape[0]):
        last = pay_ref[source, ROWS - 16 :, :].astype(F32)[8:]
        for i in range(tokd // 8):
            start = source * tokd + i * 8
            keys_scr[start : start + 8, :] = last[:, i * chans : (i + 1) * chans]
    first = pl.multiple_of(part_ref[0] * length, length)

    def augmented(p):
        residual = dot(p.astype(BF), embed_ref[...])
        residual = residual - jnp.mean(residual, axis=1, keepdims=True)
        variance = jnp.mean(residual * residual, axis=1, keepdims=True)
        lane = lax.broadcasted_iota(jnp.int32, p.shape, 1)
        return jnp.concatenate([p * lax.rsqrt(variance + 1e-6), (lane == 0).astype(F32)], axis=1)

    every = augmented(keys_scr[...])
    queries = keys_scr[pl.ds(first, length), :]
    queries_ref[...] = queries.astype(BF)
    mine = every if length == keys_scr.shape[0] else augmented(queries)
    keys = every[:, :chans].astype(BF)
    every_t = every.T[: chans + 16].astype(BF)
    products, values = [], []
    for h in range(heads):
        product = None
        value_parts = []
        for j in range(n_sub):
            source, slot = divmod(h * n_sub + j, per)
            part = pay_ref[source, :, slot * chans : (slot + 1) * chans].astype(F32)
            product = part if product is None else product + part
            start = per * chans + slot * sub
            value_parts.append(pay_ref[source, :, start : start + sub])
        products.append(product.astype(BF))
        values.append(jnp.concatenate(value_parts, axis=1) if n_sub > 1 else value_parts[0])
    factor = hdim**-0.5 * math.log2(math.e)
    sides = (dot(mine[:, :ROWS].astype(BF), jnp.concatenate(products, axis=1)) * factor).astype(BF)

    def scores(h):
        return dot(keys, sides[:, h * chans : (h + 1) * chans], ((1,), (1,)))

    mixed = []
    now = scores(0)
    for h in range(heads):
        following = scores(h + 1) if h + 1 < heads else None
        weights = jnp.exp2(now - jnp.max(now, axis=0, keepdims=True)).astype(BF)
        rows = dot(every_t, weights)
        mixed.append(rows * (1.0 / rows[chans : chans + 1]))
        now = following
    for h in range(heads):
        result = dot(mixed[h].T.astype(BF), values[h])
        out_ref[:, h * hdim : (h + 1) * hdim] = result.astype(BF)


def attend(part, embed, payload, tokd, share, heads, n_sub, per, sub):
    length = payload.shape[0] * tokd
    return pl.pallas_call(
        functools.partial(attend_kernel, heads, n_sub, per, sub, tokd),
        out_shape=[
            jax.ShapeDtypeStruct((length // share, heads * n_sub * sub), BF),
            jax.ShapeDtypeStruct((length // share, embed.shape[0]), BF),
        ],
        in_specs=[SMEM, VMEM, VMEM],
        scratch_shapes=[pltpu.VMEM((length, embed.shape[0]), F32)],
        compiler_params=params(14 if share == 1 else 40),
        name="attend",
    )(part, embed, payload)


def finish_kernel(tokd, chip_ref, coef_ref, embed_ref, queries_ref, att_ref, gate_ref, final_ref, *refs):
    *wo_refs, out_ref = refs
    projection = None
    for i, ref in enumerate(wo_refs):
        if len(wo_refs) == 1:
            columns = att_ref[...]
        else:
            rows = ref.shape[0]
            start = pl.multiple_of(chip_ref[1 + i] * 2 * rows, 2 * rows)
            chip = att_ref[:, pl.ds(start, 2 * rows)]
            columns = jnp.where(chip_ref[0] == i % 2, chip[:, :rows], chip[:, rows:])
        term = dot(columns, ref[...])
        projection = term if projection is None else projection + term
    updated = dot(queries_ref[...], embed_ref[...]) + gate_ref[...] * projection
    centred = updated - jnp.mean(updated, axis=1, keepdims=True)
    variance = jnp.mean(centred * centred, axis=1, keepdims=True)
    normed = (centred * lax.rsqrt(variance + 1e-6)).astype(BF)
    noise = dot(normed, final_ref[...], ((1,), (1,))) * coef_ref[0]
    half = tokd // 2
    for i in range(out_ref.shape[1]):
        block = noise[i * tokd : (i + 1) * tokd]
        block = jnp.concatenate([block[:half], block[half:]], axis=1)
        for j in range(out_ref.shape[0]):
            out_ref[j, i] = block


def finish(chips, coef, embed, queries, att, gate, final, wo_parts, tokd, repeats):
    chans = final.shape[0]
    length = queries.shape[0]
    return pl.pallas_call(
        functools.partial(finish_kernel, tokd),
        out_shape=jax.ShapeDtypeStruct((repeats, length // tokd, tokd // 2, 2 * chans), F32),
        in_specs=[SMEM] * 2 + [VMEM] * (5 + len(wo_parts)),
        compiler_params=params(24),
        name="finish",
    )(chips, coef, embed, queries, att, gate, final, *wo_parts)


def advance_kernel(share, place_ref, keep_ref, noise_ref, states_ref, opening_ref, first_ref, kept_ref, out_ref, square_ref):
    groups, count = noise_ref.shape[:2]
    steps, tokd, chans = states_ref.shape
    packed = jnp.zeros(noise_ref.shape[2:], F32)
    for group in range(groups - 1):
        total = noise_ref[group, 0]
        for i in range(1, count):
            total = total + noise_ref[group, i]
        packed = packed + jnp.where(place_ref[0] > group, total, jnp.zeros_like(total))

    def unpack(x):
        return jnp.concatenate([x[:, :chans], x[:, chans:]], axis=0)

    state = first_ref[...] + kept_ref[...] + unpack(packed)
    for t in range(steps):
        noise = noise_ref[place_ref[0], t * share]
        for i in range(1, share):
            noise = noise + noise_ref[place_ref[0], t * share + i]
        before = opening_ref[...] if t == 0 else states_ref[t - 1]
        state = state + (keep_ref[t] * before + unpack(noise))
        out_ref[t] = state
        error = state - states_ref[t]
        square_ref[t : t + 1, :] = jnp.sum(error * error, axis=0, keepdims=True)


def advance(place, keep, noise, states, opening, first, kept, share):
    steps, _, chans = states.shape
    return pl.pallas_call(
        functools.partial(advance_kernel, share),
        out_shape=[
            jax.ShapeDtypeStruct(states.shape, F32),
            jax.ShapeDtypeStruct((steps, chans), F32),
        ],
        in_specs=[SMEM] * 2 + [VMEM] * 5,
        compiler_params=params(8),
        name="advance",
    )(place, keep, noise, states, opening, first, kept)


def swap(x, mask, count):
    return lax.ppermute(x, "seq", [(i, i ^ mask) for i in range(count)])


def turn_by_plane(x, count, tm_count, swapped=0):
    pairs = []
    for i in range(tm_count):
        for j in range(count):
            pairs.append((i * count + j, i * count + (j ^ (4 if (i + j + swapped) % 2 else 2))))
    return lax.ppermute(x, ("tm", "seq"), pairs)


def earlier_total(total, count):
    place = lax.axis_index("tm")
    carried = jnp.zeros_like(total)
    for by in range(1, count):
        carried += lax.ppermute(total, "tm", [(i, i + by) for i in range(count - by)])
    return carried


def total_over_seq(part, count):
    if count != 8:
        return lax.psum(part, "seq")
    part = part + swap(part, 1, count)
    return part + swap(part, 2, count) + swap(part, 4, count) + swap(part, 6, count)


def per_device(
    states,
    first_state,
    now_step,
    next_step,
    embed_weight,
    mod_weight,
    qkv_weight,
    out_weight,
    final_weight,
):
    steps, tokd, chans = states.shape
    count = lax.axis_size("seq")
    tm_count = lax.axis_size("tm")
    time_index = lax.axis_index("tm")
    seq_index = lax.axis_index("seq")
    rows, heads, width_three = qkv_weight.shape
    hdim = width_three // 3
    width = heads * hdim
    share = count // steps
    n_sub = count // math.gcd(count, heads)
    per = heads * n_sub // count
    sub = hdim // n_sub
    barrier = lax.optimization_barrier
    mine = seq_index // share
    part = seq_index % share

    w_sent = cut(jnp.transpose(qkv_weight, (1, 0, 2)), count, n_sub, per, sub)
    w_mine = lax.all_to_all(w_sent, "seq", 0, 0, tiled=True).reshape(count * rows, 3 * per * sub)

    by_planes = count == 8 and tm_count % 2 == 0
    late_states, own, _ = barrier((states, out_weight, w_sent))
    edge = lax.ppermute(late_states[-1], "tm", [(i, i + 1) for i in range(tm_count - 1)])
    opening = jnp.where(time_index == 0, first_state, edge)
    if by_planes:
        wo_first = turn_by_plane(own, count, tm_count)
    keep_coef, noise_coef = coefficients(now_step, next_step)
    kept = keep_coef[0] * opening + jnp.sum(keep_coef[1:, None, None] * states[:-1], axis=0)
    kept = earlier_total(kept, tm_count)
    mod_all = modulation(now_step, mod_weight)
    gate = lax.dynamic_slice(mod_all, (mine, 2 * width), (1, width))
    coef = lax.dynamic_slice(noise_coef, (mine,), (1,))
    w_mine, mod_all, opening, kept, gate, coef = barrier((w_mine, mod_all, opening, kept, gate, coef))

    payload = prepare(embed_weight, mod_all, w_mine, states, opening, per, sub)
    sent = jnp.repeat(payload, share, axis=0)
    received = lax.all_to_all(sent, "seq", 0, 0, tiled=True)
    if by_planes:
        own, first, _ = barrier((own, wo_first, payload))
        second = lax.ppermute(first, "tm", [(i, i ^ 1) for i in range(tm_count)])
        third = turn_by_plane(first, count, tm_count, 1)
        late_second, late_third, _ = barrier((second, third, received))
        wo_parts = [own, swap(own, 1, count), first, swap(first, 1, count)]
        wo_parts += [late_third, swap(late_third, 1, count)]
        wo_parts += [late_second, swap(late_second, 1, count)]
        chip = seq_index // 2
        one = jnp.where((seq_index + time_index) % 2 == 0, 1, 2)
        two = 3 - one
        chips = jnp.stack([seq_index % 2, chip, chip, chip ^ one, chip ^ two])
        chips = jnp.concatenate([chips, jnp.stack([chip ^ 3, chip ^ 3, chip ^ two, chip ^ one])])
    else:
        wo_parts = [lax.all_gather(out_weight, "seq", axis=0, tiled=True)]
        chips = jnp.zeros((2,), jnp.int32)
    part_place = jnp.full((1,), part, jnp.int32)
    att, queries = attend(part_place, embed_weight, received, tokd, share, heads, n_sub, per, sub)
    repeats = tm_count if share == 1 else 1
    noise = finish(
        chips, coef, embed_weight, queries, att, gate, final_weight.T, wo_parts, tokd, repeats
    )

    if share > 1:
        full = jnp.zeros((share,) + noise.shape[1:], F32)
        full = lax.dynamic_update_slice(full, noise, (part, 0, 0, 0))
        noise = jnp.broadcast_to(full[None], (tm_count,) + full.shape)
    block = noise.shape[-2:]
    noise = noise.reshape((tm_count * count,) + block)
    noise = lax.all_to_all(noise, ("tm", "seq"), 0, 0, tiled=True)
    noise = noise.reshape((tm_count, count) + block)
    time_place = jnp.full((1,), time_index, jnp.int32)
    advanced, squares = advance(time_place, keep_coef, noise, states, opening, first_state, kept, share)
    errors = jnp.sum(total_over_seq(squares, count), axis=1) / (tokd * count * chans)
    return (advanced, errors)


def solution(mesh):
    in_specs = (
        P("tm", "seq", None),
        P("seq", None),
        P("tm"),
        P("tm"),
        P(),
        P(),
        P("seq", None, None),
        P("seq", None),
        P(),
    )
    out_specs = (P("tm", "seq", None), P("tm"))
    return jax.shard_map(
        per_device, mesh=mesh, in_specs=in_specs, out_specs=out_specs, check_vma=False
    )
```

time: 166 us -> 97.4 us (0.59)
  local copies, waits for them, and re-layouts: 36 us -> 5.67 us
  waiting for transfers between devices: 45.1 us -> 23.1 us
  other arithmetic: 16.6 us -> 2.33 us
  blocking collectives: 11.8 us -> 16.8 us
  starting transfers between devices: 35.4 us -> 30.5 us
  Pallas kernels: 19 us -> 17.2 us
    all_to_all x0 -> x1, blocking collectives: none -> 16.8 us  [per_device(): noise = lax.all_to_all(noise, ('tm', 'seq'), 0, 0, tiled=True)]
    unnamed x51 -> x24, local copies, waits for them, and re-layouts: 20.3 us -> 4.92 us
    all_to_all x4 -> x2, waiting for transfers between devices: 31.1 us -> 17.9 us  [the longest x1 10.6 us: per_device(): received = lax.all_to_all(sent, 'seq', 0, 0, tiled=True)]
    psum x1 -> x0, blocking collectives: 11.8 us -> none  [per_device(): errors = lax.psum(partial_value, 'seq') / (tokd * count * chans)]
    ppermute x7 -> x8, waiting for transfers between devices: 11.7 us -> 3.38 us  [swap(): return lax.ppermute(x, 'seq', [(i, i ^ mask) for i in range(count)])]
    another operation x4 -> x1, other arithmetic: 6.4 us -> 0.11 us  [the longest x2 5.27 us: gather_rows(): pairs = jnp.stack([first, second], axis=1)]
    all_to_all x4 -> x2, starting transfers between devices: 15.3 us -> 9.18 us  [the longest x1 5.31 us: per_device(): lax.all_to_all(w_sent, 'seq', 0, 0, tiled=True)]
    ppermute x1 -> x4, starting transfers between devices: 3.61 us -> 9.05 us  [the longest x1 4.86 us: per_device(): lax.ppermute(late_states[-1], 'tm', [(i, i + 1) for i in range(tm_count -...]
  transfers between devices with their start and end apart: 15 -> 17, of which waited for: 9 -> 8; matrix products, arithmetic and copies ran while one was open for 14% -> 3% of each run, Pallas kernels for 8% -> 9%
where the time goes in v2:
time: 97.4 us; the launch traced here: 96.8 us
  starting transfers between devices  30.5 us (31%)
  waiting for transfers between devices  23.1 us (24%)
  Pallas kernels  17.2 us (18%)
  blocking collectives  16.8 us (17%)
  local copies, waits for them, and re-layouts  5.67 us (6%)
  other arithmetic  2.33 us (2%)
    all_to_all x1, blocking collectives, per_device(): noise = lax.all_to_all(noise, ('tm', 'seq'), 0, 0, tiled=True)  16.8 us
    all_to_all x1, waiting for transfers between devices, per_device(): received = lax.all_to_all(sent, 'seq', 0, 0, tiled=True)  10.6 us
    ppermute x3, starting transfers between devices, earlier_total(): lax.ppermute(total, 'tm', [(i, i + by) for i in range(count - by)])  7.72 us
    all_to_all x1, waiting for transfers between devices, per_device(): lax.all_to_all(w_sent, 'seq', 0, 0, tiled=True)  7.23 us
    pallas_call x1, Pallas kernels, finish(): pl.pallas_call(functools.partial(finish_kernel, tokd), out_shape=jax.Shap...  7.12 us
    all_to_all x1, starting transfers between devices, per_device(): lax.all_to_all(w_sent, 'seq', 0, 0, tiled=True)  5.31 us
    unnamed x24, local copies, waits for them, and re-layouts  4.92 us
    ppermute x1, starting transfers between devices, per_device(): lax.ppermute(late_states[-1], 'tm', [(i, i + 1) for i in range(tm_count -...  4.86 us
  transfers between devices with their start and end apart: 17, of which 8 were waited for; matrix products, arithmetic and copies ran while one was open for 3% of the time, Pallas kernels for 9%

profile of v2, /device:TPU:0, one launch (start us, length us, event | category | flops | bytes accessed | tf_op | source)
XLA Modules:
  0.0 96.8 jit_solution(7801064197868965367)
XLA Ops:
  0.7 1.6 %copy-done.3 = bf16[192,12,384]{2,0,1:T(8,128)(2,1)S(1)} copy-done((bf16[192,12,384]{2,0,1:T(8,128)(2,1)S(1)}, bf16[192,12,384]{2,0,1:T(8,128)(2,1)}, u32[]{:S(2)}) %copy-start.3) | copy-done | bytes 1769496
  2.7 1.3 %copy-done.1 = bf16[8,192,576]{2,1,0:T(8,128)(2,1)} copy-done((bf16[8,192,576]{2,1,0:T(8,128)(2,1)}, bf16[8,192,576]{2,1,0:T(8,128)(2,1)S(1)}, u32[]{:S(2)}) %copy-start.1) | copy-done | bytes 1769496
  4.0 5.3 %all-to-all-start = ((bf16[8,192,576]{2,1,0:T(8,128)(2,1)}), bf16[8,192,576]{2,1,0:T(8,128)(2,1)}, u32[]{:S(2)}, u32[]{:S(2)}) async-start(bf16[8,192,576]{2,1,0:T(8,128)(2,1)} %copy-done.1), calls=%async_computation | async-start | bytes 3932160 | tf_op jit(solution)/shard_map/all_to_all | solution.py:329
  9.3 4.9 %collective-permute-start = (f32[48,64]{1,0:T(8,128)S(1)}, f32[48,64]{1,0:T(8,128)}, u32[]{:S(2)}, u32[]{:S(2)}) collective-permute-start(f32[48,64]{1,0:T(8,128)S(1)} %slice_bitcast_fusion), channel_id=1, source_target_pairs={{0,8},{8,16},{16,24},{1,9},{9,17},{17,25},{2,10},{10,18},{18,26},{... | collective-permute-start | bytes 36872 | tf_op jit(solution)/shard_map/ppermute | solution.py:333
  14.2 1.9 %collective-permute-start.4 = (bf16[192,1536]{1,0:T(8,128)(2,1)S(1)}, bf16[192,1536]{1,0:T(8,128)(2,1)}, u32[]{:S(2)}, u32[]{:S(2)}) collective-permute-start(bf16[192,1536]{1,0:T(8,128)(2,1)S(1)} %copy-done.5), channel_id=1, source_target_pairs={{0,2},{1,5},{2,0},{3,7},{4,6},{5,1},{6,4},{7,3},{8,12},{9,11},{10,... | collective-permute-start | bytes 1769480 | tf_op jit(solution)/shard_map/ppermute | solution.py:283
  18.2 4.0 %collective-permute-start.3 = (f32[48,64]{1,0:T(8,128)S(1)}, f32[48,64]{1,0:T(8,128)S(1)}, u32[]{:S(2)}, u32[]{:S(2)}) collective-permute-start(f32[48,64]{1,0:T(8,128)S(1)} %get-tuple-element.36), channel_id=1, source_target_pairs={{0,24},{1,25},{2,26},{3,27},{4,28},{5,29},{6,30},{7,31}} | collective-permute-start | bytes 36872 | tf_op jit(solution)/shard_map/ppermute | solution.py:290
  22.2 1.3 %collective-permute-start.1 = (f32[48,64]{1,0:T(8,128)S(1)}, f32[48,64]{1,0:T(8,128)S(1)}, u32[]{:S(2)}, u32[]{:S(2)}) collective-permute-start(f32[48,64]{1,0:T(8,128)S(1)} %get-tuple-element.36), channel_id=1, source_target_pairs={{0,8},{8,16},{16,24},{1,9},{9,17},{17,25},{2,10},{10,18},{18,26},{... | collective-permute-start | bytes 36872 | tf_op jit(solution)/shard_map/ppermute | solution.py:290
  23.5 2.5 %collective-permute-start.2 = (f32[48,64]{1,0:T(8,128)S(1)}, f32[48,64]{1,0:T(8,128)S(1)}, u32[]{:S(2)}, u32[]{:S(2)}) collective-permute-start(f32[48,64]{1,0:T(8,128)S(1)} %get-tuple-element.36), channel_id=1, source_target_pairs={{0,16},{8,24},{1,17},{9,25},{2,18},{10,26},{3,19},{11,27},{4,20},{... | collective-permute-start | bytes 36872 | tf_op jit(solution)/shard_map/ppermute | solution.py:290
  27.5 7.2 %all-to-all-done = bf16[8,192,576]{2,1,0:T(8,128)(2,1)} async-done(((bf16[8,192,576]{2,1,0:T(8,128)(2,1)}), bf16[8,192,576]{2,1,0:T(8,128)(2,1)}, u32[]{:S(2)}, u32[]{:S(2)}) %all-to-all-start) | async-done | bytes 1769504 | tf_op jit(solution)/shard_map/all_to_all | solution.py:329
  34.7 4.4 %prepare.1 = bf16[8,80,384]{2,1,0:T(8,128)(2,1)} custom-call(bf16[64,1536]{1,0:T(8,128)(2,1)S(1)} %copy-done.2, f32[8,4608]{1,0:T(8,128)S(1)} %fusion.2.mod_ref, bf16[1536,576]{1,0:T(8,128)(2,1)} %bitcast.7.w_ref, f32[8,48,64]{2,1,0:T(8,128)S(1)} %copy-done.4, f32[48,64]{1,0:T(8,128)S(1)} %get-tuple-element.22.opening_ref), custom_call_target="tpu_custom_call" | custom-call | tf_op jit(solution)/shard_map/prepare/pallas_call | solution.py:116
  39.1 0.9 collective-permute-done.4.refs_2_
  40.1 2.0 %collective-permute-start.7 = (bf16[192,1536]{1,0:T(8,128)(2,1)}, bf16[192,1536]{1,0:T(8,128)(2,1)}, u32[]{:S(2)}, u32[]{:S(2)}) collective-permute-start(bf16[192,1536]{1,0:T(8,128)(2,1)} %collective-permute-done.4.refs_2_), channel_id=1, source_target_pairs={{0,8},{8,0},{16,24},{24,16},{1,9},{9,1},{17,25},{25,17},{2,10},{10... | collective-permute-start | bytes 1769480 | tf_op jit(solution)/shard_map/ppermute | solution.py:350
  42.4 3.9 %all-to-all-start.1 = ((bf16[8,80,384]{2,1,0:T(8,128)(2,1)}), bf16[8,80,384]{2,1,0:T(8,128)(2,1)S(1)}, u32[]{:S(2)}, u32[]{:S(2)}) async-start(bf16[8,80,384]{2,1,0:T(8,128)(2,1)} %prepare.1), calls=%async_computation.1 | async-start | bytes 983040 | tf_op jit(solution)/shard_map/all_to_all | solution.py:347
  46.8 10.6 %all-to-all-done.1.pay_ref = bf16[8,80,384]{2,1,0:T(8,128)(2,1)S(1)} async-done(((bf16[8,80,384]{2,1,0:T(8,128)(2,1)}), bf16[8,80,384]{2,1,0:T(8,128)(2,1)S(1)}, u32[]{:S(2)}, u32[]{:S(2)}) %all-to-all-start.1) | async-done | bytes 491552 | tf_op jit(solution)/shard_map/all_to_all | solution.py:347
  58.0 4.0 %attend.1 = (bf16[384,1536]{1,0:T(8,128)(2,1)S(1)}, bf16[384,64]{1,0:T(8,128)(2,1)S(1)}) custom-call(s32[1]{0:T(128)} %constant.86.clone.1.part_ref, bf16[64,1536]{1,0:T(8,128)(2,1)S(1)} %copy-done.2, bf16[8,80,384]{2,1,0:T(8,128)(2,1)S(1)} %all-to-all-done.1.pay_ref), custom_call_target="tpu_custom_call" | custom-call | tf_op jit(solution)/shard_map/attend/pallas_call | solution.py:184
  62.1 1.1 %copy-done.6 = bf16[192,1536]{1,0:T(8,128)(2,1)S(1)} copy-done((bf16[192,1536]{1,0:T(8,128)(2,1)S(1)}, bf16[192,1536]{1,0:T(8,128)(2,1)}, u32[]{:S(2)}) %copy-start.6) | copy-done | bytes 589848
  63.1 0.9 copy-done.7
  64.0 7.1 %finish.1 = f32[4,8,24,128]{3,2,1,0:T(8,128)S(1)} custom-call(s32[9]{0:T(128)S(1)} %concatenate.7.chip_ref, f32[1]{0:T(128)} %dynamic_slice.7.coef_ref, bf16[64,1536]{1,0:T(8,128)(2,1)S(1)} %copy-done.2, bf16[384,64]{1,0:T(8,128)(2,1)S(1)} %get-tuple-element.23.queries_ref, bf16[384,1536]{1,0:T(8,128)(2,1)S(1)} %get-tuple-element.24.att_ref, ...), custom_call_target="tpu_custom_call" | custom-call | tf_op jit(solution)/shard_map/finish/pallas_call | solution.py:226
  71.2 16.8 %all_to_all.15 = f32[32,24,128]{2,1,0:T(8,128)S(1)} all-to-all(f32[32,24,128]{2,1,0:T(8,128)S(1)} %bitcast.17), channel_id=1, replica_groups=mesh['tm'=4,'seq'=8] {'tm','seq'}, dimensions={0} | all-to-all | bytes 786432 | tf_op jit(solution)/shard_map/all_to_all | solution.py:377
  88.0 1.3 %advance.1 = (f32[8,48,64]{2,1,0:T(8,128)}, f32[8,64]{1,0:T(8,128)S(1)}) custom-call(s32[1]{0:T(128)} %bitcast.place_ref, f32[8]{0:T(128)S(1)} %broadcast_add_fusion.keep_ref, f32[4,8,24,128]{3,2,1,0:T(8,128)S(1)} %bitcast.18, f32[8,48,64]{2,1,0:T(8,128)S(1)} %copy-done.4, f32[48,64]{1,0:T(8,128)S(1)} %get-tuple-element.22.opening_ref, ...), custom_call_target="tpu_custom_call" | custom-call | tf_op jit(solution)/shard_map/advance/pallas_call | solution.py:262
  89.3 1.2 %collective-permute-done.11 = f32[8,64]{1,0:T(8,128)S(1)} collective-permute-done((f32[8,64]{1,0:T(8,128)S(1)}, f32[8,64]{1,0:T(8,128)S(1)}, u32[]{:S(2)}, u32[]{:S(2)}) %collective-permute-start.11) | collective-permute-done | bytes 2080 | tf_op jit(solution)/shard_map/ppermute | solution.py:275
  90.5 1.4 %collective-permute-start.14 = (f32[8,64]{1,0:T(8,128)S(1)}, f32[8,64]{1,0:T(8,128)S(1)}, u32[]{:S(2)}, u32[]{:S(2)}) collective-permute-start(f32[8,64]{1,0:T(8,128)S(1)} %add.54), channel_id=1, source_target_pairs={{0,6},{1,7},{2,4},{3,5},{4,2},{5,3},{6,0},{7,1},{8,14},{9,15},{10,... | collective-permute-start | bytes 6152 | tf_op jit(solution)/shard_map/ppermute | solution.py:275
  92.6 1.4 %collective-permute-start.12 = (f32[8,64]{1,0:T(8,128)S(1)}, f32[8,64]{1,0:T(8,128)S(1)}, u32[]{:S(2)}, u32[]{:S(2)}) collective-permute-start(f32[8,64]{1,0:T(8,128)S(1)} %add.54), channel_id=1, source_target_pairs={{0,2},{1,3},{2,0},{3,1},{4,6},{5,7},{6,4},{7,5},{8,10},{9,11},{10,... | collective-permute-start | bytes 6152 | tf_op jit(solution)/shard_map/ppermute | solution.py:275
  94.0 1.0 %collective-permute-done.14 = f32[8,64]{1,0:T(8,128)S(1)} collective-permute-done((f32[8,64]{1,0:T(8,128)S(1)}, f32[8,64]{1,0:T(8,128)S(1)}, u32[]{:S(2)}, u32[]{:S(2)}) %collective-permute-start.14) | collective-permute-done | bytes 2080 | tf_op jit(solution)/shard_map/ppermute | solution.py:275
  (57 shorter events, 8.1 us)
Async XLA Ops:
  0.6 15.7 %copy-start = (bf16[256,4608]{1,0:T(8,128)(2,1)S(1)}, bf16[256,4608]{1,0:T(8,128)(2,1)}, u32[]{:S(2)}) copy-start(bf16[256,4608]{1,0:T(8,128)(2,1)} %param.14) | copy-start | bytes 7077892
  3.9 10.2 %copy-start.5 = (bf16[192,1536]{1,0:T(8,128)(2,1)S(1)}, bf16[192,1536]{1,0:T(8,128)(2,1)}, u32[]{:S(2)}) copy-start(bf16[192,1536]{1,0:T(8,128)(2,1)} %refs_0_) | copy-start | bytes 1769476
  3.9 12.1 %copy-start.11 = (s32[8]{0:T(128)S(1)}, s32[8]{0:T(128)}, u32[]{:S(2)}) copy-start(s32[8]{0:T(128)} %param.11) | copy-start | bytes 100
  3.9 12.1 %copy-start.10 = (s32[8]{0:T(128)S(1)}, s32[8]{0:T(128)}, u32[]{:S(2)}) copy-start(s32[8]{0:T(128)} %param.12) | copy-start | bytes 100
  4.0 30.8 %all-to-all-start = ((bf16[8,192,576]{2,1,0:T(8,128)(2,1)}), bf16[8,192,576]{2,1,0:T(8,128)(2,1)}, u32[]{:S(2)}, u32[]{:S(2)}) async-start(bf16[8,192,576]{2,1,0:T(8,128)(2,1)} %copy-done.1), calls=%async_computation | async-start | bytes 3932160 | tf_op jit(solution)/shard_map/all_to_all | solution.py:329
  9.3 8.2 %copy-start.8 = (f32[48,64]{1,0:T(8,128)S(1)}, f32[48,64]{1,0:T(8,128)}, u32[]{:S(2)}) copy-start(f32[48,64]{1,0:T(8,128)} %first_ref.1) | copy-start | bytes 36868
  9.3 25.4 %copy-start.2 = (bf16[64,1536]{1,0:T(8,128)(2,1)S(1)}, bf16[64,1536]{1,0:T(8,128)(2,1)}, u32[]{:S(2)}) copy-start(bf16[64,1536]{1,0:T(8,128)(2,1)} %embed_ref.5) | copy-start | bytes 589828
  9.3 8.1 %collective-permute-start = (f32[48,64]{1,0:T(8,128)S(1)}, f32[48,64]{1,0:T(8,128)}, u32[]{:S(2)}, u32[]{:S(2)}) collective-permute-start(f32[48,64]{1,0:T(8,128)S(1)} %slice_bitcast_fusion), channel_id=1, source_target_pairs={{0,8},{8,16},{16,24},{1,9},{9,17},{17,25},{2,10},{10,18},{18,26},{... | collective-permute-start | bytes 36872 | tf_op jit(solution)/shard_map/ppermute | solution.py:333
  14.2 25.9 %collective-permute-start.4 = (bf16[192,1536]{1,0:T(8,128)(2,1)S(1)}, bf16[192,1536]{1,0:T(8,128)(2,1)}, u32[]{:S(2)}, u32[]{:S(2)}) collective-permute-start(bf16[192,1536]{1,0:T(8,128)(2,1)S(1)} %copy-done.5), channel_id=1, source_target_pairs={{0,2},{1,5},{2,0},{3,7},{4,6},{5,1},{6,4},{7,3},{8,12},{9,11},{10,... | collective-permute-start | bytes 1769480 | tf_op jit(solution)/shard_map/ppermute | solution.py:283
  18.2 8.3 %collective-permute-start.3 = (f32[48,64]{1,0:T(8,128)S(1)}, f32[48,64]{1,0:T(8,128)S(1)}, u32[]{:S(2)}, u32[]{:S(2)}) collective-permute-start(f32[48,64]{1,0:T(8,128)S(1)} %get-tuple-element.36), channel_id=1, source_target_pairs={{0,24},{1,25},{2,26},{3,27},{4,28},{5,29},{6,30},{7,31}} | collective-permute-start | bytes 36872 | tf_op jit(solution)/shard_map/ppermute | solution.py:290
  22.2 4.4 %collective-permute-start.1 = (f32[48,64]{1,0:T(8,128)S(1)}, f32[48,64]{1,0:T(8,128)S(1)}, u32[]{:S(2)}, u32[]{:S(2)}) collective-permute-start(f32[48,64]{1,0:T(8,128)S(1)} %get-tuple-element.36), channel_id=1, source_target_pairs={{0,8},{8,16},{16,24},{1,9},{9,17},{17,25},{2,10},{10,18},{18,26},{... | collective-permute-start | bytes 36872 | tf_op jit(solution)/shard_map/ppermute | solution.py:290
  23.5 4.0 %collective-permute-start.2 = (f32[48,64]{1,0:T(8,128)S(1)}, f32[48,64]{1,0:T(8,128)S(1)}, u32[]{:S(2)}, u32[]{:S(2)}) collective-permute-start(f32[48,64]{1,0:T(8,128)S(1)} %get-tuple-element.36), channel_id=1, source_target_pairs={{0,16},{8,24},{1,17},{9,25},{2,18},{10,26},{3,19},{11,27},{4,20},{... | collective-permute-start | bytes 36872 | tf_op jit(solution)/shard_map/ppermute | solution.py:290
  40.1 17.4 %collective-permute-start.7 = (bf16[192,1536]{1,0:T(8,128)(2,1)}, bf16[192,1536]{1,0:T(8,128)(2,1)}, u32[]{:S(2)}, u32[]{:S(2)}) collective-permute-start(bf16[192,1536]{1,0:T(8,128)(2,1)} %collective-permute-done.4.refs_2_), channel_id=1, source_target_pairs={{0,8},{8,0},{16,24},{24,16},{1,9},{9,1},{17,25},{25,17},{2,10},{10... | collective-permute-start | bytes 1769480 | tf_op jit(solution)/shard_map/ppermute | solution.py:350
  42.1 15.4 %collective-permute-start.8 = (bf16[192,1536]{1,0:T(8,128)(2,1)}, bf16[192,1536]{1,0:T(8,128)(2,1)}, u32[]{:S(2)}, u32[]{:S(2)}) collective-permute-start(bf16[192,1536]{1,0:T(8,128)(2,1)} %collective-permute-done.4.refs_2_), channel_id=1, source_target_pairs={{0,4},{1,3},{2,6},{3,1},{4,0},{5,7},{6,2},{7,5},{8,10},{9,13},{10,... | collective-permute-start | bytes 1769480 | tf_op jit(solution)/shard_map/ppermute | solution.py:283
  42.4 15.0 %all-to-all-start.1 = ((bf16[8,80,384]{2,1,0:T(8,128)(2,1)}), bf16[8,80,384]{2,1,0:T(8,128)(2,1)S(1)}, u32[]{:S(2)}, u32[]{:S(2)}) async-start(bf16[8,80,384]{2,1,0:T(8,128)(2,1)} %prepare.1), calls=%async_computation.1 | async-start | bytes 983040 | tf_op jit(solution)/shard_map/all_to_all | solution.py:347
  46.3 15.7 %collective-permute-start.6 = (bf16[192,1536]{1,0:T(8,128)(2,1)}, bf16[192,1536]{1,0:T(8,128)(2,1)}, u32[]{:S(2)}, u32[]{:S(2)}) collective-permute-start(bf16[192,1536]{1,0:T(8,128)(2,1)} %collective-permute-done.4.refs_2_), channel_id=1, source_target_pairs={{0,1},{1,0},{2,3},{3,2},{4,5},{5,4},{6,7},{7,6},{8,9},{9,8},{10,11... | collective-permute-start | bytes 1769480 | tf_op jit(solution)/shard_map/ppermute | solution.py:275
  46.8 15.2 %collective-permute-start.5 = (bf16[192,1536]{1,0:T(8,128)(2,1)}, bf16[192,1536]{1,0:T(8,128)(2,1)}, u32[]{:S(2)}, u32[]{:S(2)}) collective-permute-start(bf16[192,1536]{1,0:T(8,128)(2,1)} %refs_0_), channel_id=1, source_target_pairs={{0,1},{1,0},{2,3},{3,2},{4,5},{5,4},{6,7},{7,6},{8,9},{9,8},{10,11... | collective-permute-start | bytes 1769480 | tf_op jit(solution)/shard_map/ppermute | solution.py:275
  57.4 4.6 %collective-permute-start.9 = (bf16[192,1536]{1,0:T(8,128)(2,1)}, bf16[192,1536]{1,0:T(8,128)(2,1)}, u32[]{:S(2)}, u32[]{:S(2)}) collective-permute-start(bf16[192,1536]{1,0:T(8,128)(2,1)} %collective-permute-done.8.refs_4_), channel_id=1, source_target_pairs={{0,1},{1,0},{2,3},{3,2},{4,5},{5,4},{6,7},{7,6},{8,9},{9,8},{10,11... | collective-permute-start | bytes 1769480 | tf_op jit(solution)/shard_map/ppermute | solution.py:275
  57.4 4.6 %collective-permute-start.10 = (bf16[192,1536]{1,0:T(8,128)(2,1)}, bf16[192,1536]{1,0:T(8,128)(2,1)}, u32[]{:S(2)}, u32[]{:S(2)}) collective-permute-start(bf16[192,1536]{1,0:T(8,128)(2,1)} %collective-permute-done.7.refs_6_), channel_id=1, source_target_pairs={{0,1},{1,0},{2,3},{3,2},{4,5},{5,4},{6,7},{7,6},{8,9},{9,8},{10,11... | collective-permute-start | bytes 1769480 | tf_op jit(solution)/shard_map/ppermute | solution.py:275
  64.0 24.0 %copy-start.9 = (f32[48,64]{1,0:T(8,128)S(1)}, f32[48,64]{1,0:T(8,128)}, u32[]{:S(2)}) copy-start(f32[48,64]{1,0:T(8,128)} %first_ref.1) | copy-start | bytes 36868
  89.3 1.2 %collective-permute-start.11 = (f32[8,64]{1,0:T(8,128)S(1)}, f32[8,64]{1,0:T(8,128)S(1)}, u32[]{:S(2)}, u32[]{:S(2)}) collective-permute-start(f32[8,64]{1,0:T(8,128)S(1)} %get-tuple-element.33), channel_id=1, source_target_pairs={{0,1},{1,0},{2,3},{3,2},{4,5},{5,4},{6,7},{7,6},{8,9},{9,8},{10,11... | collective-permute-start | bytes 6152 | tf_op jit(solution)/shard_map/ppermute | solution.py:275
  90.5 4.5 %collective-permute-start.14 = (f32[8,64]{1,0:T(8,128)S(1)}, f32[8,64]{1,0:T(8,128)S(1)}, u32[]{:S(2)}, u32[]{:S(2)}) collective-permute-start(f32[8,64]{1,0:T(8,128)S(1)} %add.54), channel_id=1, source_target_pairs={{0,6},{1,7},{2,4},{3,5},{4,2},{5,3},{6,0},{7,1},{8,14},{9,15},{10,... | collective-permute-start | bytes 6152 | tf_op jit(solution)/shard_map/ppermute | solution.py:275
  91.9 3.6 %collective-permute-start.13 = (f32[8,64]{1,0:T(8,128)S(1)}, f32[8,64]{1,0:T(8,128)S(1)}, u32[]{:S(2)}, u32[]{:S(2)}) collective-permute-start(f32[8,64]{1,0:T(8,128)S(1)} %add.54), channel_id=1, source_target_pairs={{0,4},{1,5},{2,6},{3,7},{4,0},{5,1},{6,2},{7,3},{8,12},{9,13},{10,... | collective-permute-start | bytes 6152 | tf_op jit(solution)/shard_map/ppermute | solution.py:275
  92.6 3.6 %collective-permute-start.12 = (f32[8,64]{1,0:T(8,128)S(1)}, f32[8,64]{1,0:T(8,128)S(1)}, u32[]{:S(2)}, u32[]{:S(2)}) collective-permute-start(f32[8,64]{1,0:T(8,128)S(1)} %add.54), channel_id=1, source_target_pairs={{0,2},{1,3},{2,0},{3,1},{4,6},{5,7},{6,4},{7,5},{8,10},{9,11},{10,... | collective-permute-start | bytes 6152 | tf_op jit(solution)/shard_map/ppermute | solution.py:275
  (5 other events, 10.2 us)

commit v3 on v2

--- a/solution.py
+++ b/solution.py
@@ -46,6 +46,15 @@
 
 def params(mib):
     return pltpu.CompilerParams(vmem_limit_bytes=mib * MIB)
+
+
+def packing(rows, lanes):
+    main = lanes // 128 * 128
+    rest = lanes - main
+    if rest == 0:
+        return (main, 0, 1, 0)
+    each = main // rest
+    return (main, rest, each, -(-(rows // 16) // each))
 
 
 def cut_kernel(n_sub, per, sub, w_ref, out_ref):
@@ -56,19 +65,30 @@
                 head, part = divmod(dest * per + i, n_sub)
                 start = kind * n_sub * sub + part * sub
                 pieces.append(w_ref[head, :, start : start + sub])
-        out_ref[dest] = jnp.concatenate(pieces, axis=1)
+        block = jnp.concatenate(pieces, axis=1)
+        rows, lanes = block.shape
+        main, rest, each, strips = packing(rows, lanes)
+        out_ref[dest, :rows, :] = block[:, :main]
+        groups = [block[i : i + 16, main:] for i in range(0, rows, 16) if rest]
+        groups += [jnp.zeros((16, rest), BF)] * (strips * each - len(groups))
+        for i in range(strips):
+            strip = jnp.concatenate(groups[i * each : (i + 1) * each], axis=1)
+            out_ref[dest, rows + 16 * i : rows + 16 * (i + 1), :] = strip
 
 
 def cut(w, count, n_sub, per, sub):
+    main, _, _, strips = packing(w.shape[1], 3 * per * sub)
     return pl.pallas_call(
         functools.partial(cut_kernel, n_sub, per, sub),
-        out_shape=jax.ShapeDtypeStruct((count, w.shape[1], 3 * per * sub), BF),
-        compiler_params=params(8),
+        out_shape=jax.ShapeDtypeStruct((count, w.shape[1] + 16 * strips, main), BF),
+        compiler_params=params(6),
         name="cut",
     )(w)
 
 
-def prepare_kernel(per, sub, embed_ref, mod_ref, w_ref, states_ref, opening_ref, out_ref, basis_scr):
+def prepare_kernel(
+    per, sub, embed_ref, mod_ref, w_ref, states_ref, opening_ref, out_ref, basis_scr, rest_scr
+):
     steps, tokd, chans = states_ref.shape
     width = embed_ref.shape[1]
     embed = embed_ref[...].astype(F32)
@@ -87,8 +107,23 @@
     same = row == lane
     body = per * (chans + sub)
     values = lax.broadcasted_iota(jnp.int32, (ROWS, body), 1) >= per * chans
+    rows = width // w_ref.shape[0]
+    main, rest, each, _ = packing(rows, 3 * cols)
+    for source in range(w_ref.shape[0]):
+        for i in range(rows // 16 if rest else 0):
+            strip, j = divmod(i, each)
+            group = w_ref[source, rows + 16 * strip : rows + 16 * (strip + 1), :]
+            start = source * rows + 16 * i
+            rest_scr[start : start + 16, :rest] = group[:, j * rest : (j + 1) * rest]
+    whole = w_ref[:, :rows, :].reshape(width, main)
     half = steps // 2 * ROWS
-    sides = [dot(basis_scr[:half, :], w_ref[...]), dot(basis_scr[half:, :], w_ref[...])]
+    sides = []
+    for start in (0, half):
+        part = basis_scr[start : start + half, :]
+        side = dot(part, whole)
+        if rest:
+            side = jnp.concatenate([side, dot(part, rest_scr[:, :rest])], axis=1)
+        sides.append(side)
     for t in range(steps):
         start = t * ROWS % half
         a_t = sides[t * ROWS // half][start : start + ROWS]
@@ -116,8 +151,11 @@
     return pl.pallas_call(
         functools.partial(prepare_kernel, per, sub),
         out_shape=jax.ShapeDtypeStruct((steps, ROWS, lanes), BF),
-        scratch_shapes=[pltpu.VMEM((steps * ROWS, embed.shape[1]), BF)],
-        compiler_params=params(16),
+        scratch_shapes=[
+            pltpu.VMEM((steps * ROWS, embed.shape[1]), BF),
+            pltpu.VMEM((embed.shape[1], 128), BF),
+        ],
+        compiler_params=params(10),
         name="prepare",
     )(embed, mod_all, w_mine, states, opening)
 
@@ -189,26 +227,36 @@
         ],
         in_specs=[SMEM, VMEM, VMEM],
         scratch_shapes=[pltpu.VMEM((length, embed.shape[0]), F32)],
-        compiler_params=params(14 if share == 1 else 40),
+        compiler_params=params(9 if share == 1 else 40),
         name="attend",
     )(part, embed, payload)
 
 
-def finish_kernel(tokd, chip_ref, coef_ref, embed_ref, queries_ref, att_ref, gate_ref, final_ref, *refs):
-    *wo_refs, out_ref = refs
-    projection = None
-    for i, ref in enumerate(wo_refs):
-        if len(wo_refs) == 1:
-            columns = att_ref[...]
-        else:
+def finish_kernel(
+    tokd, owner_ref, coef_ref, embed_ref, queries_ref, att_ref, gate_ref, final_ref, *refs
+):
+    *wo_refs, out_ref, wo_scr, sum_scr, sem = refs
+    width = wo_scr.shape[1]
+    chunk = width // 2
+    copies = []
+    for c in range(2):
+        lanes = pl.ds(c * chunk, chunk)
+        for i, ref in enumerate(wo_refs):
             rows = ref.shape[0]
-            start = pl.multiple_of(chip_ref[1 + i] * 2 * rows, 2 * rows)
-            chip = att_ref[:, pl.ds(start, 2 * rows)]
-            columns = jnp.where(chip_ref[0] == i % 2, chip[:, :rows], chip[:, rows:])
-        term = dot(columns, ref[...])
-        projection = term if projection is None else projection + term
-    updated = dot(queries_ref[...], embed_ref[...]) + gate_ref[...] * projection
-    centred = updated - jnp.mean(updated, axis=1, keepdims=True)
+            start = pl.multiple_of(owner_ref[i] * rows, rows)
+            target = wo_scr.at[pl.ds(start, rows), lanes]
+            copies.append(pltpu.make_async_copy(ref.at[:, lanes], target, sem.at[c, i]))
+            copies[-1].start()
+    total = 0.0
+    for c in range(2):
+        lanes = slice(c * chunk, (c + 1) * chunk)
+        residual = dot(queries_ref[...], embed_ref[:, lanes])
+        for copy in copies[c * len(wo_refs) : (c + 1) * len(wo_refs)]:
+            copy.wait()
+        updated = residual + gate_ref[:, lanes] * dot(att_ref[...], wo_scr[:, lanes])
+        sum_scr[:, lanes] = updated
+        total = total + jnp.sum(updated, axis=1, keepdims=True)
+    centred = sum_scr[...] - total * (1.0 / width)
     variance = jnp.mean(centred * centred, axis=1, keepdims=True)
     normed = (centred * lax.rsqrt(variance + 1e-6)).astype(BF)
     noise = dot(normed, final_ref[...], ((1,), (1,))) * coef_ref[0]
@@ -220,16 +268,21 @@
             out_ref[j, i] = block
 
 
-def finish(chips, coef, embed, queries, att, gate, final, wo_parts, tokd, repeats):
-    chans = final.shape[0]
+def finish(owners, coef, embed, queries, att, gate, final, parts, tokd, repeats):
+    chans, width = final.shape
     length = queries.shape[0]
     return pl.pallas_call(
         functools.partial(finish_kernel, tokd),
         out_shape=jax.ShapeDtypeStruct((repeats, length // tokd, tokd // 2, 2 * chans), F32),
-        in_specs=[SMEM] * 2 + [VMEM] * (5 + len(wo_parts)),
-        compiler_params=params(24),
+        in_specs=[SMEM] * 2 + [VMEM] * 5 + [pl.BlockSpec(memory_space=pl.ANY)] * len(parts),
+        scratch_shapes=[
+            pltpu.VMEM((att.shape[1], width), BF),
+            pltpu.VMEM((length, width), F32),
+            pltpu.SemaphoreType.DMA((2, len(parts))),
+        ],
+        compiler_params=params(15),
         name="finish",
-    )(chips, coef, embed, queries, att, gate, final, *wo_parts)
+    )(owners, coef, embed, queries, att, gate, final, *parts)
 
 
 def advance_kernel(share, place_ref, keep_ref, noise_ref, states_ref, opening_ref, first_ref, kept_ref, out_ref, square_ref):
@@ -266,7 +319,7 @@
             jax.ShapeDtypeStruct((steps, chans), F32),
         ],
         in_specs=[SMEM] * 2 + [VMEM] * 5,
-        compiler_params=params(8),
+        compiler_params=params(4),
         name="advance",
     )(place, keep, noise, states, opening, first, kept)
 
@@ -326,46 +379,50 @@
     part = seq_index % share
 
     w_sent = cut(jnp.transpose(qkv_weight, (1, 0, 2)), count, n_sub, per, sub)
-    w_mine = lax.all_to_all(w_sent, "seq", 0, 0, tiled=True).reshape(count * rows, 3 * per * sub)
+    w_mine = lax.all_to_all(w_sent, "seq", 0, 0, tiled=True)
 
     by_planes = count == 8 and tm_count % 2 == 0
-    late_states, own, _ = barrier((states, out_weight, w_sent))
+    if by_planes:
+        first = turn_by_plane(out_weight, count, tm_count)
+    late_states, _ = barrier((states, w_sent))
     edge = lax.ppermute(late_states[-1], "tm", [(i, i + 1) for i in range(tm_count - 1)])
     opening = jnp.where(time_index == 0, first_state, edge)
-    if by_planes:
-        wo_first = turn_by_plane(own, count, tm_count)
     keep_coef, noise_coef = coefficients(now_step, next_step)
     kept = keep_coef[0] * opening + jnp.sum(keep_coef[1:, None, None] * states[:-1], axis=0)
     kept = earlier_total(kept, tm_count)
     mod_all = modulation(now_step, mod_weight)
     gate = lax.dynamic_slice(mod_all, (mine, 2 * width), (1, width))
     coef = lax.dynamic_slice(noise_coef, (mine,), (1,))
+    if by_planes:
+        late_first, _ = barrier((first, (kept, mod_all, gate, coef)))
+        second = lax.ppermute(late_first, "tm", [(i, i ^ 1) for i in range(tm_count)])
     w_mine, mod_all, opening, kept, gate, coef = barrier((w_mine, mod_all, opening, kept, gate, coef))
+    if by_planes:
+        late_first, _ = barrier((first, w_mine))
+        third = turn_by_plane(late_first, count, tm_count, 1)
 
     payload = prepare(embed_weight, mod_all, w_mine, states, opening, per, sub)
     sent = jnp.repeat(payload, share, axis=0)
     received = lax.all_to_all(sent, "seq", 0, 0, tiled=True)
     if by_planes:
-        own, first, _ = barrier((own, wo_first, payload))
-        second = lax.ppermute(first, "tm", [(i, i ^ 1) for i in range(tm_count)])
-        third = turn_by_plane(first, count, tm_count, 1)
-        late_second, late_third, _ = barrier((second, third, received))
-        wo_parts = [own, swap(own, 1, count), first, swap(first, 1, count)]
-        wo_parts += [late_third, swap(late_third, 1, count)]
-        wo_parts += [late_second, swap(late_second, 1, count)]
-        chip = seq_index // 2
-        one = jnp.where((seq_index + time_index) % 2 == 0, 1, 2)
-        two = 3 - one
-        chips = jnp.stack([seq_index % 2, chip, chip, chip ^ one, chip ^ two])
-        chips = jnp.concatenate([chips, jnp.stack([chip ^ 3, chip ^ 3, chip ^ two, chip ^ one])])
+        own, first, second, _ = barrier((out_weight, first, second, payload))
+        third, _ = barrier((third, received))
+        parts = []
+        for block in (own, first, second, third):
+            parts += [block, swap(block, 1, count)]
+        one = jnp.where((seq_index + time_index) % 2 == 0, 2, 4)
+        two = 6 - one
+        zero = jnp.zeros_like(one)
+        owners = [zero, zero + 1, one, two + 1, two, one + 1, zero + 6, zero + 7]
+        owners = seq_index ^ jnp.stack(owners)
     else:
-        wo_parts = [lax.all_gather(out_weight, "seq", axis=0, tiled=True)]
-        chips = jnp.zeros((2,), jnp.int32)
+        parts = [lax.all_gather(out_weight, "seq", axis=0, tiled=True)]
+        owners = jnp.zeros((1,), jnp.int32)
     part_place = jnp.full((1,), part, jnp.int32)
     att, queries = attend(part_place, embed_weight, received, tokd, share, heads, n_sub, per, sub)
     repeats = tm_count if share == 1 else 1
     noise = finish(
-        chips, coef, embed_weight, queries, att, gate, final_weight.T, wo_parts, tokd, repeats
+        owners, coef, embed_weight, queries, att, gate, final_weight.T, parts, tokd, repeats
     )
 
     if share > 1:

time: 97.4 us -> 91.3 us (0.937)
  waiting for transfers between devices: 23.1 us -> 18 us
  starting transfers between devices: 30.5 us -> 31.9 us
  other arithmetic: 2.33 us -> 0.98 us
  local copies, waits for them, and re-layouts: 5.67 us -> 4.53 us
    all_to_all x1, waiting for transfers between devices: 7.23 us -> 4.69 us  [per_device(): w_mine = lax.all_to_all(w_sent, 'seq', 0, 0, tiled=True)]
    ppermute x3, starting transfers between devices: 7.72 us -> 10 us  [earlier_total(): lax.ppermute(total, 'tm', [(i, i + by) for i in range(count - by)])]
    all_to_all x1, waiting for transfers between devices: 10.6 us -> 8.4 us  [per_device(): received = lax.all_to_all(sent, 'seq', 0, 0, tiled=True)]
    ppermute x2, starting transfers between devices: 2.21 us -> 3.54 us  [turn_by_plane(): return lax.ppermute(x, ('tm', 'seq'), pairs)]
    ppermute x1, starting transfers between devices: 4.86 us -> 3.66 us  [per_device(): lax.ppermute(late_states[-1], 'tm', [(i, i + 1) for i in range(tm_count -...]
    unnamed x24 -> x20, local copies, waits for them, and re-layouts: 4.92 us -> 3.78 us
  transfers between devices with their start and end apart: 17 -> 17, of which waited for: 8 -> 8; matrix products, arithmetic and copies ran while one was open for 3% -> 2% of each run, Pallas kernels for 9% -> 10%
where the time goes in v3:
time: 91.3 us; the launch traced here: 90.9 us
  starting transfers between devices  31.9 us (35%)
  waiting for transfers between devices  18 us (20%)
  blocking collectives  17.1 us (19%)
  Pallas kernels  17 us (19%)
  local copies, waits for them, and re-layouts  4.53 us (5%)
  other arithmetic  0.98 us (1%)
    all_to_all x1, blocking collectives, per_device(): noise = lax.all_to_all(noise, ('tm', 'seq'), 0, 0, tiled=True)  17.1 us
    ppermute x3, starting transfers between devices, earlier_total(): lax.ppermute(total, 'tm', [(i, i + by) for i in range(count - by)])  10 us
    all_to_all x1, waiting for transfers between devices, per_device(): received = lax.all_to_all(sent, 'seq', 0, 0, tiled=True)  8.4 us
    pallas_call x1, Pallas kernels, finish(): pl.pallas_call(functools.partial(finish_kernel, tokd), out_shape=jax.Shap...  6.76 us
    all_to_all x1, waiting for transfers between devices, per_device(): w_mine = lax.all_to_all(w_sent, 'seq', 0, 0, tiled=True)  4.69 us
    all_to_all x1, starting transfers between devices, per_device(): w_mine = lax.all_to_all(w_sent, 'seq', 0, 0, tiled=True)  4.47 us
    ppermute x8, starting transfers between devices, swap(): return lax.ppermute(x, 'seq', [(i, i ^ mask) for i in range(count)])  4.4 us
    pallas_call x1, Pallas kernels, prepare(): pl.pallas_call(functools.partial(prepare_kernel, per, sub), out_shape=jax...  4.38 us
  transfers between devices with their start and end apart: 17, of which 8 were waited for; matrix products, arithmetic and copies ran while one was open for 2% of the time, Pallas kernels for 10%

profile of v3, /device:TPU:0, one launch (start us, length us, event | category | flops | bytes accessed | tf_op | source)
XLA Modules:
  0.0 90.9 jit_solution(6189778541349394732)
XLA Ops:
  0.6 3.0 %collective-permute-start.4 = (bf16[192,1536]{1,0:T(8,128)(2,1)}, bf16[192,1536]{1,0:T(8,128)(2,1)}, u32[]{:S(2)}, u32[]{:S(2)}) collective-permute-start(bf16[192,1536]{1,0:T(8,128)(2,1)} %refs_0_), channel_id=1, source_target_pairs={{0,2},{1,5},{2,0},{3,7},{4,6},{5,1},{6,4},{7,3},{8,12},{9,11},{10,... | collective-permute-start | bytes 1769480 | tf_op jit(solution)/shard_map/ppermute | solution.py:336
  3.7 1.5 %copy-done.3 = bf16[192,12,384]{2,0,1:T(8,128)(2,1)S(1)} copy-done((bf16[192,12,384]{2,0,1:T(8,128)(2,1)S(1)}, bf16[192,12,384]{2,0,1:T(8,128)(2,1)}, u32[]{:S(2)}) %copy-start.3) | copy-done | bytes 1769496
  5.7 1.2 %copy-done.1 = bf16[8,224,512]{2,1,0:T(8,128)(2,1)} copy-done((bf16[8,224,512]{2,1,0:T(8,128)(2,1)}, bf16[8,224,512]{2,1,0:T(8,128)(2,1)S(1)}, u32[]{:S(2)}) %copy-start.1) | copy-done | bytes 1835032
  7.0 4.5 %all-to-all-start = ((bf16[8,224,512]{2,1,0:T(8,128)(2,1)}), bf16[8,224,512]{2,1,0:T(8,128)(2,1)}, u32[]{:S(2)}, u32[]{:S(2)}) async-start(bf16[8,224,512]{2,1,0:T(8,128)(2,1)} %copy-done.1), calls=%async_computation | async-start | bytes 3670016 | tf_op jit(solution)/shard_map/all_to_all | solution.py:382
  11.5 3.7 %collective-permute-start = (f32[48,64]{1,0:T(8,128)S(1)}, f32[48,64]{1,0:T(8,128)S(1)}, u32[]{:S(2)}, u32[]{:S(2)}) collective-permute-start(f32[48,64]{1,0:T(8,128)S(1)} %slice_bitcast_fusion), channel_id=1, source_target_pairs={{0,8},{8,16},{16,24},{1,9},{9,17},{17,25},{2,10},{10,18},{18,26},{... | collective-permute-start | bytes 36872 | tf_op jit(solution)/shard_map/ppermute | solution.py:388
  16.7 6.2 %collective-permute-start.3 = (f32[48,64]{1,0:T(8,128)S(1)}, f32[48,64]{1,0:T(8,128)S(1)}, u32[]{:S(2)}, u32[]{:S(2)}) collective-permute-start(f32[48,64]{1,0:T(8,128)S(1)} %get-tuple-element.38), channel_id=1, source_target_pairs={{0,24},{1,25},{2,26},{3,27},{4,28},{5,29},{6,30},{7,31}} | collective-permute-start | bytes 36872 | tf_op jit(solution)/shard_map/ppermute | solution.py:343
  22.9 1.3 %collective-permute-start.2 = (f32[48,64]{1,0:T(8,128)S(1)}, f32[48,64]{1,0:T(8,128)S(1)}, u32[]{:S(2)}, u32[]{:S(2)}) collective-permute-start(f32[48,64]{1,0:T(8,128)S(1)} %get-tuple-element.38), channel_id=1, source_target_pairs={{0,16},{8,24},{1,17},{9,25},{2,18},{10,26},{3,19},{11,27},{4,20},{... | collective-permute-start | bytes 36872 | tf_op jit(solution)/shard_map/ppermute | solution.py:343
  24.2 2.5 %collective-permute-start.1 = (f32[48,64]{1,0:T(8,128)S(1)}, f32[48,64]{1,0:T(8,128)S(1)}, u32[]{:S(2)}, u32[]{:S(2)}) collective-permute-start(f32[48,64]{1,0:T(8,128)S(1)} %get-tuple-element.38), channel_id=1, source_target_pairs={{0,8},{8,16},{16,24},{1,9},{9,17},{17,25},{2,10},{10,18},{18,26},{... | collective-permute-start | bytes 36872 | tf_op jit(solution)/shard_map/ppermute | solution.py:343
  27.3 0.9 collective-permute-done.1
  28.2 2.4 %collective-permute-start.5 = (bf16[192,1536]{1,0:T(8,128)(2,1)}, bf16[192,1536]{1,0:T(8,128)(2,1)}, u32[]{:S(2)}, u32[]{:S(2)}) collective-permute-start(bf16[192,1536]{1,0:T(8,128)(2,1)} %collective-permute-done.4.refs_2_), channel_id=1, source_target_pairs={{0,8},{8,0},{16,24},{24,16},{1,9},{9,1},{17,25},{25,17},{2,10},{10... | collective-permute-start | bytes 1769480 | tf_op jit(solution)/shard_map/ppermute | solution.py:398
  30.6 4.7 %all-to-all-done.w_ref = bf16[8,224,512]{2,1,0:T(8,128)(2,1)} async-done(((bf16[8,224,512]{2,1,0:T(8,128)(2,1)}), bf16[8,224,512]{2,1,0:T(8,128)(2,1)}, u32[]{:S(2)}, u32[]{:S(2)}) %all-to-all-start) | async-done | bytes 1835040 | tf_op jit(solution)/shard_map/all_to_all | solution.py:382
  35.8 4.4 %prepare.1 = bf16[8,80,384]{2,1,0:T(8,128)(2,1)} custom-call(bf16[64,1536]{1,0:T(8,128)(2,1)S(1)} %copy-done.2, f32[8,4608]{1,0:T(8,128)S(1)} %fusion.2.mod_ref, bf16[8,224,512]{2,1,0:T(8,128)(2,1)} %all-to-all-done.w_ref, f32[8,48,64]{2,1,0:T(8,128)S(1)} %copy-done.4, f32[48,64]{1,0:T(8,128)S(1)} %get-tuple-element.23.opening_ref), custom_call_target="tpu_custom_call" | custom-call | tf_op jit(solution)/shard_map/prepare/pallas_call | solution.py:151
  40.2 3.5 %all-to-all-start.1 = ((bf16[8,80,384]{2,1,0:T(8,128)(2,1)}), bf16[8,80,384]{2,1,0:T(8,128)(2,1)S(1)}, u32[]{:S(2)}, u32[]{:S(2)}) async-start(bf16[8,80,384]{2,1,0:T(8,128)(2,1)} %prepare.1), calls=%async_computation.1 | async-start | bytes 983040 | tf_op jit(solution)/shard_map/all_to_all | solution.py:406
  44.6 8.4 %all-to-all-done.1.pay_ref = bf16[8,80,384]{2,1,0:T(8,128)(2,1)S(1)} async-done(((bf16[8,80,384]{2,1,0:T(8,128)(2,1)}), bf16[8,80,384]{2,1,0:T(8,128)(2,1)S(1)}, u32[]{:S(2)}, u32[]{:S(2)}) %all-to-all-start.1) | async-done | bytes 491552 | tf_op jit(solution)/shard_map/all_to_all | solution.py:406
  53.1 4.0 %attend.1 = (bf16[384,1536]{1,0:T(8,128)(2,1)S(1)}, bf16[384,64]{1,0:T(8,128)(2,1)S(1)}) custom-call(s32[1]{0:T(128)} %constant.70.clone.1.part_ref, bf16[64,1536]{1,0:T(8,128)(2,1)S(1)} %copy-done.2, bf16[8,80,384]{2,1,0:T(8,128)(2,1)S(1)} %all-to-all-done.1.pay_ref), custom_call_target="tpu_custom_call" | custom-call | tf_op jit(solution)/shard_map/attend/pallas_call | solution.py:222
  57.1 1.1 %copy-done.5 = bf16[192,1536]{1,0:T(8,128)(2,1)S(1)} copy-done((bf16[192,1536]{1,0:T(8,128)(2,1)S(1)}, bf16[192,1536]{1,0:T(8,128)(2,1)}, u32[]{:S(2)}) %copy-start.5) | copy-done | bytes 589848
  58.2 6.8 %finish.1 = f32[4,8,24,128]{3,2,1,0:T(8,128)S(1)} custom-call(s32[8]{0:T(128)S(1)} %broadcast_xor_fusion.owner_ref, f32[1]{0:T(128)} %dynamic_slice.7.coef_ref, bf16[64,1536]{1,0:T(8,128)(2,1)S(1)} %copy-done.2, bf16[384,64]{1,0:T(8,128)(2,1)S(1)} %get-tuple-element.24.queries_ref, bf16[384,1536]{1,0:T(8,128)(2,1)S(1)} %get-tuple-element.25.att_ref, ...), custom_call_target="tpu_custom_call" | custom-call | tf_op jit(solution)/shard_map/finish/pallas_call | solution.py:274
  65.0 17.1 %all_to_all.15 = f32[32,24,128]{2,1,0:T(8,128)S(1)} all-to-all(f32[32,24,128]{2,1,0:T(8,128)S(1)} %bitcast.15), channel_id=1, replica_groups=mesh['tm'=4,'seq'=8] {'tm','seq'}, dimensions={0} | all-to-all | bytes 786432 | tf_op jit(solution)/shard_map/all_to_all | solution.py:434
  82.0 1.3 %advance.1 = (f32[8,48,64]{2,1,0:T(8,128)}, f32[8,64]{1,0:T(8,128)S(1)}) custom-call(s32[1]{0:T(128)} %bitcast.place_ref, f32[8]{0:T(128)S(1)} %broadcast_add_fusion.keep_ref, f32[4,8,24,128]{3,2,1,0:T(8,128)S(1)} %bitcast.16, f32[8,48,64]{2,1,0:T(8,128)S(1)} %copy-done.4, f32[48,64]{1,0:T(8,128)S(1)} %get-tuple-element.23.opening_ref, ...), custom_call_target="tpu_custom_call" | custom-call | tf_op jit(solution)/shard_map/advance/pallas_call | solution.py:315
  83.4 1.2 %collective-permute-done.11 = f32[8,64]{1,0:T(8,128)S(1)} collective-permute-done((f32[8,64]{1,0:T(8,128)S(1)}, f32[8,64]{1,0:T(8,128)S(1)}, u32[]{:S(2)}, u32[]{:S(2)}) %collective-permute-start.11) | collective-permute-done | bytes 2080 | tf_op jit(solution)/shard_map/ppermute | solution.py:328
  84.5 1.4 %collective-permute-start.14 = (f32[8,64]{1,0:T(8,128)S(1)}, f32[8,64]{1,0:T(8,128)S(1)}, u32[]{:S(2)}, u32[]{:S(2)}) collective-permute-start(f32[8,64]{1,0:T(8,128)S(1)} %add.58), channel_id=1, source_target_pairs={{0,6},{1,7},{2,4},{3,5},{4,2},{5,3},{6,0},{7,1},{8,14},{9,15},{10,... | collective-permute-start | bytes 6152 | tf_op jit(solution)/shard_map/ppermute | solution.py:328
  85.9 0.7 collective-permute-start.13
  86.6 1.4 %collective-permute-start.12 = (f32[8,64]{1,0:T(8,128)S(1)}, f32[8,64]{1,0:T(8,128)S(1)}, u32[]{:S(2)}, u32[]{:S(2)}) collective-permute-start(f32[8,64]{1,0:T(8,128)S(1)} %add.58), channel_id=1, source_target_pairs={{0,2},{1,3},{2,0},{3,1},{4,6},{5,7},{6,4},{7,5},{8,10},{9,11},{10,... | collective-permute-start | bytes 6152 | tf_op jit(solution)/shard_map/ppermute | solution.py:328
  88.0 1.0 %collective-permute-done.14 = f32[8,64]{1,0:T(8,128)S(1)} collective-permute-done((f32[8,64]{1,0:T(8,128)S(1)}, f32[8,64]{1,0:T(8,128)S(1)}, u32[]{:S(2)}, u32[]{:S(2)}) %collective-permute-start.14) | collective-permute-done | bytes 2080 | tf_op jit(solution)/shard_map/ppermute | solution.py:328
  (54 shorter events, 6.1 us)
Async XLA Ops:
  0.6 14.8 %copy-start = (bf16[256,4608]{1,0:T(8,128)(2,1)S(1)}, bf16[256,4608]{1,0:T(8,128)(2,1)}, u32[]{:S(2)}) copy-start(bf16[256,4608]{1,0:T(8,128)(2,1)} %param.14) | copy-start | bytes 7077892
  0.6 27.6 %collective-permute-start.4 = (bf16[192,1536]{1,0:T(8,128)(2,1)}, bf16[192,1536]{1,0:T(8,128)(2,1)}, u32[]{:S(2)}, u32[]{:S(2)}) collective-permute-start(bf16[192,1536]{1,0:T(8,128)(2,1)} %refs_0_), channel_id=1, source_target_pairs={{0,2},{1,5},{2,0},{3,7},{4,6},{5,1},{6,4},{7,3},{8,12},{9,11},{10,... | collective-permute-start | bytes 1769480 | tf_op jit(solution)/shard_map/ppermute | solution.py:336
  6.9 4.5 %copy-start.4 = (f32[8,48,64]{2,1,0:T(8,128)S(1)}, f32[8,48,64]{2,1,0:T(8,128)}, u32[]{:S(2)}) copy-start(f32[8,48,64]{2,1,0:T(8,128)} %states_ref.3) | copy-start | bytes 294916
  7.0 8.2 %copy-start.9 = (s32[8]{0:T(128)S(1)}, s32[8]{0:T(128)}, u32[]{:S(2)}) copy-start(s32[8]{0:T(128)} %param.11) | copy-start | bytes 100
  7.0 8.2 %copy-start.8 = (s32[8]{0:T(128)S(1)}, s32[8]{0:T(128)}, u32[]{:S(2)}) copy-start(s32[8]{0:T(128)} %param.12) | copy-start | bytes 100
  7.0 9.7 %copy-start.7 = (f32[48,64]{1,0:T(8,128)S(1)}, f32[48,64]{1,0:T(8,128)}, u32[]{:S(2)}) copy-start(f32[48,64]{1,0:T(8,128)} %first_ref.1) | copy-start | bytes 36868
  7.0 28.3 %all-to-all-start = ((bf16[8,224,512]{2,1,0:T(8,128)(2,1)}), bf16[8,224,512]{2,1,0:T(8,128)(2,1)}, u32[]{:S(2)}, u32[]{:S(2)}) async-start(bf16[8,224,512]{2,1,0:T(8,128)(2,1)} %copy-done.1), calls=%async_computation | async-start | bytes 3670016 | tf_op jit(solution)/shard_map/all_to_all | solution.py:382
  11.4 24.4 %copy-start.2 = (bf16[64,1536]{1,0:T(8,128)(2,1)S(1)}, bf16[64,1536]{1,0:T(8,128)(2,1)}, u32[]{:S(2)}) copy-start(bf16[64,1536]{1,0:T(8,128)(2,1)} %embed_ref.5) | copy-start | bytes 589828
  11.5 5.2 %collective-permute-start = (f32[48,64]{1,0:T(8,128)S(1)}, f32[48,64]{1,0:T(8,128)S(1)}, u32[]{:S(2)}, u32[]{:S(2)}) collective-permute-start(f32[48,64]{1,0:T(8,128)S(1)} %slice_bitcast_fusion), channel_id=1, source_target_pairs={{0,8},{8,16},{16,24},{1,9},{9,17},{17,25},{2,10},{10,18},{18,26},{... | collective-permute-start | bytes 36872 | tf_op jit(solution)/shard_map/ppermute | solution.py:388
  16.7 10.6 %collective-permute-start.3 = (f32[48,64]{1,0:T(8,128)S(1)}, f32[48,64]{1,0:T(8,128)S(1)}, u32[]{:S(2)}, u32[]{:S(2)}) collective-permute-start(f32[48,64]{1,0:T(8,128)S(1)} %get-tuple-element.38), channel_id=1, source_target_pairs={{0,24},{1,25},{2,26},{3,27},{4,28},{5,29},{6,30},{7,31}} | collective-permute-start | bytes 36872 | tf_op jit(solution)/shard_map/ppermute | solution.py:343
  22.9 4.4 %collective-permute-start.2 = (f32[48,64]{1,0:T(8,128)S(1)}, f32[48,64]{1,0:T(8,128)S(1)}, u32[]{:S(2)}, u32[]{:S(2)}) collective-permute-start(f32[48,64]{1,0:T(8,128)S(1)} %get-tuple-element.38), channel_id=1, source_target_pairs={{0,16},{8,24},{1,17},{9,25},{2,18},{10,26},{3,19},{11,27},{4,20},{... | collective-permute-start | bytes 36872 | tf_op jit(solution)/shard_map/ppermute | solution.py:343
  24.2 4.0 %collective-permute-start.1 = (f32[48,64]{1,0:T(8,128)S(1)}, f32[48,64]{1,0:T(8,128)S(1)}, u32[]{:S(2)}, u32[]{:S(2)}) collective-permute-start(f32[48,64]{1,0:T(8,128)S(1)} %get-tuple-element.38), channel_id=1, source_target_pairs={{0,8},{8,16},{16,24},{1,9},{9,17},{17,25},{2,10},{10,18},{18,26},{... | collective-permute-start | bytes 36872 | tf_op jit(solution)/shard_map/ppermute | solution.py:343
  26.7 30.4 %copy-start.6 = (bf16[1536,64]{0,1:T(8,128)(2,1)S(1)}, bf16[1536,64]{0,1:T(8,128)(2,1)}, u32[]{:S(2)}) copy-start(bf16[1536,64]{0,1:T(8,128)(2,1)} %param.17) | copy-start | bytes 589828
  28.2 15.5 %collective-permute-start.5 = (bf16[192,1536]{1,0:T(8,128)(2,1)}, bf16[192,1536]{1,0:T(8,128)(2,1)}, u32[]{:S(2)}, u32[]{:S(2)}) collective-permute-start(bf16[192,1536]{1,0:T(8,128)(2,1)} %collective-permute-done.4.refs_2_), channel_id=1, source_target_pairs={{0,8},{8,0},{16,24},{24,16},{1,9},{9,1},{17,25},{25,17},{2,10},{10... | collective-permute-start | bytes 1769480 | tf_op jit(solution)/shard_map/ppermute | solution.py:398
  35.3 17.7 %collective-permute-start.9 = (bf16[192,1536]{1,0:T(8,128)(2,1)}, bf16[192,1536]{1,0:T(8,128)(2,1)}, u32[]{:S(2)}, u32[]{:S(2)}) collective-permute-start(bf16[192,1536]{1,0:T(8,128)(2,1)} %collective-permute-done.4.refs_2_), channel_id=1, source_target_pairs={{0,4},{1,3},{2,6},{3,1},{4,0},{5,7},{6,2},{7,5},{8,10},{9,13},{10,... | collective-permute-start | bytes 1769480 | tf_op jit(solution)/shard_map/ppermute | solution.py:336
  40.2 12.8 %all-to-all-start.1 = ((bf16[8,80,384]{2,1,0:T(8,128)(2,1)}), bf16[8,80,384]{2,1,0:T(8,128)(2,1)S(1)}, u32[]{:S(2)}, u32[]{:S(2)}) async-start(bf16[8,80,384]{2,1,0:T(8,128)(2,1)} %prepare.1), calls=%async_computation.1 | async-start | bytes 983040 | tf_op jit(solution)/shard_map/all_to_all | solution.py:406
  43.7 13.4 %collective-permute-start.6 = (bf16[192,1536]{1,0:T(8,128)(2,1)}, bf16[192,1536]{1,0:T(8,128)(2,1)}, u32[]{:S(2)}, u32[]{:S(2)}) collective-permute-start(bf16[192,1536]{1,0:T(8,128)(2,1)} %refs_0_), channel_id=1, source_target_pairs={{0,1},{1,0},{2,3},{3,2},{4,5},{5,4},{6,7},{7,6},{8,9},{9,8},{10,11... | collective-permute-start | bytes 1769480 | tf_op jit(solution)/shard_map/ppermute | solution.py:328
  44.1 13.0 %collective-permute-start.7 = (bf16[192,1536]{1,0:T(8,128)(2,1)}, bf16[192,1536]{1,0:T(8,128)(2,1)}, u32[]{:S(2)}, u32[]{:S(2)}) collective-permute-start(bf16[192,1536]{1,0:T(8,128)(2,1)} %collective-permute-done.4.refs_2_), channel_id=1, source_target_pairs={{0,1},{1,0},{2,3},{3,2},{4,5},{5,4},{6,7},{7,6},{8,9},{9,8},{10,11... | collective-permute-start | bytes 1769480 | tf_op jit(solution)/shard_map/ppermute | solution.py:328
  44.3 12.8 %collective-permute-start.8 = (bf16[192,1536]{1,0:T(8,128)(2,1)}, bf16[192,1536]{1,0:T(8,128)(2,1)}, u32[]{:S(2)}, u32[]{:S(2)}) collective-permute-start(bf16[192,1536]{1,0:T(8,128)(2,1)} %collective-permute-done.5.refs_4_), channel_id=1, source_target_pairs={{0,1},{1,0},{2,3},{3,2},{4,5},{5,4},{6,7},{7,6},{8,9},{9,8},{10,11... | collective-permute-start | bytes 1769480 | tf_op jit(solution)/shard_map/ppermute | solution.py:328
  53.0 4.1 %collective-permute-start.10 = (bf16[192,1536]{1,0:T(8,128)(2,1)}, bf16[192,1536]{1,0:T(8,128)(2,1)}, u32[]{:S(2)}, u32[]{:S(2)}) collective-permute-start(bf16[192,1536]{1,0:T(8,128)(2,1)} %collective-permute-done.9.refs_6_), channel_id=1, source_target_pairs={{0,1},{1,0},{2,3},{3,2},{4,5},{5,4},{6,7},{7,6},{8,9},{9,8},{10,11... | collective-permute-start | bytes 1769480 | tf_op jit(solution)/shard_map/ppermute | solution.py:328
  83.4 1.2 %collective-permute-start.11 = (f32[8,64]{1,0:T(8,128)S(1)}, f32[8,64]{1,0:T(8,128)S(1)}, u32[]{:S(2)}, u32[]{:S(2)}) collective-permute-start(f32[8,64]{1,0:T(8,128)S(1)} %get-tuple-element.35), channel_id=1, source_target_pairs={{0,1},{1,0},{2,3},{3,2},{4,5},{5,4},{6,7},{7,6},{8,9},{9,8},{10,11... | collective-permute-start | bytes 6152 | tf_op jit(solution)/shard_map/ppermute | solution.py:328
  84.5 4.5 %collective-permute-start.14 = (f32[8,64]{1,0:T(8,128)S(1)}, f32[8,64]{1,0:T(8,128)S(1)}, u32[]{:S(2)}, u32[]{:S(2)}) collective-permute-start(f32[8,64]{1,0:T(8,128)S(1)} %add.58), channel_id=1, source_target_pairs={{0,6},{1,7},{2,4},{3,5},{4,2},{5,3},{6,0},{7,1},{8,14},{9,15},{10,... | collective-permute-start | bytes 6152 | tf_op jit(solution)/shard_map/ppermute | solution.py:328
  85.9 3.6 %collective-permute-start.13 = (f32[8,64]{1,0:T(8,128)S(1)}, f32[8,64]{1,0:T(8,128)S(1)}, u32[]{:S(2)}, u32[]{:S(2)}) collective-permute-start(f32[8,64]{1,0:T(8,128)S(1)} %add.58), channel_id=1, source_target_pairs={{0,4},{1,5},{2,6},{3,7},{4,0},{5,1},{6,2},{7,3},{8,12},{9,13},{10,... | collective-permute-start | bytes 6152 | tf_op jit(solution)/shard_map/ppermute | solution.py:328
  86.6 3.6 %collective-permute-start.12 = (f32[8,64]{1,0:T(8,128)S(1)}, f32[8,64]{1,0:T(8,128)S(1)}, u32[]{:S(2)}, u32[]{:S(2)}) collective-permute-start(f32[8,64]{1,0:T(8,128)S(1)} %add.58), channel_id=1, source_target_pairs={{0,2},{1,3},{2,0},{3,1},{4,6},{5,7},{6,4},{7,5},{8,10},{9,11},{10,... | collective-permute-start | bytes 6152 | tf_op jit(solution)/shard_map/ppermute | solution.py:328
  (3 other events, 3.8 us)

commit v4 on v3

--- a/solution.py
+++ b/solution.py
@@ -258,12 +258,14 @@
         total = total + jnp.sum(updated, axis=1, keepdims=True)
     centred = sum_scr[...] - total * (1.0 / width)
     variance = jnp.mean(centred * centred, axis=1, keepdims=True)
-    normed = (centred * lax.rsqrt(variance + 1e-6)).astype(BF)
-    noise = dot(normed, final_ref[...], ((1,), (1,))) * coef_ref[0]
+    normed = centred * lax.rsqrt(variance + 1e-6)
+    high = normed.astype(BF)
+    noise = dot(high, final_ref[...], ((1,), (1,)))
+    noise = noise * coef_ref[0]
     half = tokd // 2
     for i in range(out_ref.shape[1]):
         block = noise[i * tokd : (i + 1) * tokd]
-        block = jnp.concatenate([block[:half], block[half:]], axis=1)
+        block = jnp.concatenate([block[:half], block[half:]], axis=1).astype(BF)
         for j in range(out_ref.shape[0]):
             out_ref[j, i] = block
 
@@ -273,7 +275,7 @@
     length = queries.shape[0]
     return pl.pallas_call(
         functools.partial(finish_kernel, tokd),
-        out_shape=jax.ShapeDtypeStruct((repeats, length // tokd, tokd // 2, 2 * chans), F32),
+        out_shape=jax.ShapeDtypeStruct((repeats, length // tokd, tokd // 2, 2 * chans), BF),
         in_specs=[SMEM] * 2 + [VMEM] * 5 + [pl.BlockSpec(memory_space=pl.ANY)] * len(parts),
         scratch_shapes=[
             pltpu.VMEM((att.shape[1], width), BF),
@@ -290,9 +292,9 @@
     steps, tokd, chans = states_ref.shape
     packed = jnp.zeros(noise_ref.shape[2:], F32)
     for group in range(groups - 1):
-        total = noise_ref[group, 0]
+        total = noise_ref[group, 0].astype(F32)
         for i in range(1, count):
-            total = total + noise_ref[group, i]
+            total = total + noise_ref[group, i].astype(F32)
         packed = packed + jnp.where(place_ref[0] > group, total, jnp.zeros_like(total))
 
     def unpack(x):
@@ -300,9 +302,9 @@
 
     state = first_ref[...] + kept_ref[...] + unpack(packed)
     for t in range(steps):
-        noise = noise_ref[place_ref[0], t * share]
+        noise = noise_ref[place_ref[0], t * share].astype(F32)
         for i in range(1, share):
-            noise = noise + noise_ref[place_ref[0], t * share + i]
+            noise = noise + noise_ref[place_ref[0], t * share + i].astype(F32)
         before = opening_ref[...] if t == 0 else states_ref[t - 1]
         state = state + (keep_ref[t] * before + unpack(noise))
         out_ref[t] = state
@@ -426,7 +428,7 @@
     )
 
     if share > 1:
-        full = jnp.zeros((share,) + noise.shape[1:], F32)
+        full = jnp.zeros((share,) + noise.shape[1:], BF)
         full = lax.dynamic_update_slice(full, noise, (part, 0, 0, 0))
         noise = jnp.broadcast_to(full[None], (tm_count,) + full.shape)
     block = noise.shape[-2:]

time: 91.3 us -> 87.2 us (0.955)
  blocking collectives: 17.1 us -> 12.8 us
    all_to_all x1, blocking collectives: 17.1 us -> 12.8 us  [per_device(): noise = lax.all_to_all(noise, ('tm', 'seq'), 0, 0, tiled=True)]
where the time goes in v4:
time: 87.2 us; the launch traced here: 86.7 us
  starting transfers between devices  32.5 us (37%)
  waiting for transfers between devices  17.6 us (20%)
  Pallas kernels  17 us (19%)
  blocking collectives  12.8 us (15%)
  local copies, waits for them, and re-layouts  4.53 us (5%)
  other arithmetic  0.98 us (1%)
  between operations  0.9 us (1%)
    all_to_all x1, blocking collectives, per_device(): noise = lax.all_to_all(noise, ('tm', 'seq'), 0, 0, tiled=True)  12.8 us
    ppermute x3, starting transfers between devices, earlier_total(): lax.ppermute(total, 'tm', [(i, i + by) for i in range(count - by)])  10 us
    all_to_all x1, waiting for transfers between devices, per_device(): received = lax.all_to_all(sent, 'seq', 0, 0, tiled=True)  8.4 us
    pallas_call x1, Pallas kernels, finish(): pl.pallas_call(functools.partial(finish_kernel, tokd), out_shape=jax.Shap...  6.76 us
    ppermute x8, starting transfers between devices, swap(): return lax.ppermute(x, 'seq', [(i, i ^ mask) for i in range(count)])  4.99 us
    all_to_all x1, waiting for transfers between devices, per_device(): w_mine = lax.all_to_all(w_sent, 'seq', 0, 0, tiled=True)  4.69 us
    all_to_all x1, starting transfers between devices, per_device(): w_mine = lax.all_to_all(w_sent, 'seq', 0, 0, tiled=True)  4.47 us
    pallas_call x1, Pallas kernels, prepare(): pl.pallas_call(functools.partial(prepare_kernel, per, sub), out_shape=jax...  4.38 us
  transfers between devices with their start and end apart: 17, of which 8 were waited for; matrix products, arithmetic and copies ran while one was open for 2% of the time, Pallas kernels for 10%

profile of v4, /device:TPU:0, one launch (start us, length us, event | category | flops | bytes accessed | tf_op | source)
XLA Modules:
  0.0 86.7 jit_solution(15014970451153141723)
XLA Ops:
  0.6 3.0 %collective-permute-start.4 = (bf16[192,1536]{1,0:T(8,128)(2,1)}, bf16[192,1536]{1,0:T(8,128)(2,1)}, u32[]{:S(2)}, u32[]{:S(2)}) collective-permute-start(bf16[192,1536]{1,0:T(8,128)(2,1)} %refs_0_), channel_id=1, source_target_pairs={{0,2},{1,5},{2,0},{3,7},{4,6},{5,1},{6,4},{7,3},{8,12},{9,11},{10,... | collective-permute-start | bytes 1769480 | tf_op jit(solution)/shard_map/ppermute | solution.py:338
  3.7 1.5 %copy-done.4 = bf16[192,12,384]{2,0,1:T(8,128)(2,1)S(1)} copy-done((bf16[192,12,384]{2,0,1:T(8,128)(2,1)S(1)}, bf16[192,12,384]{2,0,1:T(8,128)(2,1)}, u32[]{:S(2)}) %copy-start.4) | copy-done | bytes 1769496
  5.7 1.2 %copy-done.1 = bf16[8,224,512]{2,1,0:T(8,128)(2,1)} copy-done((bf16[8,224,512]{2,1,0:T(8,128)(2,1)}, bf16[8,224,512]{2,1,0:T(8,128)(2,1)S(1)}, u32[]{:S(2)}) %copy-start.1) | copy-done | bytes 1835032
  7.0 4.5 %all-to-all-start = ((bf16[8,224,512]{2,1,0:T(8,128)(2,1)}), bf16[8,224,512]{2,1,0:T(8,128)(2,1)}, u32[]{:S(2)}, u32[]{:S(2)}) async-start(bf16[8,224,512]{2,1,0:T(8,128)(2,1)} %copy-done.1), calls=%async_computation | async-start | bytes 3670016 | tf_op jit(solution)/shard_map/all_to_all | solution.py:384
  11.5 3.7 %collective-permute-start = (f32[48,64]{1,0:T(8,128)S(1)}, f32[48,64]{1,0:T(8,128)S(1)}, u32[]{:S(2)}, u32[]{:S(2)}) collective-permute-start(f32[48,64]{1,0:T(8,128)S(1)} %slice_bitcast_fusion), channel_id=1, source_target_pairs={{0,8},{8,16},{16,24},{1,9},{9,17},{17,25},{2,10},{10,18},{18,26},{... | collective-permute-start | bytes 36872 | tf_op jit(solution)/shard_map/ppermute | solution.py:390
  16.7 6.2 %collective-permute-start.3 = (f32[48,64]{1,0:T(8,128)S(1)}, f32[48,64]{1,0:T(8,128)S(1)}, u32[]{:S(2)}, u32[]{:S(2)}) collective-permute-start(f32[48,64]{1,0:T(8,128)S(1)} %get-tuple-element.38), channel_id=1, source_target_pairs={{0,24},{1,25},{2,26},{3,27},{4,28},{5,29},{6,30},{7,31}} | collective-permute-start | bytes 36872 | tf_op jit(solution)/shard_map/ppermute | solution.py:345
  22.9 1.3 %collective-permute-start.2 = (f32[48,64]{1,0:T(8,128)S(1)}, f32[48,64]{1,0:T(8,128)S(1)}, u32[]{:S(2)}, u32[]{:S(2)}) collective-permute-start(f32[48,64]{1,0:T(8,128)S(1)} %get-tuple-element.38), channel_id=1, source_target_pairs={{0,16},{8,24},{1,17},{9,25},{2,18},{10,26},{3,19},{11,27},{4,20},{... | collective-permute-start | bytes 36872 | tf_op jit(solution)/shard_map/ppermute | solution.py:345
  24.2 2.5 %collective-permute-start.1 = (f32[48,64]{1,0:T(8,128)S(1)}, f32[48,64]{1,0:T(8,128)S(1)}, u32[]{:S(2)}, u32[]{:S(2)}) collective-permute-start(f32[48,64]{1,0:T(8,128)S(1)} %get-tuple-element.38), channel_id=1, source_target_pairs={{0,8},{8,16},{16,24},{1,9},{9,17},{17,25},{2,10},{10,18},{18,26},{... | collective-permute-start | bytes 36872 | tf_op jit(solution)/shard_map/ppermute | solution.py:345
  27.3 0.9 %collective-permute-done.1 = f32[48,64]{1,0:T(8,128)S(1)} collective-permute-done((f32[48,64]{1,0:T(8,128)S(1)}, f32[48,64]{1,0:T(8,128)S(1)}, u32[]{:S(2)}, u32[]{:S(2)}) %collective-permute-start.1) | collective-permute-done | bytes 12320 | tf_op jit(solution)/shard_map/ppermute | solution.py:345
  28.2 2.4 %collective-permute-start.5 = (bf16[192,1536]{1,0:T(8,128)(2,1)}, bf16[192,1536]{1,0:T(8,128)(2,1)}, u32[]{:S(2)}, u32[]{:S(2)}) collective-permute-start(bf16[192,1536]{1,0:T(8,128)(2,1)} %collective-permute-done.4.refs_2_), channel_id=1, source_target_pairs={{0,8},{8,0},{16,24},{24,16},{1,9},{9,1},{17,25},{25,17},{2,10},{10... | collective-permute-start | bytes 1769480 | tf_op jit(solution)/shard_map/ppermute | solution.py:400
  30.6 4.7 %all-to-all-done.w_ref = bf16[8,224,512]{2,1,0:T(8,128)(2,1)} async-done(((bf16[8,224,512]{2,1,0:T(8,128)(2,1)}), bf16[8,224,512]{2,1,0:T(8,128)(2,1)}, u32[]{:S(2)}, u32[]{:S(2)}) %all-to-all-start) | async-done | bytes 1835040 | tf_op jit(solution)/shard_map/all_to_all | solution.py:384
  35.8 4.4 %prepare.1 = bf16[8,80,384]{2,1,0:T(8,128)(2,1)} custom-call(bf16[64,1536]{1,0:T(8,128)(2,1)S(1)} %copy-done.2, f32[8,4608]{1,0:T(8,128)S(1)} %fusion.2.mod_ref, bf16[8,224,512]{2,1,0:T(8,128)(2,1)} %all-to-all-done.w_ref, f32[8,48,64]{2,1,0:T(8,128)S(1)} %copy-done.3, f32[48,64]{1,0:T(8,128)S(1)} %get-tuple-element.23.opening_ref), custom_call_target="tpu_custom_call" | custom-call | tf_op jit(solution)/shard_map/prepare/pallas_call | solution.py:151
  40.2 3.5 %all-to-all-start.1 = ((bf16[8,80,384]{2,1,0:T(8,128)(2,1)}), bf16[8,80,384]{2,1,0:T(8,128)(2,1)S(1)}, u32[]{:S(2)}, u32[]{:S(2)}) async-start(bf16[8,80,384]{2,1,0:T(8,128)(2,1)} %prepare.1), calls=%async_computation.1 | async-start | bytes 983040 | tf_op jit(solution)/shard_map/all_to_all | solution.py:408
  44.6 8.4 %all-to-all-done.1.pay_ref = bf16[8,80,384]{2,1,0:T(8,128)(2,1)S(1)} async-done(((bf16[8,80,384]{2,1,0:T(8,128)(2,1)}), bf16[8,80,384]{2,1,0:T(8,128)(2,1)S(1)}, u32[]{:S(2)}, u32[]{:S(2)}) %all-to-all-start.1) | async-done | bytes 491552 | tf_op jit(solution)/shard_map/all_to_all | solution.py:408
  53.1 4.0 %attend.1 = (bf16[384,1536]{1,0:T(8,128)(2,1)S(1)}, bf16[384,64]{1,0:T(8,128)(2,1)S(1)}) custom-call(s32[1]{0:T(128)} %constant.70.clone.1.part_ref, bf16[64,1536]{1,0:T(8,128)(2,1)S(1)} %copy-done.2, bf16[8,80,384]{2,1,0:T(8,128)(2,1)S(1)} %all-to-all-done.1.pay_ref), custom_call_target="tpu_custom_call" | custom-call | tf_op jit(solution)/shard_map/attend/pallas_call | solution.py:222
  57.1 1.1 %copy-done.5 = bf16[192,1536]{1,0:T(8,128)(2,1)S(1)} copy-done((bf16[192,1536]{1,0:T(8,128)(2,1)S(1)}, bf16[192,1536]{1,0:T(8,128)(2,1)}, u32[]{:S(2)}) %copy-start.5) | copy-done | bytes 589848
  58.2 6.8 %finish.1 = bf16[4,8,24,128]{3,2,1,0:T(8,128)(2,1)S(1)} custom-call(s32[8]{0:T(128)S(1)} %broadcast_xor_fusion.owner_ref, f32[1]{0:T(128)} %dynamic_slice.7.coef_ref, bf16[64,1536]{1,0:T(8,128)(2,1)S(1)} %copy-done.2, bf16[384,64]{1,0:T(8,128)(2,1)S(1)} %get-tuple-element.24.queries_ref, bf16[384,1536]{1,0:T(8,128)(2,1)S(1)} %get-tuple-element.25.att_ref, ...), custom_call_target="tpu_custom_call" | custom-call | tf_op jit(solution)/shard_map/finish/pallas_call | solution.py:276
  65.0 12.8 %all_to_all.15 = bf16[32,24,128]{2,1,0:T(8,128)(2,1)S(1)} all-to-all(bf16[32,24,128]{2,1,0:T(8,128)(2,1)S(1)} %bitcast.15), channel_id=1, replica_groups=mesh['tm'=4,'seq'=8] {'tm','seq'}, dimensions={0} | all-to-all | bytes 393216 | tf_op jit(solution)/shard_map/all_to_all | solution.py:436
  77.7 1.3 %advance.1 = (f32[8,48,64]{2,1,0:T(8,128)}, f32[8,64]{1,0:T(8,128)S(1)}) custom-call(s32[1]{0:T(128)} %bitcast.place_ref, f32[8]{0:T(128)S(1)} %broadcast_add_fusion.keep_ref, bf16[4,8,24,128]{3,2,1,0:T(8,128)(2,1)S(1)} %bitcast.16, f32[8,48,64]{2,1,0:T(8,128)S(1)} %copy-done.3, f32[48,64]{1,0:T(8,128)S(1)} %get-tuple-element.23.opening_ref, ...), custom_call_target="tpu_custom_call" | custom-call | tf_op jit(solution)/shard_map/advance/pallas_call | solution.py:317
  79.7 0.8 collective-permute-done.11
  80.5 1.2 %collective-permute-start.14 = (f32[8,64]{1,0:T(8,128)S(1)}, f32[8,64]{1,0:T(8,128)S(1)}, u32[]{:S(2)}, u32[]{:S(2)}) collective-permute-start(f32[8,64]{1,0:T(8,128)S(1)} %add.58), channel_id=1, source_target_pairs={{0,6},{1,7},{2,4},{3,5},{4,2},{5,3},{6,0},{7,1},{8,14},{9,15},{10,... | collective-permute-start | bytes 6152 | tf_op jit(solution)/shard_map/ppermute | solution.py:330
  81.7 0.8 collective-permute-start.13
  82.5 1.5 %collective-permute-start.12 = (f32[8,64]{1,0:T(8,128)S(1)}, f32[8,64]{1,0:T(8,128)S(1)}, u32[]{:S(2)}, u32[]{:S(2)}) collective-permute-start(f32[8,64]{1,0:T(8,128)S(1)} %add.58), channel_id=1, source_target_pairs={{0,2},{1,3},{2,0},{3,1},{4,6},{5,7},{6,4},{7,5},{8,10},{9,11},{10,... | collective-permute-start | bytes 6152 | tf_op jit(solution)/shard_map/ppermute | solution.py:330
  84.0 1.0 %collective-permute-done.14 = f32[8,64]{1,0:T(8,128)S(1)} collective-permute-done((f32[8,64]{1,0:T(8,128)S(1)}, f32[8,64]{1,0:T(8,128)S(1)}, u32[]{:S(2)}, u32[]{:S(2)}) %collective-permute-start.14) | collective-permute-done | bytes 2080 | tf_op jit(solution)/shard_map/ppermute | solution.py:330
  (54 shorter events, 6.6 us)
Async XLA Ops:
  0.6 14.8 %copy-start = (bf16[256,4608]{1,0:T(8,128)(2,1)S(1)}, bf16[256,4608]{1,0:T(8,128)(2,1)}, u32[]{:S(2)}) copy-start(bf16[256,4608]{1,0:T(8,128)(2,1)} %param.14) | copy-start | bytes 7077892
  0.6 27.6 %collective-permute-start.4 = (bf16[192,1536]{1,0:T(8,128)(2,1)}, bf16[192,1536]{1,0:T(8,128)(2,1)}, u32[]{:S(2)}, u32[]{:S(2)}) collective-permute-start(bf16[192,1536]{1,0:T(8,128)(2,1)} %refs_0_), channel_id=1, source_target_pairs={{0,2},{1,5},{2,0},{3,7},{4,6},{5,1},{6,4},{7,3},{8,12},{9,11},{10,... | collective-permute-start | bytes 1769480 | tf_op jit(solution)/shard_map/ppermute | solution.py:338
  6.9 4.5 %copy-start.3 = (f32[8,48,64]{2,1,0:T(8,128)S(1)}, f32[8,48,64]{2,1,0:T(8,128)}, u32[]{:S(2)}) copy-start(f32[8,48,64]{2,1,0:T(8,128)} %states_ref.3) | copy-start | bytes 294916
  7.0 8.2 %copy-start.9 = (s32[8]{0:T(128)S(1)}, s32[8]{0:T(128)}, u32[]{:S(2)}) copy-start(s32[8]{0:T(128)} %param.11) | copy-start | bytes 100
  7.0 8.2 %copy-start.8 = (s32[8]{0:T(128)S(1)}, s32[8]{0:T(128)}, u32[]{:S(2)}) copy-start(s32[8]{0:T(128)} %param.12) | copy-start | bytes 100
  7.0 9.7 %copy-start.7 = (f32[48,64]{1,0:T(8,128)S(1)}, f32[48,64]{1,0:T(8,128)}, u32[]{:S(2)}) copy-start(f32[48,64]{1,0:T(8,128)} %first_ref.1) | copy-start | bytes 36868
  7.0 28.3 %all-to-all-start = ((bf16[8,224,512]{2,1,0:T(8,128)(2,1)}), bf16[8,224,512]{2,1,0:T(8,128)(2,1)}, u32[]{:S(2)}, u32[]{:S(2)}) async-start(bf16[8,224,512]{2,1,0:T(8,128)(2,1)} %copy-done.1), calls=%async_computation | async-start | bytes 3670016 | tf_op jit(solution)/shard_map/all_to_all | solution.py:384
  11.4 24.4 %copy-start.2 = (bf16[64,1536]{1,0:T(8,128)(2,1)S(1)}, bf16[64,1536]{1,0:T(8,128)(2,1)}, u32[]{:S(2)}) copy-start(bf16[64,1536]{1,0:T(8,128)(2,1)} %embed_ref.5) | copy-start | bytes 589828
  11.5 5.2 %collective-permute-start = (f32[48,64]{1,0:T(8,128)S(1)}, f32[48,64]{1,0:T(8,128)S(1)}, u32[]{:S(2)}, u32[]{:S(2)}) collective-permute-start(f32[48,64]{1,0:T(8,128)S(1)} %slice_bitcast_fusion), channel_id=1, source_target_pairs={{0,8},{8,16},{16,24},{1,9},{9,17},{17,25},{2,10},{10,18},{18,26},{... | collective-permute-start | bytes 36872 | tf_op jit(solution)/shard_map/ppermute | solution.py:390
  16.7 10.6 %collective-permute-start.3 = (f32[48,64]{1,0:T(8,128)S(1)}, f32[48,64]{1,0:T(8,128)S(1)}, u32[]{:S(2)}, u32[]{:S(2)}) collective-permute-start(f32[48,64]{1,0:T(8,128)S(1)} %get-tuple-element.38), channel_id=1, source_target_pairs={{0,24},{1,25},{2,26},{3,27},{4,28},{5,29},{6,30},{7,31}} | collective-permute-start | bytes 36872 | tf_op jit(solution)/shard_map/ppermute | solution.py:345
  22.9 4.4 %collective-permute-start.2 = (f32[48,64]{1,0:T(8,128)S(1)}, f32[48,64]{1,0:T(8,128)S(1)}, u32[]{:S(2)}, u32[]{:S(2)}) collective-permute-start(f32[48,64]{1,0:T(8,128)S(1)} %get-tuple-element.38), channel_id=1, source_target_pairs={{0,16},{8,24},{1,17},{9,25},{2,18},{10,26},{3,19},{11,27},{4,20},{... | collective-permute-start | bytes 36872 | tf_op jit(solution)/shard_map/ppermute | solution.py:345
  24.2 4.0 %collective-permute-start.1 = (f32[48,64]{1,0:T(8,128)S(1)}, f32[48,64]{1,0:T(8,128)S(1)}, u32[]{:S(2)}, u32[]{:S(2)}) collective-permute-start(f32[48,64]{1,0:T(8,128)S(1)} %get-tuple-element.38), channel_id=1, source_target_pairs={{0,8},{8,16},{16,24},{1,9},{9,17},{17,25},{2,10},{10,18},{18,26},{... | collective-permute-start | bytes 36872 | tf_op jit(solution)/shard_map/ppermute | solution.py:345
  26.7 30.4 %copy-start.6 = (bf16[1536,64]{0,1:T(8,128)(2,1)S(1)}, bf16[1536,64]{0,1:T(8,128)(2,1)}, u32[]{:S(2)}) copy-start(bf16[1536,64]{0,1:T(8,128)(2,1)} %param.17) | copy-start | bytes 589828
  28.2 15.5 %collective-permute-start.5 = (bf16[192,1536]{1,0:T(8,128)(2,1)}, bf16[192,1536]{1,0:T(8,128)(2,1)}, u32[]{:S(2)}, u32[]{:S(2)}) collective-permute-start(bf16[192,1536]{1,0:T(8,128)(2,1)} %collective-permute-done.4.refs_2_), channel_id=1, source_target_pairs={{0,8},{8,0},{16,24},{24,16},{1,9},{9,1},{17,25},{25,17},{2,10},{10... | collective-permute-start | bytes 1769480 | tf_op jit(solution)/shard_map/ppermute | solution.py:400
  35.3 17.7 %collective-permute-start.9 = (bf16[192,1536]{1,0:T(8,128)(2,1)}, bf16[192,1536]{1,0:T(8,128)(2,1)}, u32[]{:S(2)}, u32[]{:S(2)}) collective-permute-start(bf16[192,1536]{1,0:T(8,128)(2,1)} %collective-permute-done.4.refs_2_), channel_id=1, source_target_pairs={{0,4},{1,3},{2,6},{3,1},{4,0},{5,7},{6,2},{7,5},{8,10},{9,13},{10,... | collective-permute-start | bytes 1769480 | tf_op jit(solution)/shard_map/ppermute | solution.py:338
  40.2 12.8 %all-to-all-start.1 = ((bf16[8,80,384]{2,1,0:T(8,128)(2,1)}), bf16[8,80,384]{2,1,0:T(8,128)(2,1)S(1)}, u32[]{:S(2)}, u32[]{:S(2)}) async-start(bf16[8,80,384]{2,1,0:T(8,128)(2,1)} %prepare.1), calls=%async_computation.1 | async-start | bytes 983040 | tf_op jit(solution)/shard_map/all_to_all | solution.py:408
  43.7 13.4 %collective-permute-start.6 = (bf16[192,1536]{1,0:T(8,128)(2,1)}, bf16[192,1536]{1,0:T(8,128)(2,1)}, u32[]{:S(2)}, u32[]{:S(2)}) collective-permute-start(bf16[192,1536]{1,0:T(8,128)(2,1)} %refs_0_), channel_id=1, source_target_pairs={{0,1},{1,0},{2,3},{3,2},{4,5},{5,4},{6,7},{7,6},{8,9},{9,8},{10,11... | collective-permute-start | bytes 1769480 | tf_op jit(solution)/shard_map/ppermute | solution.py:330
  44.1 13.0 %collective-permute-start.7 = (bf16[192,1536]{1,0:T(8,128)(2,1)}, bf16[192,1536]{1,0:T(8,128)(2,1)}, u32[]{:S(2)}, u32[]{:S(2)}) collective-permute-start(bf16[192,1536]{1,0:T(8,128)(2,1)} %collective-permute-done.4.refs_2_), channel_id=1, source_target_pairs={{0,1},{1,0},{2,3},{3,2},{4,5},{5,4},{6,7},{7,6},{8,9},{9,8},{10,11... | collective-permute-start | bytes 1769480 | tf_op jit(solution)/shard_map/ppermute | solution.py:330
  44.3 12.8 %collective-permute-start.8 = (bf16[192,1536]{1,0:T(8,128)(2,1)}, bf16[192,1536]{1,0:T(8,128)(2,1)}, u32[]{:S(2)}, u32[]{:S(2)}) collective-permute-start(bf16[192,1536]{1,0:T(8,128)(2,1)} %collective-permute-done.5.refs_4_), channel_id=1, source_target_pairs={{0,1},{1,0},{2,3},{3,2},{4,5},{5,4},{6,7},{7,6},{8,9},{9,8},{10,11... | collective-permute-start | bytes 1769480 | tf_op jit(solution)/shard_map/ppermute | solution.py:330
  53.0 4.1 %collective-permute-start.10 = (bf16[192,1536]{1,0:T(8,128)(2,1)}, bf16[192,1536]{1,0:T(8,128)(2,1)}, u32[]{:S(2)}, u32[]{:S(2)}) collective-permute-start(bf16[192,1536]{1,0:T(8,128)(2,1)} %collective-permute-done.9.refs_6_), channel_id=1, source_target_pairs={{0,1},{1,0},{2,3},{3,2},{4,5},{5,4},{6,7},{7,6},{8,9},{9,8},{10,11... | collective-permute-start | bytes 1769480 | tf_op jit(solution)/shard_map/ppermute | solution.py:330
  79.1 1.4 %collective-permute-start.11 = (f32[8,64]{1,0:T(8,128)S(1)}, f32[8,64]{1,0:T(8,128)S(1)}, u32[]{:S(2)}, u32[]{:S(2)}) collective-permute-start(f32[8,64]{1,0:T(8,128)S(1)} %get-tuple-element.35), channel_id=1, source_target_pairs={{0,1},{1,0},{2,3},{3,2},{4,5},{5,4},{6,7},{7,6},{8,9},{9,8},{10,11... | collective-permute-start | bytes 6152 | tf_op jit(solution)/shard_map/ppermute | solution.py:330
  80.5 4.5 %collective-permute-start.14 = (f32[8,64]{1,0:T(8,128)S(1)}, f32[8,64]{1,0:T(8,128)S(1)}, u32[]{:S(2)}, u32[]{:S(2)}) collective-permute-start(f32[8,64]{1,0:T(8,128)S(1)} %add.58), channel_id=1, source_target_pairs={{0,6},{1,7},{2,4},{3,5},{4,2},{5,3},{6,0},{7,1},{8,14},{9,15},{10,... | collective-permute-start | bytes 6152 | tf_op jit(solution)/shard_map/ppermute | solution.py:330
  81.7 3.6 %collective-permute-start.13 = (f32[8,64]{1,0:T(8,128)S(1)}, f32[8,64]{1,0:T(8,128)S(1)}, u32[]{:S(2)}, u32[]{:S(2)}) collective-permute-start(f32[8,64]{1,0:T(8,128)S(1)} %add.58), channel_id=1, source_target_pairs={{0,4},{1,5},{2,6},{3,7},{4,0},{5,1},{6,2},{7,3},{8,12},{9,13},{10,... | collective-permute-start | bytes 6152 | tf_op jit(solution)/shard_map/ppermute | solution.py:330
  82.5 3.6 %collective-permute-start.12 = (f32[8,64]{1,0:T(8,128)S(1)}, f32[8,64]{1,0:T(8,128)S(1)}, u32[]{:S(2)}, u32[]{:S(2)}) collective-permute-start(f32[8,64]{1,0:T(8,128)S(1)} %add.58), channel_id=1, source_target_pairs={{0,2},{1,3},{2,0},{3,1},{4,6},{5,7},{6,4},{7,5},{8,10},{9,11},{10,... | collective-permute-start | bytes 6152 | tf_op jit(solution)/shard_map/ppermute | solution.py:330
  (3 other events, 3.8 us)

commit v5 on v4

--- a/solution.py
+++ b/solution.py
@@ -57,31 +57,54 @@
     return (main, rest, each, -(-(rows // 16) // each))
 
 
-def cut_kernel(n_sub, per, sub, w_ref, out_ref):
+def cut_kernel(n_sub, per, sub, w_ref, out_ref, w_scr, out_scr, in_sem, out_sem):
+    arriving = []
+    for head in range(w_ref.shape[0]):
+        arriving.append(pltpu.make_async_copy(w_ref.at[head], w_scr.at[head], in_sem.at[head]))
+        arriving[-1].start()
+    here = 0
+    leaving = []
     for dest in range(out_ref.shape[0]):
+        needed = ((dest + 1) * per - 1) // n_sub + 1
+        for copy in arriving[here:needed]:
+            copy.wait()
+        here = max(here, needed)
         pieces = []
         for kind in (0, 2, 1):
             for i in range(per):
                 head, part = divmod(dest * per + i, n_sub)
                 start = kind * n_sub * sub + part * sub
-                pieces.append(w_ref[head, :, start : start + sub])
+                pieces.append(w_scr[head, :, start : start + sub])
         block = jnp.concatenate(pieces, axis=1)
         rows, lanes = block.shape
         main, rest, each, strips = packing(rows, lanes)
-        out_ref[dest, :rows, :] = block[:, :main]
+        out_scr[dest, :rows, :] = block[:, :main]
         groups = [block[i : i + 16, main:] for i in range(0, rows, 16) if rest]
         groups += [jnp.zeros((16, rest), BF)] * (strips * each - len(groups))
         for i in range(strips):
             strip = jnp.concatenate(groups[i * each : (i + 1) * each], axis=1)
-            out_ref[dest, rows + 16 * i : rows + 16 * (i + 1), :] = strip
+            out_scr[dest, rows + 16 * i : rows + 16 * (i + 1), :] = strip
+        leaving.append(pltpu.make_async_copy(out_scr.at[dest], out_ref.at[dest], out_sem.at[dest]))
+        leaving[-1].start()
+    for copy in leaving:
+        copy.wait()
 
 
 def cut(w, count, n_sub, per, sub):
     main, _, _, strips = packing(w.shape[1], 3 * per * sub)
+    shape = (count, w.shape[1] + 16 * strips, main)
     return pl.pallas_call(
         functools.partial(cut_kernel, n_sub, per, sub),
-        out_shape=jax.ShapeDtypeStruct((count, w.shape[1] + 16 * strips, main), BF),
-        compiler_params=params(6),
+        out_shape=jax.ShapeDtypeStruct(shape, BF),
+        in_specs=[pl.BlockSpec(memory_space=pl.ANY)],
+        out_specs=pl.BlockSpec(memory_space=pl.ANY),
+        scratch_shapes=[
+            pltpu.VMEM(w.shape, BF),
+            pltpu.VMEM(shape, BF),
+            pltpu.SemaphoreType.DMA((w.shape[0],)),
+            pltpu.SemaphoreType.DMA((count,)),
+        ],
+        compiler_params=params(56),
         name="cut",
     )(w)
 
@@ -155,7 +178,7 @@
             pltpu.VMEM((steps * ROWS, embed.shape[1]), BF),
             pltpu.VMEM((embed.shape[1], 128), BF),
         ],
-        compiler_params=params(10),
+        compiler_params=params(7),
         name="prepare",
     )(embed, mod_all, w_mine, states, opening)
 
@@ -227,7 +250,7 @@
         ],
         in_specs=[SMEM, VMEM, VMEM],
         scratch_shapes=[pltpu.VMEM((length, embed.shape[0]), F32)],
-        compiler_params=params(9 if share == 1 else 40),
+        compiler_params=params(7 if share == 1 else 40),
         name="attend",
     )(part, embed, payload)
 
@@ -282,7 +305,7 @@
             pltpu.VMEM((length, width), F32),
             pltpu.SemaphoreType.DMA((2, len(parts))),
         ],
-        compiler_params=params(15),
+        compiler_params=params(12),
         name="finish",
     )(owners, coef, embed, queries, att, gate, final, *parts)
 
@@ -321,7 +344,7 @@
             jax.ShapeDtypeStruct((steps, chans), F32),
         ],
         in_specs=[SMEM] * 2 + [VMEM] * 5,
-        compiler_params=params(4),
+        compiler_params=params(2),
         name="advance",
     )(place, keep, noise, states, opening, first, kept)
 
@@ -396,7 +419,7 @@
     gate = lax.dynamic_slice(mod_all, (mine, 2 * width), (1, width))
     coef = lax.dynamic_slice(noise_coef, (mine,), (1,))
     if by_planes:
-        late_first, _ = barrier((first, (kept, mod_all, gate, coef)))
+        late_first, _ = barrier((first, opening))
         second = lax.ppermute(late_first, "tm", [(i, i ^ 1) for i in range(tm_count)])
     w_mine, mod_all, opening, kept, gate, coef = barrier((w_mine, mod_all, opening, kept, gate, coef))
     if by_planes:

time: 87.2 us -> 86.8 us (level)
  local copies, waits for them, and re-layouts: 4.53 us -> 1.87 us
  Pallas kernels: 17 us -> 19.3 us
  starting transfers between devices: 32.5 us -> 30.2 us
  waiting for transfers between devices: 17.6 us -> 19.9 us
    unnamed x20 -> x16, local copies, waits for them, and re-layouts: 3.78 us -> 1.11 us
    ppermute x1, starting transfers between devices: 2.37 us -> 0.02 us  [per_device(): lax.ppermute(late_first, 'tm', [(i, i ^ 1) for i in range(tm_count)])]
    all_to_all x1, waiting for transfers between devices: 4.69 us -> 7.01 us  [per_device(): w_mine = lax.all_to_all(w_sent, 'seq', 0, 0, tiled=True)]
    pallas_call x1, Pallas kernels: 0.61 us -> 2.85 us  [cut(): pl.pallas_call(functools.partial(cut_kernel, n_sub, per, sub), out_shape=...]
  transfers between devices with their start and end apart: 17 -> 17, of which waited for: 8 -> 8; matrix products, arithmetic and copies ran while one was open for 2% -> 2% of each run, Pallas kernels for 10% -> 13%
where the time goes in v5:
time: 86.8 us; the launch traced here: 86.3 us
  starting transfers between devices  30.2 us (35%)
  waiting for transfers between devices  19.9 us (23%)
  Pallas kernels  19.3 us (22%)
  blocking collectives  12.8 us (15%)
  local copies, waits for them, and re-layouts  1.87 us (2%)
  other arithmetic  0.99 us (1%)
  between operations  0.92 us (1%)
    all_to_all x1, blocking collectives, per_device(): noise = lax.all_to_all(noise, ('tm', 'seq'), 0, 0, tiled=True)  12.8 us
    ppermute x3, starting transfers between devices, earlier_total(): lax.ppermute(total, 'tm', [(i, i + by) for i in range(count - by)])  10 us
    all_to_all x1, waiting for transfers between devices, per_device(): received = lax.all_to_all(sent, 'seq', 0, 0, tiled=True)  8.4 us
    all_to_all x1, waiting for transfers between devices, per_device(): w_mine = lax.all_to_all(w_sent, 'seq', 0, 0, tiled=True)  7.01 us
    pallas_call x1, Pallas kernels, finish(): pl.pallas_call(functools.partial(finish_kernel, tokd), out_shape=jax.Shap...  6.76 us
    ppermute x8, starting transfers between devices, swap(): return lax.ppermute(x, 'seq', [(i, i ^ mask) for i in range(count)])  4.99 us
    all_to_all x1, starting transfers between devices, per_device(): w_mine = lax.all_to_all(w_sent, 'seq', 0, 0, tiled=True)  4.47 us
    pallas_call x1, Pallas kernels, prepare(): pl.pallas_call(functools.partial(prepare_kernel, per, sub), out_shape=jax...  4.36 us
  transfers between devices with their start and end apart: 17, of which 8 were waited for; matrix products, arithmetic and copies ran while one was open for 2% of the time, Pallas kernels for 13%

profile of v5, /device:TPU:0, one launch (start us, length us, event | category | flops | bytes accessed | tf_op | source)
XLA Modules:
  0.0 86.3 jit_solution(4142911948382463056)
XLA Ops:
  0.6 3.0 %collective-permute-start.4 = (bf16[192,1536]{1,0:T(8,128)(2,1)}, bf16[192,1536]{1,0:T(8,128)(2,1)}, u32[]{:S(2)}, u32[]{:S(2)}) collective-permute-start(bf16[192,1536]{1,0:T(8,128)(2,1)} %refs_0_), channel_id=1, source_target_pairs={{0,2},{1,5},{2,0},{3,7},{4,6},{5,1},{6,4},{7,3},{8,12},{9,11},{10,... | collective-permute-start | bytes 1769480 | tf_op jit(solution)/shard_map/ppermute | solution.py:361
  3.6 2.9 %cut.1 = bf16[8,224,512]{2,1,0:T(8,128)(2,1)} custom-call(bf16[12,192,384]{2,1,0:T(8,128)(2,1)} %bitcast.18), custom_call_target="tpu_custom_call" | custom-call | tf_op jit(solution)/shard_map/cut/pallas_call | solution.py:96
  6.6 4.5 %all-to-all-start = ((bf16[8,224,512]{2,1,0:T(8,128)(2,1)}), bf16[8,224,512]{2,1,0:T(8,128)(2,1)}, u32[]{:S(2)}, u32[]{:S(2)}) async-start(bf16[8,224,512]{2,1,0:T(8,128)(2,1)} %cut.1), calls=%async_computation | async-start | bytes 3670016 | tf_op jit(solution)/shard_map/all_to_all | solution.py:407
  11.1 3.7 %collective-permute-start = (f32[48,64]{1,0:T(8,128)S(1)}, f32[48,64]{1,0:T(8,128)S(1)}, u32[]{:S(2)}, u32[]{:S(2)}) collective-permute-start(f32[48,64]{1,0:T(8,128)S(1)} %slice_bitcast_fusion), channel_id=1, source_target_pairs={{0,8},{8,16},{16,24},{1,9},{9,17},{17,25},{2,10},{10,18},{18,26},{... | collective-permute-start | bytes 36872 | tf_op jit(solution)/shard_map/ppermute | solution.py:413
  15.6 0.7 collective-permute-done
  16.3 6.2 %collective-permute-start.3 = (f32[48,64]{1,0:T(8,128)S(1)}, f32[48,64]{1,0:T(8,128)S(1)}, u32[]{:S(2)}, u32[]{:S(2)}) collective-permute-start(f32[48,64]{1,0:T(8,128)S(1)} %get-tuple-element.38), channel_id=1, source_target_pairs={{0,24},{1,25},{2,26},{3,27},{4,28},{5,29},{6,30},{7,31}} | collective-permute-start | bytes 36872 | tf_op jit(solution)/shard_map/ppermute | solution.py:368
  22.5 1.3 %collective-permute-start.2 = (f32[48,64]{1,0:T(8,128)S(1)}, f32[48,64]{1,0:T(8,128)S(1)}, u32[]{:S(2)}, u32[]{:S(2)}) collective-permute-start(f32[48,64]{1,0:T(8,128)S(1)} %get-tuple-element.38), channel_id=1, source_target_pairs={{0,16},{8,24},{1,17},{9,25},{2,18},{10,26},{3,19},{11,27},{4,20},{... | collective-permute-start | bytes 36872 | tf_op jit(solution)/shard_map/ppermute | solution.py:368
  23.8 2.5 %collective-permute-start.1 = (f32[48,64]{1,0:T(8,128)S(1)}, f32[48,64]{1,0:T(8,128)S(1)}, u32[]{:S(2)}, u32[]{:S(2)}) collective-permute-start(f32[48,64]{1,0:T(8,128)S(1)} %get-tuple-element.38), channel_id=1, source_target_pairs={{0,8},{8,16},{16,24},{1,9},{9,17},{17,25},{2,10},{10,18},{18,26},{... | collective-permute-start | bytes 36872 | tf_op jit(solution)/shard_map/ppermute | solution.py:368
  27.0 0.9 %collective-permute-done.1 = f32[48,64]{1,0:T(8,128)S(1)} collective-permute-done((f32[48,64]{1,0:T(8,128)S(1)}, f32[48,64]{1,0:T(8,128)S(1)}, u32[]{:S(2)}, u32[]{:S(2)}) %collective-permute-start.1) | collective-permute-done | bytes 12320 | tf_op jit(solution)/shard_map/ppermute | solution.py:368
  27.9 7.0 %all-to-all-done.w_ref = bf16[8,224,512]{2,1,0:T(8,128)(2,1)} async-done(((bf16[8,224,512]{2,1,0:T(8,128)(2,1)}), bf16[8,224,512]{2,1,0:T(8,128)(2,1)}, u32[]{:S(2)}, u32[]{:S(2)}) %all-to-all-start) | async-done | bytes 1835040 | tf_op jit(solution)/shard_map/all_to_all | solution.py:407
  35.4 4.4 %prepare.1 = bf16[8,80,384]{2,1,0:T(8,128)(2,1)} custom-call(bf16[64,1536]{1,0:T(8,128)(2,1)S(1)} %copy-done.1, f32[8,4608]{1,0:T(8,128)S(1)} %fusion.2.mod_ref, bf16[8,224,512]{2,1,0:T(8,128)(2,1)} %all-to-all-done.w_ref, f32[8,48,64]{2,1,0:T(8,128)S(1)} %copy-done.2, f32[48,64]{1,0:T(8,128)S(1)} %get-tuple-element.23.opening_ref), custom_call_target="tpu_custom_call" | custom-call | tf_op jit(solution)/shard_map/prepare/pallas_call | solution.py:174
  39.8 3.5 %all-to-all-start.1 = ((bf16[8,80,384]{2,1,0:T(8,128)(2,1)}), bf16[8,80,384]{2,1,0:T(8,128)(2,1)S(1)}, u32[]{:S(2)}, u32[]{:S(2)}) async-start(bf16[8,80,384]{2,1,0:T(8,128)(2,1)} %prepare.1), calls=%async_computation.1 | async-start | bytes 983040 | tf_op jit(solution)/shard_map/all_to_all | solution.py:431
  44.2 8.4 %all-to-all-done.1.pay_ref = bf16[8,80,384]{2,1,0:T(8,128)(2,1)S(1)} async-done(((bf16[8,80,384]{2,1,0:T(8,128)(2,1)}), bf16[8,80,384]{2,1,0:T(8,128)(2,1)S(1)}, u32[]{:S(2)}, u32[]{:S(2)}) %all-to-all-start.1) | async-done | bytes 491552 | tf_op jit(solution)/shard_map/all_to_all | solution.py:431
  52.7 4.0 %attend.1 = (bf16[384,1536]{1,0:T(8,128)(2,1)S(1)}, bf16[384,64]{1,0:T(8,128)(2,1)S(1)}) custom-call(s32[1]{0:T(128)} %constant.70.clone.1.part_ref, bf16[64,1536]{1,0:T(8,128)(2,1)S(1)} %copy-done.1, bf16[8,80,384]{2,1,0:T(8,128)(2,1)S(1)} %all-to-all-done.1.pay_ref), custom_call_target="tpu_custom_call" | custom-call | tf_op jit(solution)/shard_map/attend/pallas_call | solution.py:245
  56.7 1.1 %copy-done.3 = bf16[192,1536]{1,0:T(8,128)(2,1)S(1)} copy-done((bf16[192,1536]{1,0:T(8,128)(2,1)S(1)}, bf16[192,1536]{1,0:T(8,128)(2,1)}, u32[]{:S(2)}) %copy-start.3) | copy-done | bytes 589848
  57.8 6.8 %finish.1 = bf16[4,8,24,128]{3,2,1,0:T(8,128)(2,1)S(1)} custom-call(s32[8]{0:T(128)S(1)} %broadcast_xor_fusion.owner_ref, f32[1]{0:T(128)} %dynamic_slice.7.coef_ref, bf16[64,1536]{1,0:T(8,128)(2,1)S(1)} %copy-done.1, bf16[384,64]{1,0:T(8,128)(2,1)S(1)} %get-tuple-element.24.queries_ref, bf16[384,1536]{1,0:T(8,128)(2,1)S(1)} %get-tuple-element.25.att_ref, ...), custom_call_target="tpu_custom_call" | custom-call | tf_op jit(solution)/shard_map/finish/pallas_call | solution.py:299
  64.5 12.8 %all_to_all.15 = bf16[32,24,128]{2,1,0:T(8,128)(2,1)S(1)} all-to-all(bf16[32,24,128]{2,1,0:T(8,128)(2,1)S(1)} %bitcast.14), channel_id=1, replica_groups=mesh['tm'=4,'seq'=8] {'tm','seq'}, dimensions={0} | all-to-all | bytes 393216 | tf_op jit(solution)/shard_map/all_to_all | solution.py:459
  77.3 1.3 %advance.1 = (f32[8,48,64]{2,1,0:T(8,128)}, f32[8,64]{1,0:T(8,128)S(1)}) custom-call(s32[1]{0:T(128)} %bitcast.place_ref, f32[8]{0:T(128)S(1)} %broadcast_add_fusion.keep_ref, bf16[4,8,24,128]{3,2,1,0:T(8,128)(2,1)S(1)} %bitcast.15, f32[8,48,64]{2,1,0:T(8,128)S(1)} %copy-done.2, f32[48,64]{1,0:T(8,128)S(1)} %get-tuple-element.23.opening_ref, ...), custom_call_target="tpu_custom_call" | custom-call | tf_op jit(solution)/shard_map/advance/pallas_call | solution.py:340
  79.3 0.8 collective-permute-done.11
  80.1 1.2 %collective-permute-start.14 = (f32[8,64]{1,0:T(8,128)S(1)}, f32[8,64]{1,0:T(8,128)S(1)}, u32[]{:S(2)}, u32[]{:S(2)}) collective-permute-start(f32[8,64]{1,0:T(8,128)S(1)} %add.58), channel_id=1, source_target_pairs={{0,6},{1,7},{2,4},{3,5},{4,2},{5,3},{6,0},{7,1},{8,14},{9,15},{10,... | collective-permute-start | bytes 6152 | tf_op jit(solution)/shard_map/ppermute | solution.py:353
  81.3 0.8 collective-permute-start.13
  82.1 1.5 %collective-permute-start.12 = (f32[8,64]{1,0:T(8,128)S(1)}, f32[8,64]{1,0:T(8,128)S(1)}, u32[]{:S(2)}, u32[]{:S(2)}) collective-permute-start(f32[8,64]{1,0:T(8,128)S(1)} %add.58), channel_id=1, source_target_pairs={{0,2},{1,3},{2,0},{3,1},{4,6},{5,7},{6,4},{7,5},{8,10},{9,11},{10,... | collective-permute-start | bytes 6152 | tf_op jit(solution)/shard_map/ppermute | solution.py:353
  83.6 1.0 %collective-permute-done.14 = f32[8,64]{1,0:T(8,128)S(1)} collective-permute-done((f32[8,64]{1,0:T(8,128)S(1)}, f32[8,64]{1,0:T(8,128)S(1)}, u32[]{:S(2)}, u32[]{:S(2)}) %collective-permute-start.14) | collective-permute-done | bytes 2080 | tf_op jit(solution)/shard_map/ppermute | solution.py:353
  84.9 0.8 collective-permute-done.12
  (50 shorter events, 4.6 us)
Async XLA Ops:
  0.6 14.3 %copy-start = (bf16[256,4608]{1,0:T(8,128)(2,1)S(1)}, bf16[256,4608]{1,0:T(8,128)(2,1)}, u32[]{:S(2)}) copy-start(bf16[256,4608]{1,0:T(8,128)(2,1)} %param.14) | copy-start | bytes 7077892
  0.6 26.3 %collective-permute-start.4 = (bf16[192,1536]{1,0:T(8,128)(2,1)}, bf16[192,1536]{1,0:T(8,128)(2,1)}, u32[]{:S(2)}, u32[]{:S(2)}) collective-permute-start(bf16[192,1536]{1,0:T(8,128)(2,1)} %refs_0_), channel_id=1, source_target_pairs={{0,2},{1,5},{2,0},{3,7},{4,6},{5,1},{6,4},{7,3},{8,12},{9,11},{10,... | collective-permute-start | bytes 1769480 | tf_op jit(solution)/shard_map/ppermute | solution.py:361
  6.5 4.5 %copy-start.2 = (f32[8,48,64]{2,1,0:T(8,128)S(1)}, f32[8,48,64]{2,1,0:T(8,128)}, u32[]{:S(2)}) copy-start(f32[8,48,64]{2,1,0:T(8,128)} %states_ref.3) | copy-start | bytes 294916
  6.5 8.2 %copy-start.7 = (s32[8]{0:T(128)S(1)}, s32[8]{0:T(128)}, u32[]{:S(2)}) copy-start(s32[8]{0:T(128)} %param.11) | copy-start | bytes 100
  6.5 8.2 %copy-start.6 = (s32[8]{0:T(128)S(1)}, s32[8]{0:T(128)}, u32[]{:S(2)}) copy-start(s32[8]{0:T(128)} %param.12) | copy-start | bytes 100
  6.5 9.7 %copy-start.5 = (f32[48,64]{1,0:T(8,128)S(1)}, f32[48,64]{1,0:T(8,128)}, u32[]{:S(2)}) copy-start(f32[48,64]{1,0:T(8,128)} %first_ref.1) | copy-start | bytes 36868
  6.6 28.3 %all-to-all-start = ((bf16[8,224,512]{2,1,0:T(8,128)(2,1)}), bf16[8,224,512]{2,1,0:T(8,128)(2,1)}, u32[]{:S(2)}, u32[]{:S(2)}) async-start(bf16[8,224,512]{2,1,0:T(8,128)(2,1)} %cut.1), calls=%async_computation | async-start | bytes 3670016 | tf_op jit(solution)/shard_map/all_to_all | solution.py:407
  11.0 24.4 %copy-start.1 = (bf16[64,1536]{1,0:T(8,128)(2,1)S(1)}, bf16[64,1536]{1,0:T(8,128)(2,1)}, u32[]{:S(2)}) copy-start(bf16[64,1536]{1,0:T(8,128)(2,1)} %embed_ref.5) | copy-start | bytes 589828
  11.1 5.2 %collective-permute-start = (f32[48,64]{1,0:T(8,128)S(1)}, f32[48,64]{1,0:T(8,128)S(1)}, u32[]{:S(2)}, u32[]{:S(2)}) collective-permute-start(f32[48,64]{1,0:T(8,128)S(1)} %slice_bitcast_fusion), channel_id=1, source_target_pairs={{0,8},{8,16},{16,24},{1,9},{9,17},{17,25},{2,10},{10,18},{18,26},{... | collective-permute-start | bytes 36872 | tf_op jit(solution)/shard_map/ppermute | solution.py:413
  16.3 10.7 %collective-permute-start.3 = (f32[48,64]{1,0:T(8,128)S(1)}, f32[48,64]{1,0:T(8,128)S(1)}, u32[]{:S(2)}, u32[]{:S(2)}) collective-permute-start(f32[48,64]{1,0:T(8,128)S(1)} %get-tuple-element.38), channel_id=1, source_target_pairs={{0,24},{1,25},{2,26},{3,27},{4,28},{5,29},{6,30},{7,31}} | collective-permute-start | bytes 36872 | tf_op jit(solution)/shard_map/ppermute | solution.py:368
  22.5 4.4 %collective-permute-start.2 = (f32[48,64]{1,0:T(8,128)S(1)}, f32[48,64]{1,0:T(8,128)S(1)}, u32[]{:S(2)}, u32[]{:S(2)}) collective-permute-start(f32[48,64]{1,0:T(8,128)S(1)} %get-tuple-element.38), channel_id=1, source_target_pairs={{0,16},{8,24},{1,17},{9,25},{2,18},{10,26},{3,19},{11,27},{4,20},{... | collective-permute-start | bytes 36872 | tf_op jit(solution)/shard_map/ppermute | solution.py:368
  23.8 4.0 %collective-permute-start.1 = (f32[48,64]{1,0:T(8,128)S(1)}, f32[48,64]{1,0:T(8,128)S(1)}, u32[]{:S(2)}, u32[]{:S(2)}) collective-permute-start(f32[48,64]{1,0:T(8,128)S(1)} %get-tuple-element.38), channel_id=1, source_target_pairs={{0,8},{8,16},{16,24},{1,9},{9,17},{17,25},{2,10},{10,18},{18,26},{... | collective-permute-start | bytes 36872 | tf_op jit(solution)/shard_map/ppermute | solution.py:368
  26.3 30.4 %copy-start.4 = (bf16[1536,64]{0,1:T(8,128)(2,1)S(1)}, bf16[1536,64]{0,1:T(8,128)(2,1)}, u32[]{:S(2)}) copy-start(bf16[1536,64]{0,1:T(8,128)(2,1)} %param.17) | copy-start | bytes 589828
  26.9 16.3 %collective-permute-start.5 = (bf16[192,1536]{1,0:T(8,128)(2,1)}, bf16[192,1536]{1,0:T(8,128)(2,1)}, u32[]{:S(2)}, u32[]{:S(2)}) collective-permute-start(bf16[192,1536]{1,0:T(8,128)(2,1)} %collective-permute-done.4.refs_2_), channel_id=1, source_target_pairs={{0,8},{8,0},{16,24},{24,16},{1,9},{9,1},{17,25},{25,17},{2,10},{10... | collective-permute-start | bytes 1769480 | tf_op jit(solution)/shard_map/ppermute | solution.py:423
  34.9 17.7 %collective-permute-start.9 = (bf16[192,1536]{1,0:T(8,128)(2,1)}, bf16[192,1536]{1,0:T(8,128)(2,1)}, u32[]{:S(2)}, u32[]{:S(2)}) collective-permute-start(bf16[192,1536]{1,0:T(8,128)(2,1)} %collective-permute-done.4.refs_2_), channel_id=1, source_target_pairs={{0,4},{1,3},{2,6},{3,1},{4,0},{5,7},{6,2},{7,5},{8,10},{9,13},{10,... | collective-permute-start | bytes 1769480 | tf_op jit(solution)/shard_map/ppermute | solution.py:361
  39.8 12.8 %all-to-all-start.1 = ((bf16[8,80,384]{2,1,0:T(8,128)(2,1)}), bf16[8,80,384]{2,1,0:T(8,128)(2,1)S(1)}, u32[]{:S(2)}, u32[]{:S(2)}) async-start(bf16[8,80,384]{2,1,0:T(8,128)(2,1)} %prepare.1), calls=%async_computation.1 | async-start | bytes 983040 | tf_op jit(solution)/shard_map/all_to_all | solution.py:431
  43.3 13.4 %collective-permute-start.6 = (bf16[192,1536]{1,0:T(8,128)(2,1)}, bf16[192,1536]{1,0:T(8,128)(2,1)}, u32[]{:S(2)}, u32[]{:S(2)}) collective-permute-start(bf16[192,1536]{1,0:T(8,128)(2,1)} %refs_0_), channel_id=1, source_target_pairs={{0,1},{1,0},{2,3},{3,2},{4,5},{5,4},{6,7},{7,6},{8,9},{9,8},{10,11... | collective-permute-start | bytes 1769480 | tf_op jit(solution)/shard_map/ppermute | solution.py:353
  43.7 13.0 %collective-permute-start.7 = (bf16[192,1536]{1,0:T(8,128)(2,1)}, bf16[192,1536]{1,0:T(8,128)(2,1)}, u32[]{:S(2)}, u32[]{:S(2)}) collective-permute-start(bf16[192,1536]{1,0:T(8,128)(2,1)} %collective-permute-done.4.refs_2_), channel_id=1, source_target_pairs={{0,1},{1,0},{2,3},{3,2},{4,5},{5,4},{6,7},{7,6},{8,9},{9,8},{10,11... | collective-permute-start | bytes 1769480 | tf_op jit(solution)/shard_map/ppermute | solution.py:353
  43.9 12.8 %collective-permute-start.8 = (bf16[192,1536]{1,0:T(8,128)(2,1)}, bf16[192,1536]{1,0:T(8,128)(2,1)}, u32[]{:S(2)}, u32[]{:S(2)}) collective-permute-start(bf16[192,1536]{1,0:T(8,128)(2,1)} %collective-permute-done.5.refs_4_), channel_id=1, source_target_pairs={{0,1},{1,0},{2,3},{3,2},{4,5},{5,4},{6,7},{7,6},{8,9},{9,8},{10,11... | collective-permute-start | bytes 1769480 | tf_op jit(solution)/shard_map/ppermute | solution.py:353
  52.6 4.1 %collective-permute-start.10 = (bf16[192,1536]{1,0:T(8,128)(2,1)}, bf16[192,1536]{1,0:T(8,128)(2,1)}, u32[]{:S(2)}, u32[]{:S(2)}) collective-permute-start(bf16[192,1536]{1,0:T(8,128)(2,1)} %collective-permute-done.9.refs_6_), channel_id=1, source_target_pairs={{0,1},{1,0},{2,3},{3,2},{4,5},{5,4},{6,7},{7,6},{8,9},{9,8},{10,11... | collective-permute-start | bytes 1769480 | tf_op jit(solution)/shard_map/ppermute | solution.py:353
  78.7 1.4 %collective-permute-start.11 = (f32[8,64]{1,0:T(8,128)S(1)}, f32[8,64]{1,0:T(8,128)S(1)}, u32[]{:S(2)}, u32[]{:S(2)}) collective-permute-start(f32[8,64]{1,0:T(8,128)S(1)} %get-tuple-element.35), channel_id=1, source_target_pairs={{0,1},{1,0},{2,3},{3,2},{4,5},{5,4},{6,7},{7,6},{8,9},{9,8},{10,11... | collective-permute-start | bytes 6152 | tf_op jit(solution)/shard_map/ppermute | solution.py:353
  80.1 4.5 %collective-permute-start.14 = (f32[8,64]{1,0:T(8,128)S(1)}, f32[8,64]{1,0:T(8,128)S(1)}, u32[]{:S(2)}, u32[]{:S(2)}) collective-permute-start(f32[8,64]{1,0:T(8,128)S(1)} %add.58), channel_id=1, source_target_pairs={{0,6},{1,7},{2,4},{3,5},{4,2},{5,3},{6,0},{7,1},{8,14},{9,15},{10,... | collective-permute-start | bytes 6152 | tf_op jit(solution)/shard_map/ppermute | solution.py:353
  81.3 3.6 %collective-permute-start.13 = (f32[8,64]{1,0:T(8,128)S(1)}, f32[8,64]{1,0:T(8,128)S(1)}, u32[]{:S(2)}, u32[]{:S(2)}) collective-permute-start(f32[8,64]{1,0:T(8,128)S(1)} %add.58), channel_id=1, source_target_pairs={{0,4},{1,5},{2,6},{3,7},{4,0},{5,1},{6,2},{7,3},{8,12},{9,13},{10,... | collective-permute-start | bytes 6152 | tf_op jit(solution)/shard_map/ppermute | solution.py:353
  82.1 3.6 %collective-permute-start.12 = (f32[8,64]{1,0:T(8,128)S(1)}, f32[8,64]{1,0:T(8,128)S(1)}, u32[]{:S(2)}, u32[]{:S(2)}) collective-permute-start(f32[8,64]{1,0:T(8,128)S(1)} %add.58), channel_id=1, source_target_pairs={{0,2},{1,3},{2,0},{3,1},{4,6},{5,7},{6,4},{7,5},{8,10},{9,11},{10,... | collective-permute-start | bytes 6152 | tf_op jit(solution)/shard_map/ppermute | solution.py:353
  (1 other events, 1.1 us)

commit v6 on v5

--- a/solution.py
+++ b/solution.py
@@ -104,7 +104,7 @@
             pltpu.SemaphoreType.DMA((w.shape[0],)),
             pltpu.SemaphoreType.DMA((count,)),
         ],
-        compiler_params=params(56),
+        compiler_params=params(62),
         name="cut",
     )(w)
 

time: 86.8 us -> 86 us (level)
  waiting for transfers between devices: 19.9 us -> 15.1 us
  starting transfers between devices: 30.2 us -> 26.5 us
  local copies, waits for them, and re-layouts: 1.87 us -> 5.54 us
  other arithmetic: 0.99 us -> 4.65 us
  matrix products: 0.41 us -> 2.07 us
  Pallas kernels: 19.3 us -> 17.8 us
    all_to_all x1, waiting for transfers between devices: 7.01 us -> 3.35 us  [per_device(): w_mine = lax.all_to_all(w_sent, 'seq', 0, 0, tiled=True)]
    ppermute x1, waiting for transfers between devices: 0.01 us -> 3.01 us  [per_device(): lax.ppermute(late_first, 'tm', [(i, i ^ 1) for i in range(tm_count)])]
    ppermute x3, starting transfers between devices: 10 us -> 7.05 us  [earlier_total(): lax.ppermute(total, 'tm', [(i, i + by) for i in range(count - by)])]
    all_to_all x1, waiting for transfers between devices: 8.4 us -> 5.8 us  [per_device(): received = lax.all_to_all(sent, 'seq', 0, 0, tiled=True)]
    add x1, other arithmetic: 0.04 us -> 1.93 us  [per_device(): keep_coef[0] * opening]
    unnamed x16 -> x26, local copies, waits for them, and re-layouts: 1.11 us -> 2.92 us
    dot_general x1, matrix products: 0.41 us -> 2.07 us  [modulation(): return jnp.dot(time_embed, mod_weight, preferred_element_type=F32)]
    pallas_call x1, Pallas kernels: 4.36 us -> 2.83 us  [prepare(): pl.pallas_call(functools.partial(prepare_kernel, per, sub), out_shape=jax...]
  transfers between devices with their start and end apart: 17 -> 17, of which waited for: 8 -> 7; matrix products, arithmetic and copies ran while one was open for 2% -> 10% of each run, Pallas kernels for 13% -> 11%
where the time goes in v6:
time: 86 us; the launch traced here: 85.3 us
  starting transfers between devices  26.5 us (31%)
  Pallas kernels  17.8 us (21%)
  waiting for transfers between devices  15.1 us (18%)
  blocking collectives  12.8 us (15%)
  local copies, waits for them, and re-layouts  5.54 us (6%)
  other arithmetic  4.65 us (5%)
  matrix products  2.07 us (2%)
    all_to_all x1, blocking collectives, per_device(): noise = lax.all_to_all(noise, ('tm', 'seq'), 0, 0, tiled=True)  12.8 us
    ppermute x3, starting transfers between devices, earlier_total(): lax.ppermute(total, 'tm', [(i, i + by) for i in range(count - by)])  7.05 us
    pallas_call x1, Pallas kernels, finish(): pl.pallas_call(functools.partial(finish_kernel, tokd), out_shape=jax.Shap...  6.77 us
    all_to_all x1, waiting for transfers between devices, per_device(): received = lax.all_to_all(sent, 'seq', 0, 0, tiled=True)  5.8 us
    ppermute x8, starting transfers between devices, swap(): return lax.ppermute(x, 'seq', [(i, i ^ mask) for i in range(count)])  4.6 us
    ppermute x1, starting transfers between devices, per_device(): lax.ppermute(late_states[-1], 'tm', [(i, i + 1) for i in range(tm_count -...  4.12 us
    pallas_call x1, Pallas kernels, attend(): pl.pallas_call(functools.partial(attend_kernel, heads, n_sub, per, sub, t...  3.96 us
    all_to_all x1, starting transfers between devices, per_device(): w_mine = lax.all_to_all(w_sent, 'seq', 0, 0, tiled=True)  3.74 us
  transfers between devices with their start and end apart: 17, of which 7 were waited for; matrix products, arithmetic and copies ran while one was open for 10% of the time, Pallas kernels for 11%

profile of v6, /device:TPU:0, one launch (start us, length us, event | category | flops | bytes accessed | tf_op | source)
XLA Modules:
  0.0 85.3 jit_solution(2989708900396336902)
XLA Ops:
  0.6 3.0 %collective-permute-start.4 = (bf16[192,1536]{1,0:T(8,128)(2,1)}, bf16[192,1536]{1,0:T(8,128)(2,1)S(1)}, u32[]{:S(2)}, u32[]{:S(2)}) collective-permute-start(bf16[192,1536]{1,0:T(8,128)(2,1)} %refs_0_), channel_id=1, source_target_pairs={{0,2},{1,5},{2,0},{3,7},{4,6},{5,1},{6,4},{7,3},{8,12},{9,11},{10,... | collective-permute-start | bytes 1769480 | tf_op jit(solution)/shard_map/ppermute | solution.py:361
  3.6 2.9 %cut.1 = bf16[8,224,512]{2,1,0:T(8,128)(2,1)} custom-call(bf16[12,192,384]{2,1,0:T(8,128)(2,1)} %bitcast.18), custom_call_target="tpu_custom_call" | custom-call | tf_op jit(solution)/shard_map/cut/pallas_call | solution.py:96
  6.5 3.7 %all-to-all-start = ((bf16[8,224,512]{2,1,0:T(8,128)(2,1)}), bf16[8,224,512]{2,1,0:T(8,128)(2,1)S(1)}, u32[]{:S(2)}, u32[]{:S(2)}) async-start(bf16[8,224,512]{2,1,0:T(8,128)(2,1)} %cut.1), calls=%async_computation | async-start | bytes 3670016 | tf_op jit(solution)/shard_map/all_to_all | solution.py:407
  10.9 4.1 %collective-permute-start = (f32[48,64]{1,0:T(8,128)}, f32[48,64]{1,0:T(8,128)}, u32[]{:S(2)}, u32[]{:S(2)}) collective-permute-start(f32[48,64]{1,0:T(8,128)} %slice_bitcast_fusion), channel_id=1, source_target_pairs={{0,8},{8,16},{16,24},{1,9},{9,17},{17,25},{2,10},{10,18},{18,26},{... | collective-permute-start | bytes 36872 | tf_op jit(solution)/shard_map/ppermute | solution.py:413
  15.8 2.1 %fusion.2.mod_ref = f32[8,4608]{1,0:T(8,128)S(1)} fusion(bf16[256,4608]{1,0:T(8,128)(2,1)} %param.14, bf16[8,128]{1,0:T(8,128)(2,1)S(1)} %get-tuple-element.41, bf16[8,128]{1,0:T(8,128)(2,1)S(1)} %get-tuple-element.40), kind=kOutput, calls=%fused_computation.9 | convolution fusion | flops 18882560 | bytes 2510848 | tf_op jit(solution)/shard_map/dot_general | solution.py:40
  19.2 1.9 %multiply_add_fusion = (f32[48,64]{1,0:T(8,128)S(1)}, f32[48,64]{1,0:T(8,128)}) fusion(f32[48,64]{1,0:T(8,128)} %multiply_reduce_fusion, f32[]{:T(128)} %bitcast.17, f32[48,64]{1,0:T(8,128)} %first_ref.1, f32[48,64]{1,0:T(8,128)} %collective-permute-done, pred[]{:T(512)S(6)} %eq.10), kind=kLoop, calls=%fused_computation.2 | loop fusion | flops 9216 | bytes 61445 | tf_op jit(solution)/shard_map/add | solution.py:416
  21.1 3.3 %collective-permute-start.3 = (f32[48,64]{1,0:T(8,128)S(1)}, f32[48,64]{1,0:T(8,128)S(1)}, u32[]{:S(2)}, u32[]{:S(2)}) collective-permute-start(f32[48,64]{1,0:T(8,128)S(1)} %get-tuple-element.38), channel_id=1, source_target_pairs={{0,24},{1,25},{2,26},{3,27},{4,28},{5,29},{6,30},{7,31}} | collective-permute-start | bytes 36872 | tf_op jit(solution)/shard_map/ppermute | solution.py:368
  24.4 1.3 %collective-permute-start.2 = (f32[48,64]{1,0:T(8,128)S(1)}, f32[48,64]{1,0:T(8,128)S(1)}, u32[]{:S(2)}, u32[]{:S(2)}) collective-permute-start(f32[48,64]{1,0:T(8,128)S(1)} %get-tuple-element.38), channel_id=1, source_target_pairs={{0,16},{8,24},{1,17},{9,25},{2,18},{10,26},{3,19},{11,27},{4,20},{... | collective-permute-start | bytes 36872 | tf_op jit(solution)/shard_map/ppermute | solution.py:368
  25.7 2.5 %collective-permute-start.1 = (f32[48,64]{1,0:T(8,128)S(1)}, f32[48,64]{1,0:T(8,128)S(1)}, u32[]{:S(2)}, u32[]{:S(2)}) collective-permute-start(f32[48,64]{1,0:T(8,128)S(1)} %get-tuple-element.38), channel_id=1, source_target_pairs={{0,8},{8,16},{16,24},{1,9},{9,17},{17,25},{2,10},{10,18},{18,26},{... | collective-permute-start | bytes 36872 | tf_op jit(solution)/shard_map/ppermute | solution.py:368
  28.8 1.3 %dynamic_slice.7.coef_ref = f32[1]{0:T(128)} dynamic-slice(f32[8]{0:T(128)} %get-tuple-element.36, s32[]{:T(128)S(6)} %select_n.31), dynamic_slice_sizes={1} | dynamic-slice | bytes 12 | tf_op jit(solution)/shard_map/dynamic_slice | solution.py:420
  30.7 3.4 %all-to-all-done.w_ref = bf16[8,224,512]{2,1,0:T(8,128)(2,1)S(1)} async-done(((bf16[8,224,512]{2,1,0:T(8,128)(2,1)}), bf16[8,224,512]{2,1,0:T(8,128)(2,1)S(1)}, u32[]{:S(2)}, u32[]{:S(2)}) %all-to-all-start) | async-done | bytes 1835040 | tf_op jit(solution)/shard_map/all_to_all | solution.py:407
  35.3 2.8 %prepare.1 = bf16[8,80,384]{2,1,0:T(8,128)(2,1)} custom-call(bf16[64,1536]{1,0:T(8,128)(2,1)S(1)} %copy-done, f32[8,4608]{1,0:T(8,128)S(1)} %fusion.2.mod_ref, bf16[8,224,512]{2,1,0:T(8,128)(2,1)S(1)} %all-to-all-done.w_ref, f32[8,48,64]{2,1,0:T(8,128)S(1)} %copy-done.1, f32[48,64]{1,0:T(8,128)S(1)} %copy-done.3), custom_call_target="tpu_custom_call" | custom-call | tf_op jit(solution)/shard_map/prepare/pallas_call | solution.py:174
  38.2 3.5 %all-to-all-start.1 = ((bf16[8,80,384]{2,1,0:T(8,128)(2,1)}), bf16[8,80,384]{2,1,0:T(8,128)(2,1)S(1)}, u32[]{:S(2)}, u32[]{:S(2)}) async-start(bf16[8,80,384]{2,1,0:T(8,128)(2,1)} %prepare.1), calls=%async_computation.1 | async-start | bytes 983040 | tf_op jit(solution)/shard_map/all_to_all | solution.py:431
  41.6 3.0 %collective-permute-done.5.refs_4_ = bf16[192,1536]{1,0:T(8,128)(2,1)} collective-permute-done((bf16[192,1536]{1,0:T(8,128)(2,1)S(1)}, bf16[192,1536]{1,0:T(8,128)(2,1)}, u32[]{:S(2)}, u32[]{:S(2)}) %collective-permute-start.5) | collective-permute-done | bytes 589856 | tf_op jit(solution)/shard_map/ppermute | solution.py:423
  45.2 5.8 %all-to-all-done.1.pay_ref = bf16[8,80,384]{2,1,0:T(8,128)(2,1)S(1)} async-done(((bf16[8,80,384]{2,1,0:T(8,128)(2,1)}), bf16[8,80,384]{2,1,0:T(8,128)(2,1)S(1)}, u32[]{:S(2)}, u32[]{:S(2)}) %all-to-all-start.1) | async-done | bytes 491552 | tf_op jit(solution)/shard_map/all_to_all | solution.py:431
  51.1 4.0 %attend.1 = (bf16[384,1536]{1,0:T(8,128)(2,1)S(1)}, bf16[384,64]{1,0:T(8,128)(2,1)S(1)}) custom-call(s32[1]{0:T(128)} %constant.70.clone.1.part_ref, bf16[64,1536]{1,0:T(8,128)(2,1)S(1)} %copy-done, bf16[8,80,384]{2,1,0:T(8,128)(2,1)S(1)} %all-to-all-done.1.pay_ref), custom_call_target="tpu_custom_call" | custom-call | tf_op jit(solution)/shard_map/attend/pallas_call | solution.py:245
  55.1 0.9 %copy-done.5 = bf16[1536,64]{0,1:T(8,128)(2,1)S(1)} copy-done((bf16[1536,64]{0,1:T(8,128)(2,1)S(1)}, bf16[1536,64]{0,1:T(8,128)(2,1)}, u32[]{:S(2)}) %copy-start.5) | copy-done | bytes 196632
  56.7 6.8 %finish.1 = bf16[4,8,24,128]{3,2,1,0:T(8,128)(2,1)S(1)} custom-call(s32[8]{0:T(128)S(1)} %broadcast_xor_fusion.owner_ref, f32[1]{0:T(128)} %dynamic_slice.7.coef_ref, bf16[64,1536]{1,0:T(8,128)(2,1)S(1)} %copy-done, bf16[384,64]{1,0:T(8,128)(2,1)S(1)} %get-tuple-element.24.queries_ref, bf16[384,1536]{1,0:T(8,128)(2,1)S(1)} %get-tuple-element.25.att_ref, ...), custom_call_target="tpu_custom_call" | custom-call | tf_op jit(solution)/shard_map/finish/pallas_call | solution.py:299
  63.5 12.8 %all_to_all.15 = bf16[32,24,128]{2,1,0:T(8,128)(2,1)S(1)} all-to-all(bf16[32,24,128]{2,1,0:T(8,128)(2,1)S(1)} %bitcast.14), channel_id=1, replica_groups=mesh['tm'=4,'seq'=8] {'tm','seq'}, dimensions={0} | all-to-all | bytes 393216 | tf_op jit(solution)/shard_map/all_to_all | solution.py:459
  76.3 1.3 %advance.1 = (f32[8,48,64]{2,1,0:T(8,128)}, f32[8,64]{1,0:T(8,128)S(1)}) custom-call(s32[1]{0:T(128)} %bitcast.place_ref, f32[8]{0:T(128)S(1)} %copy-done.10, bf16[4,8,24,128]{3,2,1,0:T(8,128)(2,1)S(1)} %bitcast.15, f32[8,48,64]{2,1,0:T(8,128)S(1)} %copy-done.1, f32[48,64]{1,0:T(8,128)S(1)} %copy-done.4, f32[48,64]{1,0:T(8,128)S(1)} %copy-done.7, ...), custom_call_target="tpu_custom_call" | custom-call | tf_op jit(solution)/shard_map/advance/pallas_call | solution.py:340
  78.2 0.8 collective-permute-done.11
  79.0 1.2 %collective-permute-start.14 = (f32[8,64]{1,0:T(8,128)S(1)}, f32[8,64]{1,0:T(8,128)S(1)}, u32[]{:S(2)}, u32[]{:S(2)}) collective-permute-start(f32[8,64]{1,0:T(8,128)S(1)} %add.58), channel_id=1, source_target_pairs={{0,6},{1,7},{2,4},{3,5},{4,2},{5,3},{6,0},{7,1},{8,14},{9,15},{10,... | collective-permute-start | bytes 6152 | tf_op jit(solution)/shard_map/ppermute | solution.py:353
  81.0 1.5 %collective-permute-start.12 = (f32[8,64]{1,0:T(8,128)S(1)}, f32[8,64]{1,0:T(8,128)S(1)}, u32[]{:S(2)}, u32[]{:S(2)}) collective-permute-start(f32[8,64]{1,0:T(8,128)S(1)} %add.58), channel_id=1, source_target_pairs={{0,2},{1,3},{2,0},{3,1},{4,6},{5,7},{6,4},{7,5},{8,10},{9,11},{10,... | collective-permute-start | bytes 6152 | tf_op jit(solution)/shard_map/ppermute | solution.py:353
  82.5 1.0 %collective-permute-done.14 = f32[8,64]{1,0:T(8,128)S(1)} collective-permute-done((f32[8,64]{1,0:T(8,128)S(1)}, f32[8,64]{1,0:T(8,128)S(1)}, u32[]{:S(2)}, u32[]{:S(2)}) %collective-permute-start.14) | collective-permute-done | bytes 2080 | tf_op jit(solution)/shard_map/ppermute | solution.py:353
  (60 shorter events, 9.7 us)
Async XLA Ops:
  0.6 29.4 %collective-permute-start.4 = (bf16[192,1536]{1,0:T(8,128)(2,1)}, bf16[192,1536]{1,0:T(8,128)(2,1)S(1)}, u32[]{:S(2)}, u32[]{:S(2)}) collective-permute-start(bf16[192,1536]{1,0:T(8,128)(2,1)} %refs_0_), channel_id=1, source_target_pairs={{0,2},{1,5},{2,0},{3,7},{4,6},{5,1},{6,4},{7,3},{8,12},{9,11},{10,... | collective-permute-start | bytes 1769480 | tf_op jit(solution)/shard_map/ppermute | solution.py:361
  6.5 8.5 %copy-start.12 = (s32[8]{0:T(128)S(1)}, s32[8]{0:T(128)}, u32[]{:S(2)}) copy-start(s32[8]{0:T(128)} %param.11) | copy-start | bytes 100
  6.5 27.5 %all-to-all-start = ((bf16[8,224,512]{2,1,0:T(8,128)(2,1)}), bf16[8,224,512]{2,1,0:T(8,128)(2,1)S(1)}, u32[]{:S(2)}, u32[]{:S(2)}) async-start(bf16[8,224,512]{2,1,0:T(8,128)(2,1)} %cut.1), calls=%async_computation | async-start | bytes 3670016 | tf_op jit(solution)/shard_map/all_to_all | solution.py:407
  10.3 24.3 %copy-start = (bf16[64,1536]{1,0:T(8,128)(2,1)S(1)}, bf16[64,1536]{1,0:T(8,128)(2,1)}, u32[]{:S(2)}) copy-start(bf16[64,1536]{1,0:T(8,128)(2,1)} %embed_ref.5) | copy-start | bytes 589828
  10.9 8.3 %collective-permute-start = (f32[48,64]{1,0:T(8,128)}, f32[48,64]{1,0:T(8,128)}, u32[]{:S(2)}, u32[]{:S(2)}) collective-permute-start(f32[48,64]{1,0:T(8,128)} %slice_bitcast_fusion), channel_id=1, source_target_pairs={{0,8},{8,16},{16,24},{1,9},{9,17},{17,25},{2,10},{10,18},{18,26},{... | collective-permute-start | bytes 36872 | tf_op jit(solution)/shard_map/ppermute | solution.py:413
  17.9 26.8 %copy-start.2 = (bf16[192,1536]{1,0:T(8,128)(2,1)S(1)}, bf16[192,1536]{1,0:T(8,128)(2,1)}, u32[]{:S(2)}) copy-start(bf16[192,1536]{1,0:T(8,128)(2,1)} %refs_0_) | copy-start | bytes 1769476
  21.1 9.0 %collective-permute-start.3 = (f32[48,64]{1,0:T(8,128)S(1)}, f32[48,64]{1,0:T(8,128)S(1)}, u32[]{:S(2)}, u32[]{:S(2)}) collective-permute-start(f32[48,64]{1,0:T(8,128)S(1)} %get-tuple-element.38), channel_id=1, source_target_pairs={{0,24},{1,25},{2,26},{3,27},{4,28},{5,29},{6,30},{7,31}} | collective-permute-start | bytes 36872 | tf_op jit(solution)/shard_map/ppermute | solution.py:368
  24.4 5.7 %collective-permute-start.2 = (f32[48,64]{1,0:T(8,128)S(1)}, f32[48,64]{1,0:T(8,128)S(1)}, u32[]{:S(2)}, u32[]{:S(2)}) collective-permute-start(f32[48,64]{1,0:T(8,128)S(1)} %get-tuple-element.38), channel_id=1, source_target_pairs={{0,16},{8,24},{1,17},{9,25},{2,18},{10,26},{3,19},{11,27},{4,20},{... | collective-permute-start | bytes 36872 | tf_op jit(solution)/shard_map/ppermute | solution.py:368
  25.7 4.4 %collective-permute-start.1 = (f32[48,64]{1,0:T(8,128)S(1)}, f32[48,64]{1,0:T(8,128)S(1)}, u32[]{:S(2)}, u32[]{:S(2)}) collective-permute-start(f32[48,64]{1,0:T(8,128)S(1)} %get-tuple-element.38), channel_id=1, source_target_pairs={{0,8},{8,16},{16,24},{1,9},{9,17},{17,25},{2,10},{10,18},{18,26},{... | collective-permute-start | bytes 36872 | tf_op jit(solution)/shard_map/ppermute | solution.py:368
  30.1 14.6 %collective-permute-start.5 = (bf16[192,1536]{1,0:T(8,128)(2,1)S(1)}, bf16[192,1536]{1,0:T(8,128)(2,1)}, u32[]{:S(2)}, u32[]{:S(2)}) collective-permute-start(bf16[192,1536]{1,0:T(8,128)(2,1)S(1)} %collective-permute-done.4.refs_2_), channel_id=1, source_target_pairs={{0,8},{8,0},{16,24},{24,16},{1,9},{9,1},{17,25},{25,17},{2,10},{10... | collective-permute-start | bytes 1769480 | tf_op jit(solution)/shard_map/ppermute | solution.py:423
  34.1 16.9 %collective-permute-start.9 = (bf16[192,1536]{1,0:T(8,128)(2,1)S(1)}, bf16[192,1536]{1,0:T(8,128)(2,1)}, u32[]{:S(2)}, u32[]{:S(2)}) collective-permute-start(bf16[192,1536]{1,0:T(8,128)(2,1)S(1)} %collective-permute-done.4.refs_2_), channel_id=1, source_target_pairs={{0,4},{1,3},{2,6},{3,1},{4,0},{5,7},{6,2},{7,5},{8,10},{9,13},{10,... | collective-permute-start | bytes 1769480 | tf_op jit(solution)/shard_map/ppermute | solution.py:361
  38.2 12.8 %all-to-all-start.1 = ((bf16[8,80,384]{2,1,0:T(8,128)(2,1)}), bf16[8,80,384]{2,1,0:T(8,128)(2,1)S(1)}, u32[]{:S(2)}, u32[]{:S(2)}) async-start(bf16[8,80,384]{2,1,0:T(8,128)(2,1)} %prepare.1), calls=%async_computation.1 | async-start | bytes 983040 | tf_op jit(solution)/shard_map/all_to_all | solution.py:431
  44.7 10.4 %collective-permute-start.6 = (bf16[192,1536]{1,0:T(8,128)(2,1)S(1)}, bf16[192,1536]{1,0:T(8,128)(2,1)}, u32[]{:S(2)}, u32[]{:S(2)}) collective-permute-start(bf16[192,1536]{1,0:T(8,128)(2,1)S(1)} %copy-done.2), channel_id=1, source_target_pairs={{0,1},{1,0},{2,3},{3,2},{4,5},{5,4},{6,7},{7,6},{8,9},{9,8},{10,11... | collective-permute-start | bytes 1769480 | tf_op jit(solution)/shard_map/ppermute | solution.py:353
  44.7 10.4 %collective-permute-start.7 = (bf16[192,1536]{1,0:T(8,128)(2,1)S(1)}, bf16[192,1536]{1,0:T(8,128)(2,1)}, u32[]{:S(2)}, u32[]{:S(2)}) collective-permute-start(bf16[192,1536]{1,0:T(8,128)(2,1)S(1)} %collective-permute-done.4.refs_2_), channel_id=1, source_target_pairs={{0,1},{1,0},{2,3},{3,2},{4,5},{5,4},{6,7},{7,6},{8,9},{9,8},{10,11... | collective-permute-start | bytes 1769480 | tf_op jit(solution)/shard_map/ppermute | solution.py:353
  45.2 9.9 %collective-permute-start.8 = (bf16[192,1536]{1,0:T(8,128)(2,1)}, bf16[192,1536]{1,0:T(8,128)(2,1)}, u32[]{:S(2)}, u32[]{:S(2)}) collective-permute-start(bf16[192,1536]{1,0:T(8,128)(2,1)} %collective-permute-done.5.refs_4_), channel_id=1, source_target_pairs={{0,1},{1,0},{2,3},{3,2},{4,5},{5,4},{6,7},{7,6},{8,9},{9,8},{10,11... | collective-permute-start | bytes 1769480 | tf_op jit(solution)/shard_map/ppermute | solution.py:353
  51.0 4.1 %collective-permute-start.10 = (bf16[192,1536]{1,0:T(8,128)(2,1)}, bf16[192,1536]{1,0:T(8,128)(2,1)}, u32[]{:S(2)}, u32[]{:S(2)}) collective-permute-start(bf16[192,1536]{1,0:T(8,128)(2,1)} %collective-permute-done.9.refs_6_), channel_id=1, source_target_pairs={{0,1},{1,0},{2,3},{3,2},{4,5},{5,4},{6,7},{7,6},{8,9},{9,8},{10,11... | collective-permute-start | bytes 1769480 | tf_op jit(solution)/shard_map/ppermute | solution.py:353
  56.7 19.6 %copy-start.4 = (f32[48,64]{1,0:T(8,128)S(1)}, f32[48,64]{1,0:T(8,128)}, u32[]{:S(2)}) copy-start(f32[48,64]{1,0:T(8,128)} %get-tuple-element.23.opening_ref) | copy-start | bytes 36868
  56.7 19.6 %copy-start.6 = (f32[48,64]{1,0:T(8,128)S(1)}, f32[48,64]{1,0:T(8,128)}, u32[]{:S(2)}) copy-start(f32[48,64]{1,0:T(8,128)} %add_add_fusion.kept_ref) | copy-start | bytes 36868
  56.7 19.6 %copy-start.7 = (f32[48,64]{1,0:T(8,128)S(1)}, f32[48,64]{1,0:T(8,128)}, u32[]{:S(2)}) copy-start(f32[48,64]{1,0:T(8,128)} %first_ref.1) | copy-start | bytes 36868
  56.7 19.6 %copy-start.10 = (f32[8]{0:T(128)S(1)}, f32[8]{0:T(128)}, u32[]{:S(2)}) copy-start(f32[8]{0:T(128)} %copy-done.9) | copy-start | bytes 100
  77.6 1.4 %collective-permute-start.11 = (f32[8,64]{1,0:T(8,128)S(1)}, f32[8,64]{1,0:T(8,128)S(1)}, u32[]{:S(2)}, u32[]{:S(2)}) collective-permute-start(f32[8,64]{1,0:T(8,128)S(1)} %get-tuple-element.35), channel_id=1, source_target_pairs={{0,1},{1,0},{2,3},{3,2},{4,5},{5,4},{6,7},{7,6},{8,9},{9,8},{10,11... | collective-permute-start | bytes 6152 | tf_op jit(solution)/shard_map/ppermute | solution.py:353
  79.0 4.5 %collective-permute-start.14 = (f32[8,64]{1,0:T(8,128)S(1)}, f32[8,64]{1,0:T(8,128)S(1)}, u32[]{:S(2)}, u32[]{:S(2)}) collective-permute-start(f32[8,64]{1,0:T(8,128)S(1)} %add.58), channel_id=1, source_target_pairs={{0,6},{1,7},{2,4},{3,5},{4,2},{5,3},{6,0},{7,1},{8,14},{9,15},{10,... | collective-permute-start | bytes 6152 | tf_op jit(solution)/shard_map/ppermute | solution.py:353
  80.3 3.6 %collective-permute-start.13 = (f32[8,64]{1,0:T(8,128)S(1)}, f32[8,64]{1,0:T(8,128)S(1)}, u32[]{:S(2)}, u32[]{:S(2)}) collective-permute-start(f32[8,64]{1,0:T(8,128)S(1)} %add.58), channel_id=1, source_target_pairs={{0,4},{1,5},{2,6},{3,7},{4,0},{5,1},{6,2},{7,3},{8,12},{9,13},{10,... | collective-permute-start | bytes 6152 | tf_op jit(solution)/shard_map/ppermute | solution.py:353
  81.0 3.6 %collective-permute-start.12 = (f32[8,64]{1,0:T(8,128)S(1)}, f32[8,64]{1,0:T(8,128)S(1)}, u32[]{:S(2)}, u32[]{:S(2)}) collective-permute-start(f32[8,64]{1,0:T(8,128)S(1)} %add.58), channel_id=1, source_target_pairs={{0,2},{1,3},{2,0},{3,1},{4,6},{5,7},{6,4},{7,5},{8,10},{9,11},{10,... | collective-permute-start | bytes 6152 | tf_op jit(solution)/shard_map/ppermute | solution.py:353
  (6 other events, 15.2 us)

commit v7 on v6

--- a/solution.py
+++ b/solution.py
@@ -310,20 +310,23 @@
     )(owners, coef, embed, queries, att, gate, final, *parts)
 
 
-def advance_kernel(share, place_ref, keep_ref, noise_ref, states_ref, opening_ref, first_ref, kept_ref, out_ref, square_ref):
+def advance_kernel(share, place_ref, keep_ref, noise_ref, states_ref, opening_ref, first_ref, kept_ref, out_ref, square_ref, packed_scr):
     groups, count = noise_ref.shape[:2]
     steps, tokd, chans = states_ref.shape
-    packed = jnp.zeros(noise_ref.shape[2:], F32)
+    packed_scr[...] = jnp.zeros(packed_scr.shape, F32)
     for group in range(groups - 1):
-        total = noise_ref[group, 0].astype(F32)
-        for i in range(1, count):
-            total = total + noise_ref[group, i].astype(F32)
-        packed = packed + jnp.where(place_ref[0] > group, total, jnp.zeros_like(total))
+
+        @pl.when(place_ref[0] > group)
+        def _add(group=group):
+            total = noise_ref[group, 0].astype(F32)
+            for i in range(1, count):
+                total = total + noise_ref[group, i].astype(F32)
+            packed_scr[...] += total
 
     def unpack(x):
         return jnp.concatenate([x[:, :chans], x[:, chans:]], axis=0)
 
-    state = first_ref[...] + kept_ref[...] + unpack(packed)
+    state = first_ref[...] + kept_ref[...] + unpack(packed_scr[...])
     for t in range(steps):
         noise = noise_ref[place_ref[0], t * share].astype(F32)
         for i in range(1, share):
@@ -344,6 +347,7 @@
             jax.ShapeDtypeStruct((steps, chans), F32),
         ],
         in_specs=[SMEM] * 2 + [VMEM] * 5,
+        scratch_shapes=[pltpu.VMEM(noise.shape[2:], F32)],
         compiler_params=params(2),
         name="advance",
     )(place, keep, noise, states, opening, first, kept)

time: 86 us -> 86 us (level)
  no operation moved by 1% of the time
where the time goes in v7:
time: 86 us; the launch traced here: 85.3 us
  starting transfers between devices  26.5 us (31%)
  Pallas kernels  17.8 us (21%)
  waiting for transfers between devices  15.1 us (18%)
  blocking collectives  12.8 us (15%)
  local copies, waits for them, and re-layouts  5.54 us (6%)
  other arithmetic  4.65 us (5%)
  matrix products  2.07 us (2%)
    all_to_all x1, blocking collectives, per_device(): noise = lax.all_to_all(noise, ('tm', 'seq'), 0, 0, tiled=True)  12.8 us
    ppermute x3, starting transfers between devices, earlier_total(): lax.ppermute(total, 'tm', [(i, i + by) for i in range(count - by)])  7.05 us
    pallas_call x1, Pallas kernels, finish(): pl.pallas_call(functools.partial(finish_kernel, tokd), out_shape=jax.Shap...  6.77 us
    all_to_all x1, waiting for transfers between devices, per_device(): received = lax.all_to_all(sent, 'seq', 0, 0, tiled=True)  5.8 us
    ppermute x8, starting transfers between devices, swap(): return lax.ppermute(x, 'seq', [(i, i ^ mask) for i in range(count)])  4.6 us
    ppermute x1, starting transfers between devices, per_device(): lax.ppermute(late_states[-1], 'tm', [(i, i + 1) for i in range(tm_count -...  4.12 us
    pallas_call x1, Pallas kernels, attend(): pl.pallas_call(functools.partial(attend_kernel, heads, n_sub, per, sub, t...  3.96 us
    all_to_all x1, starting transfers between devices, per_device(): w_mine = lax.all_to_all(w_sent, 'seq', 0, 0, tiled=True)  3.74 us
  transfers between devices with their start and end apart: 17, of which 7 were waited for; matrix products, arithmetic and copies ran while one was open for 10% of the time, Pallas kernels for 11%

profile of v7, /device:TPU:0, one launch (start us, length us, event | category | flops | bytes accessed | tf_op | source)
XLA Modules:
  0.0 85.3 jit_solution(8484077494679923030)
XLA Ops:
  0.6 3.0 %collective-permute-start.4 = (bf16[192,1536]{1,0:T(8,128)(2,1)}, bf16[192,1536]{1,0:T(8,128)(2,1)S(1)}, u32[]{:S(2)}, u32[]{:S(2)}) collective-permute-start(bf16[192,1536]{1,0:T(8,128)(2,1)} %refs_0_), channel_id=1, source_target_pairs={{0,2},{1,5},{2,0},{3,7},{4,6},{5,1},{6,4},{7,3},{8,12},{9,11},{10,... | collective-permute-start | bytes 1769480 | tf_op jit(solution)/shard_map/ppermute | solution.py:365
  3.6 2.9 %cut.1 = bf16[8,224,512]{2,1,0:T(8,128)(2,1)} custom-call(bf16[12,192,384]{2,1,0:T(8,128)(2,1)} %bitcast.18), custom_call_target="tpu_custom_call" | custom-call | tf_op jit(solution)/shard_map/cut/pallas_call | solution.py:96
  6.5 3.7 %all-to-all-start = ((bf16[8,224,512]{2,1,0:T(8,128)(2,1)}), bf16[8,224,512]{2,1,0:T(8,128)(2,1)S(1)}, u32[]{:S(2)}, u32[]{:S(2)}) async-start(bf16[8,224,512]{2,1,0:T(8,128)(2,1)} %cut.1), calls=%async_computation | async-start | bytes 3670016 | tf_op jit(solution)/shard_map/all_to_all | solution.py:411
  10.9 4.1 %collective-permute-start = (f32[48,64]{1,0:T(8,128)}, f32[48,64]{1,0:T(8,128)}, u32[]{:S(2)}, u32[]{:S(2)}) collective-permute-start(f32[48,64]{1,0:T(8,128)} %slice_bitcast_fusion), channel_id=1, source_target_pairs={{0,8},{8,16},{16,24},{1,9},{9,17},{17,25},{2,10},{10,18},{18,26},{... | collective-permute-start | bytes 36872 | tf_op jit(solution)/shard_map/ppermute | solution.py:417
  15.8 2.1 %fusion.2.mod_ref = f32[8,4608]{1,0:T(8,128)S(1)} fusion(bf16[256,4608]{1,0:T(8,128)(2,1)} %param.14, bf16[8,128]{1,0:T(8,128)(2,1)S(1)} %get-tuple-element.41, bf16[8,128]{1,0:T(8,128)(2,1)S(1)} %get-tuple-element.40), kind=kOutput, calls=%fused_computation.9 | convolution fusion | flops 18882560 | bytes 2510848 | tf_op jit(solution)/shard_map/dot_general | solution.py:40
  19.2 1.9 %multiply_add_fusion = (f32[48,64]{1,0:T(8,128)S(1)}, f32[48,64]{1,0:T(8,128)}) fusion(f32[48,64]{1,0:T(8,128)} %multiply_reduce_fusion, f32[]{:T(128)} %bitcast.17, f32[48,64]{1,0:T(8,128)} %first_ref.1, f32[48,64]{1,0:T(8,128)} %collective-permute-done, pred[]{:T(512)S(6)} %eq.10), kind=kLoop, calls=%fused_computation.2 | loop fusion | flops 9216 | bytes 61445 | tf_op jit(solution)/shard_map/add | solution.py:420
  21.1 3.3 %collective-permute-start.3 = (f32[48,64]{1,0:T(8,128)S(1)}, f32[48,64]{1,0:T(8,128)S(1)}, u32[]{:S(2)}, u32[]{:S(2)}) collective-permute-start(f32[48,64]{1,0:T(8,128)S(1)} %get-tuple-element.38), channel_id=1, source_target_pairs={{0,24},{1,25},{2,26},{3,27},{4,28},{5,29},{6,30},{7,31}} | collective-permute-start | bytes 36872 | tf_op jit(solution)/shard_map/ppermute | solution.py:372
  24.4 1.3 %collective-permute-start.2 = (f32[48,64]{1,0:T(8,128)S(1)}, f32[48,64]{1,0:T(8,128)S(1)}, u32[]{:S(2)}, u32[]{:S(2)}) collective-permute-start(f32[48,64]{1,0:T(8,128)S(1)} %get-tuple-element.38), channel_id=1, source_target_pairs={{0,16},{8,24},{1,17},{9,25},{2,18},{10,26},{3,19},{11,27},{4,20},{... | collective-permute-start | bytes 36872 | tf_op jit(solution)/shard_map/ppermute | solution.py:372
  25.7 2.5 %collective-permute-start.1 = (f32[48,64]{1,0:T(8,128)S(1)}, f32[48,64]{1,0:T(8,128)S(1)}, u32[]{:S(2)}, u32[]{:S(2)}) collective-permute-start(f32[48,64]{1,0:T(8,128)S(1)} %get-tuple-element.38), channel_id=1, source_target_pairs={{0,8},{8,16},{16,24},{1,9},{9,17},{17,25},{2,10},{10,18},{18,26},{... | collective-permute-start | bytes 36872 | tf_op jit(solution)/shard_map/ppermute | solution.py:372
  28.8 1.3 %dynamic_slice.7.coef_ref = f32[1]{0:T(128)} dynamic-slice(f32[8]{0:T(128)} %get-tuple-element.36, s32[]{:T(128)S(6)} %select_n.31), dynamic_slice_sizes={1} | dynamic-slice | bytes 12 | tf_op jit(solution)/shard_map/dynamic_slice | solution.py:424
  30.7 3.4 %all-to-all-done.w_ref = bf16[8,224,512]{2,1,0:T(8,128)(2,1)S(1)} async-done(((bf16[8,224,512]{2,1,0:T(8,128)(2,1)}), bf16[8,224,512]{2,1,0:T(8,128)(2,1)S(1)}, u32[]{:S(2)}, u32[]{:S(2)}) %all-to-all-start) | async-done | bytes 1835040 | tf_op jit(solution)/shard_map/all_to_all | solution.py:411
  35.3 2.8 %prepare.1 = bf16[8,80,384]{2,1,0:T(8,128)(2,1)} custom-call(bf16[64,1536]{1,0:T(8,128)(2,1)S(1)} %copy-done, f32[8,4608]{1,0:T(8,128)S(1)} %fusion.2.mod_ref, bf16[8,224,512]{2,1,0:T(8,128)(2,1)S(1)} %all-to-all-done.w_ref, f32[8,48,64]{2,1,0:T(8,128)S(1)} %copy-done.1, f32[48,64]{1,0:T(8,128)S(1)} %copy-done.3), custom_call_target="tpu_custom_call" | custom-call | tf_op jit(solution)/shard_map/prepare/pallas_call | solution.py:174
  38.2 3.5 %all-to-all-start.1 = ((bf16[8,80,384]{2,1,0:T(8,128)(2,1)}), bf16[8,80,384]{2,1,0:T(8,128)(2,1)S(1)}, u32[]{:S(2)}, u32[]{:S(2)}) async-start(bf16[8,80,384]{2,1,0:T(8,128)(2,1)} %prepare.1), calls=%async_computation.1 | async-start | bytes 983040 | tf_op jit(solution)/shard_map/all_to_all | solution.py:435
  41.6 3.0 %collective-permute-done.5.refs_4_ = bf16[192,1536]{1,0:T(8,128)(2,1)} collective-permute-done((bf16[192,1536]{1,0:T(8,128)(2,1)S(1)}, bf16[192,1536]{1,0:T(8,128)(2,1)}, u32[]{:S(2)}, u32[]{:S(2)}) %collective-permute-start.5) | collective-permute-done | bytes 589856 | tf_op jit(solution)/shard_map/ppermute | solution.py:427
  45.2 5.8 %all-to-all-done.1.pay_ref = bf16[8,80,384]{2,1,0:T(8,128)(2,1)S(1)} async-done(((bf16[8,80,384]{2,1,0:T(8,128)(2,1)}), bf16[8,80,384]{2,1,0:T(8,128)(2,1)S(1)}, u32[]{:S(2)}, u32[]{:S(2)}) %all-to-all-start.1) | async-done | bytes 491552 | tf_op jit(solution)/shard_map/all_to_all | solution.py:435
  51.1 4.0 %attend.1 = (bf16[384,1536]{1,0:T(8,128)(2,1)S(1)}, bf16[384,64]{1,0:T(8,128)(2,1)S(1)}) custom-call(s32[1]{0:T(128)} %constant.70.clone.1.part_ref, bf16[64,1536]{1,0:T(8,128)(2,1)S(1)} %copy-done, bf16[8,80,384]{2,1,0:T(8,128)(2,1)S(1)} %all-to-all-done.1.pay_ref), custom_call_target="tpu_custom_call" | custom-call | tf_op jit(solution)/shard_map/attend/pallas_call | solution.py:245
  55.1 0.9 %copy-done.5 = bf16[1536,64]{0,1:T(8,128)(2,1)S(1)} copy-done((bf16[1536,64]{0,1:T(8,128)(2,1)S(1)}, bf16[1536,64]{0,1:T(8,128)(2,1)}, u32[]{:S(2)}) %copy-start.5) | copy-done | bytes 196632
  56.7 6.8 %finish.1 = bf16[4,8,24,128]{3,2,1,0:T(8,128)(2,1)S(1)} custom-call(s32[8]{0:T(128)S(1)} %broadcast_xor_fusion.owner_ref, f32[1]{0:T(128)} %dynamic_slice.7.coef_ref, bf16[64,1536]{1,0:T(8,128)(2,1)S(1)} %copy-done, bf16[384,64]{1,0:T(8,128)(2,1)S(1)} %get-tuple-element.24.queries_ref, bf16[384,1536]{1,0:T(8,128)(2,1)S(1)} %get-tuple-element.25.att_ref, ...), custom_call_target="tpu_custom_call" | custom-call | tf_op jit(solution)/shard_map/finish/pallas_call | solution.py:299
  63.5 12.8 %all_to_all.15 = bf16[32,24,128]{2,1,0:T(8,128)(2,1)S(1)} all-to-all(bf16[32,24,128]{2,1,0:T(8,128)(2,1)S(1)} %bitcast.14), channel_id=1, replica_groups=mesh['tm'=4,'seq'=8] {'tm','seq'}, dimensions={0} | all-to-all | bytes 393216 | tf_op jit(solution)/shard_map/all_to_all | solution.py:463
  76.3 1.3 %advance.1 = (f32[8,48,64]{2,1,0:T(8,128)}, f32[8,64]{1,0:T(8,128)S(1)}) custom-call(s32[1]{0:T(128)} %bitcast.place_ref, f32[8]{0:T(128)S(1)} %copy-done.10, bf16[4,8,24,128]{3,2,1,0:T(8,128)(2,1)S(1)} %bitcast.15, f32[8,48,64]{2,1,0:T(8,128)S(1)} %copy-done.1, f32[48,64]{1,0:T(8,128)S(1)} %copy-done.4, f32[48,64]{1,0:T(8,128)S(1)} %copy-done.7, ...), custom_call_target="tpu_custom_call" | custom-call | tf_op jit(solution)/shard_map/advance/pallas_call | solution.py:343
  78.2 0.8 collective-permute-done.11
  79.0 1.2 %collective-permute-start.14 = (f32[8,64]{1,0:T(8,128)S(1)}, f32[8,64]{1,0:T(8,128)S(1)}, u32[]{:S(2)}, u32[]{:S(2)}) collective-permute-start(f32[8,64]{1,0:T(8,128)S(1)} %add.58), channel_id=1, source_target_pairs={{0,6},{1,7},{2,4},{3,5},{4,2},{5,3},{6,0},{7,1},{8,14},{9,15},{10,... | collective-permute-start | bytes 6152 | tf_op jit(solution)/shard_map/ppermute | solution.py:357
  81.1 1.5 %collective-permute-start.12 = (f32[8,64]{1,0:T(8,128)S(1)}, f32[8,64]{1,0:T(8,128)S(1)}, u32[]{:S(2)}, u32[]{:S(2)}) collective-permute-start(f32[8,64]{1,0:T(8,128)S(1)} %add.58), channel_id=1, source_target_pairs={{0,2},{1,3},{2,0},{3,1},{4,6},{5,7},{6,4},{7,5},{8,10},{9,11},{10,... | collective-permute-start | bytes 6152 | tf_op jit(solution)/shard_map/ppermute | solution.py:357
  82.5 1.0 %collective-permute-done.14 = f32[8,64]{1,0:T(8,128)S(1)} collective-permute-done((f32[8,64]{1,0:T(8,128)S(1)}, f32[8,64]{1,0:T(8,128)S(1)}, u32[]{:S(2)}, u32[]{:S(2)}) %collective-permute-start.14) | collective-permute-done | bytes 2080 | tf_op jit(solution)/shard_map/ppermute | solution.py:357
  (60 shorter events, 9.7 us)
Async XLA Ops:
  0.6 29.4 %collective-permute-start.4 = (bf16[192,1536]{1,0:T(8,128)(2,1)}, bf16[192,1536]{1,0:T(8,128)(2,1)S(1)}, u32[]{:S(2)}, u32[]{:S(2)}) collective-permute-start(bf16[192,1536]{1,0:T(8,128)(2,1)} %refs_0_), channel_id=1, source_target_pairs={{0,2},{1,5},{2,0},{3,7},{4,6},{5,1},{6,4},{7,3},{8,12},{9,11},{10,... | collective-permute-start | bytes 1769480 | tf_op jit(solution)/shard_map/ppermute | solution.py:365
  6.5 8.5 %copy-start.12 = (s32[8]{0:T(128)S(1)}, s32[8]{0:T(128)}, u32[]{:S(2)}) copy-start(s32[8]{0:T(128)} %param.11) | copy-start | bytes 100
  6.5 27.5 %all-to-all-start = ((bf16[8,224,512]{2,1,0:T(8,128)(2,1)}), bf16[8,224,512]{2,1,0:T(8,128)(2,1)S(1)}, u32[]{:S(2)}, u32[]{:S(2)}) async-start(bf16[8,224,512]{2,1,0:T(8,128)(2,1)} %cut.1), calls=%async_computation | async-start | bytes 3670016 | tf_op jit(solution)/shard_map/all_to_all | solution.py:411
  10.3 24.3 %copy-start = (bf16[64,1536]{1,0:T(8,128)(2,1)S(1)}, bf16[64,1536]{1,0:T(8,128)(2,1)}, u32[]{:S(2)}) copy-start(bf16[64,1536]{1,0:T(8,128)(2,1)} %embed_ref.5) | copy-start | bytes 589828
  10.9 8.3 %collective-permute-start = (f32[48,64]{1,0:T(8,128)}, f32[48,64]{1,0:T(8,128)}, u32[]{:S(2)}, u32[]{:S(2)}) collective-permute-start(f32[48,64]{1,0:T(8,128)} %slice_bitcast_fusion), channel_id=1, source_target_pairs={{0,8},{8,16},{16,24},{1,9},{9,17},{17,25},{2,10},{10,18},{18,26},{... | collective-permute-start | bytes 36872 | tf_op jit(solution)/shard_map/ppermute | solution.py:417
  17.9 26.8 %copy-start.2 = (bf16[192,1536]{1,0:T(8,128)(2,1)S(1)}, bf16[192,1536]{1,0:T(8,128)(2,1)}, u32[]{:S(2)}) copy-start(bf16[192,1536]{1,0:T(8,128)(2,1)} %refs_0_) | copy-start | bytes 1769476
  21.1 9.0 %collective-permute-start.3 = (f32[48,64]{1,0:T(8,128)S(1)}, f32[48,64]{1,0:T(8,128)S(1)}, u32[]{:S(2)}, u32[]{:S(2)}) collective-permute-start(f32[48,64]{1,0:T(8,128)S(1)} %get-tuple-element.38), channel_id=1, source_target_pairs={{0,24},{1,25},{2,26},{3,27},{4,28},{5,29},{6,30},{7,31}} | collective-permute-start | bytes 36872 | tf_op jit(solution)/shard_map/ppermute | solution.py:372
  24.4 5.7 %collective-permute-start.2 = (f32[48,64]{1,0:T(8,128)S(1)}, f32[48,64]{1,0:T(8,128)S(1)}, u32[]{:S(2)}, u32[]{:S(2)}) collective-permute-start(f32[48,64]{1,0:T(8,128)S(1)} %get-tuple-element.38), channel_id=1, source_target_pairs={{0,16},{8,24},{1,17},{9,25},{2,18},{10,26},{3,19},{11,27},{4,20},{... | collective-permute-start | bytes 36872 | tf_op jit(solution)/shard_map/ppermute | solution.py:372
  25.7 4.4 %collective-permute-start.1 = (f32[48,64]{1,0:T(8,128)S(1)}, f32[48,64]{1,0:T(8,128)S(1)}, u32[]{:S(2)}, u32[]{:S(2)}) collective-permute-start(f32[48,64]{1,0:T(8,128)S(1)} %get-tuple-element.38), channel_id=1, source_target_pairs={{0,8},{8,16},{16,24},{1,9},{9,17},{17,25},{2,10},{10,18},{18,26},{... | collective-permute-start | bytes 36872 | tf_op jit(solution)/shard_map/ppermute | solution.py:372
  30.1 14.6 %collective-permute-start.5 = (bf16[192,1536]{1,0:T(8,128)(2,1)S(1)}, bf16[192,1536]{1,0:T(8,128)(2,1)}, u32[]{:S(2)}, u32[]{:S(2)}) collective-permute-start(bf16[192,1536]{1,0:T(8,128)(2,1)S(1)} %collective-permute-done.4.refs_2_), channel_id=1, source_target_pairs={{0,8},{8,0},{16,24},{24,16},{1,9},{9,1},{17,25},{25,17},{2,10},{10... | collective-permute-start | bytes 1769480 | tf_op jit(solution)/shard_map/ppermute | solution.py:427
  34.1 16.9 %collective-permute-start.9 = (bf16[192,1536]{1,0:T(8,128)(2,1)S(1)}, bf16[192,1536]{1,0:T(8,128)(2,1)}, u32[]{:S(2)}, u32[]{:S(2)}) collective-permute-start(bf16[192,1536]{1,0:T(8,128)(2,1)S(1)} %collective-permute-done.4.refs_2_), channel_id=1, source_target_pairs={{0,4},{1,3},{2,6},{3,1},{4,0},{5,7},{6,2},{7,5},{8,10},{9,13},{10,... | collective-permute-start | bytes 1769480 | tf_op jit(solution)/shard_map/ppermute | solution.py:365
  38.2 12.8 %all-to-all-start.1 = ((bf16[8,80,384]{2,1,0:T(8,128)(2,1)}), bf16[8,80,384]{2,1,0:T(8,128)(2,1)S(1)}, u32[]{:S(2)}, u32[]{:S(2)}) async-start(bf16[8,80,384]{2,1,0:T(8,128)(2,1)} %prepare.1), calls=%async_computation.1 | async-start | bytes 983040 | tf_op jit(solution)/shard_map/all_to_all | solution.py:435
  44.7 10.4 %collective-permute-start.6 = (bf16[192,1536]{1,0:T(8,128)(2,1)S(1)}, bf16[192,1536]{1,0:T(8,128)(2,1)}, u32[]{:S(2)}, u32[]{:S(2)}) collective-permute-start(bf16[192,1536]{1,0:T(8,128)(2,1)S(1)} %copy-done.2), channel_id=1, source_target_pairs={{0,1},{1,0},{2,3},{3,2},{4,5},{5,4},{6,7},{7,6},{8,9},{9,8},{10,11... | collective-permute-start | bytes 1769480 | tf_op jit(solution)/shard_map/ppermute | solution.py:357
  44.7 10.4 %collective-permute-start.7 = (bf16[192,1536]{1,0:T(8,128)(2,1)S(1)}, bf16[192,1536]{1,0:T(8,128)(2,1)}, u32[]{:S(2)}, u32[]{:S(2)}) collective-permute-start(bf16[192,1536]{1,0:T(8,128)(2,1)S(1)} %collective-permute-done.4.refs_2_), channel_id=1, source_target_pairs={{0,1},{1,0},{2,3},{3,2},{4,5},{5,4},{6,7},{7,6},{8,9},{9,8},{10,11... | collective-permute-start | bytes 1769480 | tf_op jit(solution)/shard_map/ppermute | solution.py:357
  45.2 9.9 %collective-permute-start.8 = (bf16[192,1536]{1,0:T(8,128)(2,1)}, bf16[192,1536]{1,0:T(8,128)(2,1)}, u32[]{:S(2)}, u32[]{:S(2)}) collective-permute-start(bf16[192,1536]{1,0:T(8,128)(2,1)} %collective-permute-done.5.refs_4_), channel_id=1, source_target_pairs={{0,1},{1,0},{2,3},{3,2},{4,5},{5,4},{6,7},{7,6},{8,9},{9,8},{10,11... | collective-permute-start | bytes 1769480 | tf_op jit(solution)/shard_map/ppermute | solution.py:357
  51.0 4.1 %collective-permute-start.10 = (bf16[192,1536]{1,0:T(8,128)(2,1)}, bf16[192,1536]{1,0:T(8,128)(2,1)}, u32[]{:S(2)}, u32[]{:S(2)}) collective-permute-start(bf16[192,1536]{1,0:T(8,128)(2,1)} %collective-permute-done.9.refs_6_), channel_id=1, source_target_pairs={{0,1},{1,0},{2,3},{3,2},{4,5},{5,4},{6,7},{7,6},{8,9},{9,8},{10,11... | collective-permute-start | bytes 1769480 | tf_op jit(solution)/shard_map/ppermute | solution.py:357
  56.7 19.6 %copy-start.4 = (f32[48,64]{1,0:T(8,128)S(1)}, f32[48,64]{1,0:T(8,128)}, u32[]{:S(2)}) copy-start(f32[48,64]{1,0:T(8,128)} %get-tuple-element.23.opening_ref) | copy-start | bytes 36868
  56.7 19.6 %copy-start.6 = (f32[48,64]{1,0:T(8,128)S(1)}, f32[48,64]{1,0:T(8,128)}, u32[]{:S(2)}) copy-start(f32[48,64]{1,0:T(8,128)} %add_add_fusion.kept_ref) | copy-start | bytes 36868
  56.7 19.6 %copy-start.7 = (f32[48,64]{1,0:T(8,128)S(1)}, f32[48,64]{1,0:T(8,128)}, u32[]{:S(2)}) copy-start(f32[48,64]{1,0:T(8,128)} %first_ref.1) | copy-start | bytes 36868
  56.7 19.6 %copy-start.10 = (f32[8]{0:T(128)S(1)}, f32[8]{0:T(128)}, u32[]{:S(2)}) copy-start(f32[8]{0:T(128)} %copy-done.9) | copy-start | bytes 100
  77.6 1.4 %collective-permute-start.11 = (f32[8,64]{1,0:T(8,128)S(1)}, f32[8,64]{1,0:T(8,128)S(1)}, u32[]{:S(2)}, u32[]{:S(2)}) collective-permute-start(f32[8,64]{1,0:T(8,128)S(1)} %get-tuple-element.35), channel_id=1, source_target_pairs={{0,1},{1,0},{2,3},{3,2},{4,5},{5,4},{6,7},{7,6},{8,9},{9,8},{10,11... | collective-permute-start | bytes 6152 | tf_op jit(solution)/shard_map/ppermute | solution.py:357
  79.0 4.5 %collective-permute-start.14 = (f32[8,64]{1,0:T(8,128)S(1)}, f32[8,64]{1,0:T(8,128)S(1)}, u32[]{:S(2)}, u32[]{:S(2)}) collective-permute-start(f32[8,64]{1,0:T(8,128)S(1)} %add.58), channel_id=1, source_target_pairs={{0,6},{1,7},{2,4},{3,5},{4,2},{5,3},{6,0},{7,1},{8,14},{9,15},{10,... | collective-permute-start | bytes 6152 | tf_op jit(solution)/shard_map/ppermute | solution.py:357
  80.3 3.6 %collective-permute-start.13 = (f32[8,64]{1,0:T(8,128)S(1)}, f32[8,64]{1,0:T(8,128)S(1)}, u32[]{:S(2)}, u32[]{:S(2)}) collective-permute-start(f32[8,64]{1,0:T(8,128)S(1)} %add.58), channel_id=1, source_target_pairs={{0,4},{1,5},{2,6},{3,7},{4,0},{5,1},{6,2},{7,3},{8,12},{9,13},{10,... | collective-permute-start | bytes 6152 | tf_op jit(solution)/shard_map/ppermute | solution.py:357
  81.1 3.6 %collective-permute-start.12 = (f32[8,64]{1,0:T(8,128)S(1)}, f32[8,64]{1,0:T(8,128)S(1)}, u32[]{:S(2)}, u32[]{:S(2)}) collective-permute-start(f32[8,64]{1,0:T(8,128)S(1)} %add.58), channel_id=1, source_target_pairs={{0,2},{1,3},{2,0},{3,1},{4,6},{5,7},{6,4},{7,5},{8,10},{9,11},{10,... | collective-permute-start | bytes 6152 | tf_op jit(solution)/shard_map/ppermute | solution.py:357
  (6 other events, 15.2 us)
